TPU v7x, 128 devices: a whole 4x4x4 slice. The times are simulated.
128 devices in a mesh: dp: 16 (over y, z_lo, core), expert: 8 (over z_hi, x).
Axes of the slice: x: 4, y: 4, z: 4 (z_hi: 2, z_lo: 2; z = z_hi * 2 + z_lo), core: 2. Of those that a mesh axis runs over, the one named last changes fastest.
Arguments:
- tokens: bfloat16 [32768, 768], P(('dp', 'expert')), may hold values from -6 to 6
- routes: int32 [32768, 2], P(('dp', 'expert')), may hold values from 0 to 7, all different within a row; in each aligned block of 256 rows (0 to 255, 256 to 511, ...) at most 128 rows name the same one
- lengths: int32 [128, 16], P(('dp', 'expert')), may hold values from 1 to 64, 256 in all within a row
- norm_gain: float32 [768], replicated, may hold values from 0.25 to 1.75
- router_weight: bfloat16 [768, 8], replicated, may hold values from -0.21875 to 0.21875
- gate_weight: bfloat16 [8, 768, 3072], P('expert'), may hold values from -0.21875 to 0.21875
- up_weight: bfloat16 [8, 768, 3072], P('expert'), may hold values from -0.21875 to 0.21875
- down_weight: bfloat16 [8, 3072, 768], P('expert'), may hold values from -0.109375 to 0.109375
Outputs:
- hidden_out: bfloat16 [32768, 768], P(('dp', 'expert'))
- query_grad: float32 [1024, 768], P(('dp', 'expert'))
- doc_grad: float32 [1024, 768], P(('dp', 'expert'))
Inputs may be any that keep to these rules, and one draw needn't show every extreme that they name: `routes`: among the rows of one device no expert is named by more than 128 rows, a bound that some block reaches. `lengths`: each row sums to 256; the first 8 entries are queries, the others their documents in the same order; the largest entry is 64.
All inputs are finite; a program needn't handle non-finite values.
Results may differ from a plain program's by a relative error of at most 0.0053.
Values may be sent and summed in bfloat16 or wider, within the bound.
No kernel may reach another device: no remote copies, remote signals or barrier semaphores. Data moves between devices by JAX's collectives and lax.ppermute only.
A program may use at most 128 MiB of HBM per device.

v0:
```python
import jax
import jax.numpy as jnp
from jax import lax
from jax.sharding import PartitionSpec as P

logit_scale = 50.0
norm_eps = 1e-06
pool_eps = 1e-06


def rms_normalize(tokens, norm_gain):
    widened = tokens.astype(jnp.float32)
    inverse = lax.rsqrt(jnp.mean(widened * widened, axis=-1, keepdims=True) + norm_eps)
    return (widened * inverse * norm_gain).astype(jnp.bfloat16)


def expert_rows(row_block, w_gate, w_up, w_down):
    gate_act = jnp.dot(row_block, w_gate, preferred_element_type=jnp.float32)
    up_act = jnp.dot(row_block, w_up, preferred_element_type=jnp.float32)
    hidden = (jax.nn.silu(gate_act) * up_act).astype(jnp.bfloat16)
    return jnp.dot(hidden, w_down, preferred_element_type=jnp.float32).astype(jnp.bfloat16)


def embed(mixed, lengths):
    starts = jnp.cumsum(lengths, axis=1, dtype=jnp.int32) - lengths
    places = jnp.arange(mixed.shape[1], dtype=jnp.int32)
    member = (
        (places[None, None, :] >= starts[:, :, None])
        & (places[None, None, :] < (starts + lengths)[:, :, None])
    ).astype(jnp.float32)
    pooled = jnp.einsum("gst,gtd->gsd", member, mixed, precision=lax.Precision.HIGHEST) / lengths[
        :, :, None
    ].astype(jnp.float32)
    return pooled * lax.rsqrt(jnp.sum(pooled * pooled, axis=-1, keepdims=True) + pool_eps)


def body(tokens, routes, lengths, norm_gain, router_weight, gate_weight, up_weight, down_weight):
    tok_rows, width = tokens.shape
    expert_count = router_weight.shape[1]
    capacity = tok_rows // 2
    normed = rms_normalize(tokens, norm_gain)
    logits = jnp.dot(normed, router_weight, preferred_element_type=jnp.float32)
    labels = jnp.arange(expert_count, dtype=jnp.int32)
    picked = routes[:, :, None] == labels[None, None, :]
    chosen = jnp.sum(jnp.where(picked, logits[:, None, :], 0.0), axis=-1)
    leading = jax.nn.sigmoid(chosen[:, 0] - chosen[:, 1])
    route_weights = jnp.stack([leading, 1.0 - leading], axis=1)
    flat_hits = picked.reshape(-1, expert_count).astype(jnp.int32)
    ranking = jnp.sum(
        (jnp.cumsum(flat_hits, axis=0, dtype=jnp.int32) - flat_hits) * flat_hits,
        axis=1,
        dtype=jnp.int32,
    )
    slot_ids = routes.reshape(-1) * capacity + ranking
    slot_grid = slot_ids.reshape(tok_rows, 2)
    spots = jnp.arange(expert_count * capacity, dtype=jnp.int32)
    dispatch = jnp.any(spots[:, None, None] == slot_grid[None, :, :], axis=-1).astype(jnp.bfloat16)
    outgoing = jnp.dot(dispatch, normed, preferred_element_type=jnp.float32).astype(jnp.bfloat16)
    outgoing = outgoing.reshape(expert_count, capacity, width)
    w_gate = gate_weight[0]
    w_up = up_weight[0]
    w_down = down_weight[0]
    incoming = lax.all_to_all(outgoing, "expert", split_axis=0, concat_axis=0, tiled=True)
    sources, slot_span, feature_count = incoming.shape
    results = expert_rows(
        incoming.reshape(sources * slot_span, feature_count), w_gate, w_up, w_down
    )
    results = results.reshape(sources, slot_span, feature_count)
    returned = lax.all_to_all(results, "expert", split_axis=0, concat_axis=0, tiled=True)
    back_rows = returned.reshape(expert_count * capacity, width)
    gathered_rows = back_rows[slot_ids].reshape(tok_rows, 2, width).astype(jnp.float32)
    mixed = tokens.astype(jnp.float32) + jnp.sum(route_weights[:, :, None] * gathered_rows, axis=1)
    hidden_out = mixed.astype(jnp.bfloat16)
    embedded = embed(mixed[None], lengths)[0]
    pair_count = embedded.shape[0] // 2
    queries = embedded[:pair_count]
    documents = embedded[pair_count:]
    all_docs = lax.all_gather(documents, ("dp", "expert"), axis=0, tiled=True)
    total_pairs = all_docs.shape[0]
    scores = logit_scale * jnp.dot(queries, all_docs.T, precision=lax.Precision.HIGHEST)
    exps = jnp.exp(scores)
    likely = exps / jnp.sum(exps, axis=-1, keepdims=True)
    own_index = lax.axis_index(("dp", "expert")) * pair_count + jnp.arange(
        pair_count, dtype=jnp.int32
    )
    target = (jnp.arange(total_pairs, dtype=jnp.int32)[None, :] == own_index[:, None]).astype(
        jnp.float32
    )
    coefficient = logit_scale * (likely - target)
    query_grad = jnp.dot(coefficient, all_docs, precision=lax.Precision.HIGHEST)
    partial_terms = jnp.dot(coefficient.T, queries, precision=lax.Precision.HIGHEST)
    doc_grad = lax.psum_scatter(partial_terms, ("dp", "expert"), scatter_dimension=0, tiled=True)
    return (hidden_out, query_grad, doc_grad)


def solution(mesh):
    placed = (
        P(("dp", "expert"), None),
        P(("dp", "expert"), None),
        P(("dp", "expert"), None),
        P(),
        P(),
        P("expert", None, None),
        P("expert", None, None),
        P("expert", None, None),
    )
    return jax.shard_map(
        body,
        mesh=mesh,
        in_specs=placed,
        out_specs=(P(("dp", "expert"), None), P(("dp", "expert"), None), P(("dp", "expert"), None)),
        check_vma=False,
    )
```

profile of v0, /device:TPU:1, one launch (start us, length us, event | category | flops | bytes accessed | tf_op | source)
XLA Modules:
  0.0 1050.7 jit_solution(5433942430563562098)
XLA Ops:
  7.2 0.8 copy.26
  8.0 0.1 eq.66
  8.1 0.1 eq.62
  8.3 1.1 reduce-window.6
  9.5 0.2 slice_reduce_fusion
  9.8 0.1 reduce_sum.61
  10.1 0.4 fusion.11
  10.5 1.3 fusion.23
  11.8 1.7 convolution_convert_fusion
  13.5 29.9 %all_to_all.10 = bf16[8,128,768]{2,1,0:T(8,128)(2,1)S(1)} all-to-all(bf16[8,128,768]{2,1,0:T(8,128)(2,1)S(1)} %bitcast.58), channel_id=1, replica_groups=mesh['dp'=16,'expert'=8] {'expert'}, dimensions={0} | all-to-all | bytes 3145728 | tf_op jit(solution)/shard_map/all_to_all | solution.py:63
  43.4 7.9 fusion.5
  51.3 18.8 %fusion.12 = bf16[1024,768]{1,0:T(8,128)(2,1)} fusion(bf16[1,3072,768]{2,1,0:T(8,128)(2,1)} %param.15, f32[1024,3072]{1,0:T(8,128)} %fusion.5, bf16[1024,768]{1,0:T(8,128)(2,1)S(1)} %bitcast.60, bf16[1,768,3072]{2,1,0:T(8,128)(2,1)} %param.14), kind=kOutput, calls=%fused_computation.13 | convolution fusion | flops 9683337216 | bytes 25165824 | tf_op jit(solution)/shard_map/dot_general | solution.py:21
  70.1 3.7 all-to-all-start.1
  73.9 0.2 all-gather.3.cloned.1.call-start
  74.1 0.1 mul.93
  74.3 0.3 fusion.28
  74.6 0.1 copy.25
  74.8 0.2 reduce_window_sum.28
  75.0 21.7 %all-to-all-done.1 = bf16[8,128,768]{2,1,0:T(8,128)(2,1)S(1)} async-done(((bf16[8,128,768]{2,1,0:T(8,128)(2,1)}), bf16[8,128,768]{2,1,0:T(8,128)(2,1)S(1)}, u32[]{:S(2)}, u32[]{:S(2)}) %all-to-all-start.1) | async-done | bytes 1572896 | tf_op jit(solution)/shard_map/all_to_all | solution.py:69
  96.7 2.0 gather_fusion
  98.7 0.8 reshape.164
  99.5 1.9 multiply_reduce_fusion
  101.4 0.9 copy-done.2
  102.3 0.5 multiply_reduce_fusion.1
  102.9 0.6 slice.38
  103.7 303.2 %all-gather.3.cloned.1.call-done = f32[1,1024,768]{2,1,0:T(8,128)} async-done(((f32[1,8,768]{2,1,0:T(8,128)}), f32[1,1024,768]{2,1,0:T(8,128)}) %all-gather.3.cloned.1.call-update) | async-done | bytes 3145744 | tf_op jit(solution)/shard_map/all_gather | solution.py:78
  406.9 4.6 fusion.41
  411.6 0.6 copy-done.4
  412.2 4.4 fusion.30
  416.6 2.1 fusion.26
  418.7 3.0 fusion.7
  421.7 622.1 %reduce-scatter.2.cloned.1.call-done = f32[8,768]{1,0:T(8,128)} async-done(((f32[1024,768]{1,0:T(8,128)}), f32[8,768]{1,0:T(8,128)}) %reduce-scatter.2.cloned.1.call-update) | async-done | bytes 24592 | tf_op jit(solution)/shard_map/reduce_scatter | solution.py:92
  (37 shorter events, 0.6 us)
Async XLA Ops:
  7.2 67.1 %copy-start = (bf16[768,8]{0,1:T(8,128)(2,1)S(1)}, bf16[768,8]{0,1:T(8,128)(2,1)}, u32[]{:S(2)}) copy-start(bf16[768,8]{0,1:T(8,128)(2,1)} %param.12) | copy-start | bytes 36868
  10.1 33.3 %copy-start.9 = (bf16[1,768,3072]{2,1,0:T(8,128)(2,1)S(1)}, bf16[1,768,3072]{2,1,0:T(8,128)(2,1)}, u32[]{:S(2)}) copy-start(bf16[1,768,3072]{2,1,0:T(8,128)(2,1)} %param.13) | copy-start | bytes 14155780
  70.1 4.1 copy-start.3
  70.1 4.1 copy-start.6
  70.1 4.4 copy-start.5
  70.1 4.7 copy-start.8
  70.1 26.6 %all-to-all-start.1 = ((bf16[8,128,768]{2,1,0:T(8,128)(2,1)}), bf16[8,128,768]{2,1,0:T(8,128)(2,1)S(1)}, u32[]{:S(2)}, u32[]{:S(2)}) async-start(bf16[8,128,768]{2,1,0:T(8,128)(2,1)} %bitcast.7), calls=%async_computation.1 | async-start | bytes 3145728 | tf_op jit(solution)/shard_map/all_to_all | solution.py:69
  73.9 333.0 %all-gather.3.cloned.1.call-start = ((), (), s32[]{:S(2)}) async-start(), calls=%async_computation.4 | async-start | bytes 3170304 | tf_op jit(solution)/shard_map/all_gather | solution.py:78
  101.4 0.9 copy-start.2
  103.6 940.2 %reduce-scatter.2.cloned.1.call-start = ((), (), s32[]{:S(2)}) async-start(), calls=%async_computation.3 | async-start | bytes 3170304 | tf_op jit(solution)/shard_map/reduce_scatter | solution.py:92
  103.7 307.9 %copy-start.7 = (s32[8]{0:T(128)}, s32[8]{0:T(128)S(1)}, u32[]{:S(2)}) copy-start(s32[8]{0:T(128)S(1)} %iota_add_fusion) | copy-start | bytes 100
  411.5 0.6 copy-start.4
  416.6 2.1 copy-start.1
Sparse Core Ops, SparseCore 0:
  103.7 303.1 all-gather.2
  416.7 627.0 reduce-scatter.1
where the time goes:
time: 1060 us; the launch traced here: 1050 us
  waiting for transfers between devices  947 us (89%)
  matrix products  41.2 us (4%)
  blocking collectives  29.9 us (3%)
  between operations  14.3 us (1%)
    reduce_scatter x1, waiting for transfers between devices, body(): lax.psum_scatter(partial_terms, ('dp', 'expert'), scatter_dimension=0, ti...  622 us
    all_gather x1, waiting for transfers between devices, body(): all_docs = lax.all_gather(documents, ('dp', 'expert'), axis=0, tiled=True)  303 us
    all_to_all x1, blocking collectives, body(): lax.all_to_all(outgoing, 'expert', split_axis=0, concat_axis=0, tiled=True)  29.9 us
    all_to_all x1, waiting for transfers between devices, body(): lax.all_to_all(results, 'expert', split_axis=0, concat_axis=0, tiled=True)  21.7 us
  transfers between devices with their start and end apart: 3, of which 3 were waited for; matrix products, arithmetic and copies ran while one was open for 1% of the time, Pallas kernels for 0%

commit v1 on v0

--- a/solution.py
+++ b/solution.py
@@ -32,6 +32,37 @@
         :, :, None
     ].astype(jnp.float32)
     return pooled * lax.rsqrt(jnp.sum(pooled * pooled, axis=-1, keepdims=True) + pool_eps)
+
+
+def dot_nt(a, b):
+    return lax.dot_general(a, b, (((1,), (1,)), ((), ())), preferred_element_type=jnp.float32)
+
+
+def halves(x):
+    high = x.astype(jnp.bfloat16)
+    return jnp.concatenate([high, (x - high.astype(jnp.float32)).astype(jnp.bfloat16)])
+
+
+def fold(x):
+    return x[: x.shape[0] // 2] + x[x.shape[0] // 2 :]
+
+
+def gradients(queries, documents, all_queries, all_docs, member):
+    count = queries.shape[0]
+    total = all_docs.shape[0]
+    sums = jnp.sum(jnp.exp(logit_scale * dot_nt(all_docs, all_queries)), axis=0, keepdims=True)
+    columns = jnp.arange(total, dtype=jnp.int32)[None, :]
+    own = columns == (member * count + jnp.arange(count, dtype=jnp.int32))[:, None]
+    pair = jnp.exp(logit_scale * jnp.sum(queries * documents, axis=-1, keepdims=True))
+    rows = jnp.where(own, 0.0, jnp.exp(logit_scale * fold(dot_nt(halves(queries), all_docs))))
+    row_sum = jnp.sum(rows, axis=-1, keepdims=True) + pair
+    diagonal = pair / row_sum - 1.0
+    rest = fold(jnp.dot(halves(rows / row_sum), all_docs, preferred_element_type=jnp.float32))
+    query_grad = logit_scale * (rest + diagonal * documents)
+    cols = jnp.where(own, 0.0, jnp.exp(logit_scale * fold(dot_nt(halves(documents), all_queries))))
+    rest = fold(jnp.dot(halves(cols / sums), all_queries, preferred_element_type=jnp.float32))
+    doc_grad = logit_scale * (rest + diagonal * queries)
+    return query_grad, doc_grad
 
 
 def body(tokens, routes, lengths, norm_gain, router_weight, gate_weight, up_weight, down_weight):
@@ -75,21 +106,23 @@
     pair_count = embedded.shape[0] // 2
     queries = embedded[:pair_count]
     documents = embedded[pair_count:]
-    all_docs = lax.all_gather(documents, ("dp", "expert"), axis=0, tiled=True)
-    total_pairs = all_docs.shape[0]
-    scores = logit_scale * jnp.dot(queries, all_docs.T, precision=lax.Precision.HIGHEST)
-    exps = jnp.exp(scores)
-    likely = exps / jnp.sum(exps, axis=-1, keepdims=True)
-    own_index = lax.axis_index(("dp", "expert")) * pair_count + jnp.arange(
-        pair_count, dtype=jnp.int32
+
+    groups = lax.axis_size("dp")
+    devices = groups * expert_count
+    same_core = [
+        [d for d in range(devices) if (d // expert_count) % 2 == core] for core in range(2)
+    ]
+    chips = devices // 2
+    copies = jnp.broadcast_to(embedded.astype(jnp.bfloat16)[None], (chips,) + embedded.shape)
+    mine = lax.all_to_all(
+        copies, ("dp", "expert"), split_axis=0, concat_axis=0, tiled=True, axis_index_groups=same_core
     )
-    target = (jnp.arange(total_pairs, dtype=jnp.int32)[None, :] == own_index[:, None]).astype(
-        jnp.float32
-    )
-    coefficient = logit_scale * (likely - target)
-    query_grad = jnp.dot(coefficient, all_docs, precision=lax.Precision.HIGHEST)
-    partial_terms = jnp.dot(coefficient.T, queries, precision=lax.Precision.HIGHEST)
-    doc_grad = lax.psum_scatter(partial_terms, ("dp", "expert"), scatter_dimension=0, tiled=True)
+    other = lax.ppermute(mine, "dp", [(i, i ^ 1) for i in range(groups)])
+    both = jnp.concatenate([mine, other])
+    all_queries = both[:, :pair_count].reshape(devices * pair_count, width)
+    all_docs = both[:, pair_count:].reshape(devices * pair_count, width)
+    member = lax.axis_index("dp") // 2 * expert_count + lax.axis_index("expert")
+    query_grad, doc_grad = gradients(queries, documents, all_queries, all_docs, member)
     return (hidden_out, query_grad, doc_grad)
 
 

time: 1060 us -> 138 us (0.13)
  waiting for transfers between devices: 947 us -> 22.7 us
  blocking collectives: 29.9 us -> 58.6 us
  between operations: 14.3 us -> 0.82 us
    reduce_scatter x1 -> x0, waiting for transfers between devices: 622 us -> none  [body(): lax.psum_scatter(partial_terms, ('dp', 'expert'), scatter_dimension=0, ti...]
    all_gather x1 -> x0, waiting for transfers between devices: 303 us -> none  [body(): all_docs = lax.all_gather(documents, ('dp', 'expert'), axis=0, tiled=True)]
    all_to_all x0 -> x1, blocking collectives: none -> 28.7 us  [body(): lax.all_to_all(copies, ('dp', 'expert'), split_axis=0, concat_axis=0, til...]
  transfers between devices with their start and end apart: 3 -> 2, of which waited for: 3 -> 2; matrix products, arithmetic and copies ran while one was open for 1% -> 2% of each run, Pallas kernels for 0% -> 0%
where the time goes in v1:
time: 138 us
  blocking collectives  58.6 us (42%)
  matrix products  33.4 us (24%)
  waiting for transfers between devices  22.7 us (16%)
  other arithmetic  8.74 us (6%)
  local copies, waits for them, and re-layouts  7.02 us (5%)
  starting transfers between devices  6.53 us (5%)
    all_to_all x1, blocking collectives, body(): lax.all_to_all(outgoing, 'expert', split_axis=0, concat_axis=0, tiled=True)  29.9 us
    all_to_all x1, blocking collectives, body(): lax.all_to_all(copies, ('dp', 'expert'), split_axis=0, concat_axis=0, til...  28.7 us
    all_to_all x1, waiting for transfers between devices, body(): lax.all_to_all(results, 'expert', split_axis=0, concat_axis=0, tiled=True)  20.6 us
    dot_general x1, matrix products, expert_rows(): jnp.dot(hidden, w_down, preferred_element_type=jnp.float32)  18.8 us
    dot_general x1, matrix products, expert_rows(): gate_act = jnp.dot(row_block, w_gate, preferred_element_type=jnp.float32)  7.92 us
    all_to_all x1, starting transfers between devices, body(): lax.all_to_all(results, 'expert', split_axis=0, concat_axis=0, tiled=True)  3.9 us
    reduce_sum x1, other arithmetic, body(): jnp.sum(route_weights[:, :, None] * gathered_rows, axis=1)  2.87 us
    dot_general x3, matrix products, dot_nt(): lax.dot_general(a, b, (((1,), (1,)), ((), ())), preferred_element_type=jn...  2.86 us
  transfers between devices with their start and end apart: 2, of which 2 were waited for; matrix products, arithmetic and copies ran while one was open for 2% of the time, Pallas kernels for 0%

profile of v1, /device:TPU:1, one launch (start us, length us, event | category | flops | bytes accessed | tf_op | source)
XLA Modules:
  0.0 137.8 jit_solution(10468169624066676587)
XLA Ops:
  0.6 0.8 copy.26
  1.8 1.1 reduce-window.6
  2.9 0.2 slice_reduce_fusion
  3.3 0.1 reduce_sum.79
  3.5 0.4 fusion.7
  3.9 1.3 fusion.17
  5.3 1.7 %convolution_convert_fusion = bf16[1024,768]{1,0:T(8,128)(2,1)S(1)} fusion(pred[1024,256]{1,0:T(8,128)(4,1)S(1)} %fusion.7, bf16[256,768]{1,0:T(8,128)(2,1)} %param.8, f32[768]{0:T(1024)} %param.11, f32[256]{0:T(256)S(1)} %add_rsqrt_fusion), kind=kOutput, calls=%fused_computation.11 | convolution fusion | flops 404226048 | bytes 2232320 | tf_op jit(solution)/shard_map/dot_general | solution.py:89
  6.9 29.9 %all_to_all.15 = bf16[8,128,768]{2,1,0:T(8,128)(2,1)S(1)} all-to-all(bf16[8,128,768]{2,1,0:T(8,128)(2,1)S(1)} %bitcast.73), channel_id=1, replica_groups=mesh['dp'=16,'expert'=8] {'expert'}, dimensions={0} | all-to-all | bytes 3145728 | tf_op jit(solution)/shard_map/all_to_all | solution.py:94
  36.8 7.9 %fusion.5 = f32[1024,3072]{1,0:T(8,128)} fusion(bf16[1024,768]{1,0:T(8,128)(2,1)S(1)} %bitcast.74, bf16[1,768,3072]{2,1,0:T(8,128)(2,1)S(1)} %copy-done.5), kind=kOutput, calls=%fused_computation.5 | convolution fusion | flops 4831838208 | bytes 18874368 | tf_op jit(solution)/shard_map/dot_general | solution.py:18
  44.8 18.8 %fusion.8 = bf16[1024,768]{1,0:T(8,128)(2,1)} fusion(bf16[1,3072,768]{2,1,0:T(8,128)(2,1)} %param.15, f32[1024,3072]{1,0:T(8,128)} %fusion.5, bf16[1024,768]{1,0:T(8,128)(2,1)S(1)} %bitcast.75, bf16[1,768,3072]{2,1,0:T(8,128)(2,1)} %param.14), kind=kOutput, calls=%fused_computation.10 | convolution fusion | flops 9683337216 | bytes 25165824 | tf_op jit(solution)/shard_map/dot_general | solution.py:21
  63.6 3.9 %all-to-all-start.1 = ((bf16[8,128,768]{2,1,0:T(8,128)(2,1)}), bf16[8,128,768]{2,1,0:T(8,128)(2,1)S(1)}, u32[]{:S(2)}, u32[]{:S(2)}) async-start(bf16[8,128,768]{2,1,0:T(8,128)(2,1)} %bitcast.7), calls=%async_computation.1 | async-start | bytes 3145728 | tf_op jit(solution)/shard_map/all_to_all | solution.py:100
  67.7 0.3 fusion.22
  68.0 0.8 copy.25
  68.9 0.2 reduce_window_sum.28
  69.1 0.5 subtract_bitcast_fusion
  69.6 20.6 %all-to-all-done.1 = bf16[8,128,768]{2,1,0:T(8,128)(2,1)S(1)} async-done(((bf16[8,128,768]{2,1,0:T(8,128)(2,1)}), bf16[8,128,768]{2,1,0:T(8,128)(2,1)S(1)}, u32[]{:S(2)}, u32[]{:S(2)}) %all-to-all-start.1) | async-done | bytes 1572896 | tf_op jit(solution)/shard_map/all_to_all | solution.py:100
  90.2 2.0 %gather_fusion = bf16[512,768]{1,0:T(8,128)(2,1)S(1)} fusion(bf16[1024,768]{1,0:T(8,128)(2,1)S(1)} %bitcast.72, s32[1024]{0:T(1024)S(1)} %pad_clamp_fusion), kind=kCustom, calls=%fused_computation | custom fusion | bytes 1574912 | tf_op jit(solution)/shard_map/gather | solution.py:102
  92.2 0.8 reshape.192
  93.0 2.9 %multiply_reduce_fusion = f32[256,768]{1,0:T(8,128)S(1)} fusion(f32[256,2,768]{2,1,0:T(2,128)S(1)} %reshape.192, f32[256,2]{1,0:T(8,128)} %copy.25), kind=kLoop, calls=%fused_computation.14 | loop fusion | flops 589824 | bytes 2361344 | tf_op jit(solution)/shard_map/reduce_sum | solution.py:103
  95.9 1.2 multiply_reduce_fusion.1
  97.3 28.7 %all_to_all.16 = bf16[64,16,768]{2,1,0:T(8,128)(2,1)S(1)} all-to-all(bf16[64,16,768]{2,1,0:T(8,128)(2,1)S(1)} %broadcast_in_dim.21), channel_id=1, replica_groups={{0,1,2,3,4,5,6,7,16,17,18,19,20,21,22,23,32,33,34,35,36,37,38,39,48,49,..., dimensions={0} | all-to-all | bytes 3145728 | tf_op jit(solution)/shard_map/all_to_all | solution.py:117
  125.9 2.6 %collective-permute-start = (bf16[64,16,768]{2,1,0:T(8,128)(2,1)S(1)}, bf16[64,16,768]{2,1,0:T(8,128)(2,1)}, u32[]{:S(2)}, u32[]{:S(2)}) collective-permute-start(bf16[64,16,768]{2,1,0:T(8,128)(2,1)S(1)} %all_to_all.16), channel_id=1, source_target_pairs={{0,8},{8,0},{16,24},{24,16},{32,40},{40,32},{48,56},{56,48},{64,72... | collective-permute-start | bytes 4718600 | tf_op jit(solution)/shard_map/ppermute | solution.py:120
  128.7 0.8 fusion.20
  129.6 2.1 %collective-permute-done = bf16[64,16,768]{2,1,0:T(8,128)(2,1)} collective-permute-done((bf16[64,16,768]{2,1,0:T(8,128)(2,1)S(1)}, bf16[64,16,768]{2,1,0:T(8,128)(2,1)}, u32[]{:S(2)}, u32[]{:S(2)}) %collective-permute-start) | collective-permute-done | bytes 1572896 | tf_op jit(solution)/shard_map/ppermute | solution.py:120
  131.7 1.5 %constant_dynamic-update-slice_fusion = bf16[128,16,768]{2,1,0:T(8,128)(2,1)S(1)} fusion(bf16[128,16,768]{2,1,0:T(8,128)(2,1)S(1)} %constant_dynamic-update-slice_fusion.1, bf16[64,16,768]{2,1,0:T(8,128)(2,1)} %collective-permute-done), kind=kLoop, calls=%fused_computation.87 | loop fusion | bytes 3145728 | tf_op jit(solution)/shard_map/concatenate | solution.py:121
  133.2 1.8 %exponential_reduce_fusion = f32[1024]{0:T(1024)S(1)} fusion(bf16[128,16,768]{2,1,0:T(8,128)(2,1)S(1)} %constant_dynamic-update-slice_fusion), kind=kOutput, calls=%fused_computation.7 | convolution fusion | flops 1612708864 | bytes 3149824 | tf_op jit(solution)/shard_map/dot_general | solution.py:38
  135.1 0.5 fusion.16
  135.6 0.5 fusion.14
  136.1 0.2 fusion.66
  136.4 0.3 fusion.13
  136.7 0.3 fusion.15
  137.1 0.7 fusion.38
  (35 shorter events, 1.3 us)
Async XLA Ops:
  0.6 67.0 %copy-start = (bf16[768,8]{0,1:T(8,128)(2,1)S(1)}, bf16[768,8]{0,1:T(8,128)(2,1)}, u32[]{:S(2)}) copy-start(bf16[768,8]{0,1:T(8,128)(2,1)} %param.12) | copy-start | bytes 36868
  3.5 33.3 %copy-start.5 = (bf16[1,768,3072]{2,1,0:T(8,128)(2,1)S(1)}, bf16[1,768,3072]{2,1,0:T(8,128)(2,1)}, u32[]{:S(2)}) copy-start(bf16[1,768,3072]{2,1,0:T(8,128)(2,1)} %param.13) | copy-start | bytes 14155780
  63.6 4.1 %copy-start.1 = (bf16[256,768]{1,0:T(8,128)(2,1)S(1)}, bf16[256,768]{1,0:T(8,128)(2,1)}, u32[]{:S(2)}) copy-start(bf16[256,768]{1,0:T(8,128)(2,1)} %param.8) | copy-start | bytes 1179652
  63.6 4.1 %copy-start.3 = (f32[768]{0:T(1024)S(1)}, f32[768]{0:T(1024)}, u32[]{:S(2)}) copy-start(f32[768]{0:T(1024)} %param.11) | copy-start | bytes 9220
  63.6 4.4 %copy-start.2 = (s32[256,2]{0,1:T(2,128)S(1)}, s32[256,2]{0,1:T(2,128)}, u32[]{:S(2)}) copy-start(s32[256,2]{0,1:T(2,128)} %param.9) | copy-start | bytes 6148
  63.6 5.3 %copy-start.4 = (s32[1,16]{1,0:T(1,128)S(1)}, s32[1,16]{1,0:T(1,128)}, u32[]{:S(2)}) copy-start(s32[1,16]{1,0:T(1,128)} %param.10) | copy-start | bytes 196
  63.6 26.6 %all-to-all-start.1 = ((bf16[8,128,768]{2,1,0:T(8,128)(2,1)}), bf16[8,128,768]{2,1,0:T(8,128)(2,1)S(1)}, u32[]{:S(2)}, u32[]{:S(2)}) async-start(bf16[8,128,768]{2,1,0:T(8,128)(2,1)} %bitcast.7), calls=%async_computation.1 | async-start | bytes 3145728 | tf_op jit(solution)/shard_map/all_to_all | solution.py:100
  125.9 5.8 %collective-permute-start = (bf16[64,16,768]{2,1,0:T(8,128)(2,1)S(1)}, bf16[64,16,768]{2,1,0:T(8,128)(2,1)}, u32[]{:S(2)}, u32[]{:S(2)}) collective-permute-start(bf16[64,16,768]{2,1,0:T(8,128)(2,1)S(1)} %all_to_all.16), channel_id=1, source_target_pairs={{0,8},{8,0},{16,24},{24,16},{32,40},{40,32},{48,56},{56,48},{64,72... | collective-permute-start | bytes 4718600 | tf_op jit(solution)/shard_map/ppermute | solution.py:120

commit v2 on v0

v2 whole, which is shorter than its diff:
```python
import functools

import jax
import jax.numpy as jnp
from jax import lax
from jax.experimental import pallas as pl
from jax.experimental.pallas import tpu as pltpu
from jax.sharding import PartitionSpec as P

logit_scale = 50.0
norm_eps = 1e-06
pool_eps = 1e-06
f32 = jnp.float32
bf16 = jnp.bfloat16
vmem_budget = 56 * 1024 * 1024


def dot(a, b):
    return jnp.dot(a, b, preferred_element_type=f32)


def dot_nt(a, b):
    return lax.dot_general(a, b, (((1,), (1,)), ((), ())), preferred_element_type=f32)


def iota(shape, axis):
    return lax.broadcasted_iota(jnp.int32, shape, axis)


def split(x):
    high = x.astype(bf16)
    return high, (x - high.astype(f32)).astype(bf16)


def fold(x):
    return x[: x.shape[0] // 2] + x[x.shape[0] // 2 :]


def call(kernel, outs, *operands, **options):
    return pl.pallas_call(
        kernel,
        out_shape=outs,
        compiler_params=pltpu.CompilerParams(vmem_limit_bytes=vmem_budget),
        **options,
    )(*operands)


def route_kernel(tokens_ref, routes_ref, gain_ref, router_ref, out_ref, slots_ref, weights_ref):
    rows = tokens_ref.shape[0]
    experts = router_ref.shape[0]
    capacity = out_ref.shape[0] // experts
    widened = tokens_ref[...].astype(f32)
    inverse = lax.rsqrt(jnp.mean(widened * widened, axis=-1, keepdims=True) + norm_eps)
    normed = (widened * inverse * gain_ref[...]).astype(bf16)
    labels = iota((experts, rows), 0)
    hit = (routes_ref[0:1, :] == labels) | (routes_ref[1:2, :] == labels)
    hits = jnp.where(hit, 1.0, 0.0).astype(bf16)
    down, across = iota((rows, rows), 0), iota((rows, rows), 1)
    ranks = dot(hits, jnp.where(down < across, 1.0, 0.0).astype(bf16))
    ranks = jnp.where(hit, ranks, -1.0)
    places = iota((capacity, rows), 0).astype(f32)
    for e in range(experts):
        chosen = jnp.where(places == ranks[e : e + 1, :], 1.0, 0.0).astype(bf16)
        out_ref[e * capacity : (e + 1) * capacity, :] = dot(chosen, normed).astype(bf16)
    hits_down = dot_nt(jnp.where(down == across, 1.0, 0.0).astype(bf16), hits)
    ranks_down = dot_nt(jnp.where(across < down, 1.0, 0.0).astype(bf16), hits)
    logits = dot_nt(normed, router_ref[...])
    both = jnp.sum(hits_down * logits, axis=-1, keepdims=True)
    slots_ref[...] = jnp.where(hits_down > 0.5, ranks_down, -1.0)
    weights_ref[...] = hits_down / (1.0 + jnp.exp(both - 2.0 * logits))


def expert_kernel(x_ref, gate_ref, up_ref, down_ref, out_ref, acc_ref, *, chunk):
    step, last = pl.program_id(0), pl.num_programs(0) - 1
    for at in range(0, x_ref.shape[0], chunk):
        rows = pl.ds(at, chunk)
        x = x_ref[rows, :]
        gate_act = dot(x, gate_ref[...])
        up_act = dot(x, up_ref[...])
        hidden = (gate_act / (1.0 + jnp.exp(-gate_act)) * up_act).astype(bf16)
        part = dot(hidden, down_ref[...])

        @pl.when(step == 0)
        def _():
            acc_ref[rows, :] = part

        @pl.when((step > 0) & (step < last))
        def _():
            acc_ref[rows, :] += part

        @pl.when(step == last)
        def _():
            out_ref[rows, :] = (acc_ref[rows, :] + part).astype(bf16)


def expert_rows(x, w_gate, w_up, w_down, block=512, chunk=1024):
    rows, width = x.shape
    hidden = w_gate.shape[1]
    whole = pl.BlockSpec((rows, width), lambda i: (0, 0))
    return pl.pallas_call(
        functools.partial(expert_kernel, chunk=chunk),
        out_shape=jax.ShapeDtypeStruct((rows, width), bf16),
        grid=(hidden // block,),
        in_specs=[
            whole,
            pl.BlockSpec((width, block), lambda i: (0, i)),
            pl.BlockSpec((width, block), lambda i: (0, i)),
            pl.BlockSpec((block, width), lambda i: (i, 0)),
        ],
        out_specs=whole,
        scratch_shapes=[pltpu.VMEM((rows, width), f32)],
        compiler_params=pltpu.CompilerParams(vmem_limit_bytes=vmem_budget),
    )(x, w_gate, w_up, w_down)


def combine_kernel(tokens_ref, slots_ref, weights_ref, back_ref, lengths_ref, hidden_ref, embedded_ref):
    rows = tokens_ref.shape[0]
    experts = slots_ref.shape[1]
    capacity = back_ref.shape[0] // experts
    lanes = iota((rows, capacity), 1).astype(f32)
    terms = [
        jnp.where(lanes == slots_ref[:, e : e + 1], weights_ref[:, e : e + 1], 0.0)
        for e in range(experts)
    ]
    high, low = split(jnp.concatenate(terms, axis=1))
    back = back_ref[...]
    mixed = tokens_ref[...].astype(f32) + (dot(high, back) + dot(low, back))
    hidden_ref[...] = mixed.astype(bf16)
    count = lengths_ref.shape[1]
    spans = jnp.broadcast_to(lengths_ref[...], (count, count)).astype(f32)
    down, across = iota((count, count), 0), iota((count, count), 1)
    ends = jnp.sum(jnp.where(across <= down, spans, 0.0), axis=1, keepdims=True)
    sizes = jnp.sum(jnp.where(across == down, spans, 0.0), axis=1, keepdims=True)
    places = iota((count, rows), 1).astype(f32)
    member = jnp.where((places >= ends - sizes) & (places < ends), 1.0, 0.0).astype(bf16)
    first, rest = split(mixed)
    second, third = split(mixed - first.astype(f32))
    pooled = (dot(member, first) + dot(member, second) + dot(member, third)) / sizes
    embedded_ref[...] = pooled * lax.rsqrt(
        jnp.sum(pooled * pooled, axis=-1, keepdims=True) + pool_eps
    )


def gradients(queries_ref, docs_ref, embedded_ref, first, query_grad_ref, doc_grad_ref):
    embedded = embedded_ref[...]
    count = embedded.shape[0] // 2
    total = queries_ref.shape[0]
    queries, documents = embedded[:count], embedded[count:]
    all_queries, all_docs = queries_ref[...], docs_ref[...]
    block = 256
    sums = jnp.zeros((1, total), f32)
    for at in range(0, total, block):
        scores = dot_nt(docs_ref[at : at + block, :], all_queries)
        sums = sums + jnp.sum(jnp.exp(logit_scale * scores), axis=0, keepdims=True)
    stacked = jnp.concatenate(split(embedded), axis=0)
    rows = fold(dot_nt(stacked, all_docs))[:count]
    cols = fold(dot_nt(stacked, all_queries))[count:]
    own = iota((count, total), 1) == first + iota((count, total), 0)
    pair = jnp.exp(logit_scale * jnp.sum(queries * documents, axis=-1, keepdims=True))
    rows = jnp.where(own, 0.0, jnp.exp(logit_scale * rows))
    cols = jnp.where(own, 0.0, jnp.exp(logit_scale * cols))
    row_sum = jnp.sum(rows, axis=-1, keepdims=True) + pair
    diagonal = pair / row_sum - 1.0
    likely = jnp.concatenate([rows / row_sum, cols / sums], axis=0)
    likely = jnp.concatenate(split(likely), axis=0)
    query_grad_ref[...] = logit_scale * (fold(dot(likely, all_docs))[:count] + diagonal * documents)
    doc_grad_ref[...] = logit_scale * (fold(dot(likely, all_queries))[count:] + diagonal * queries)


def gradient_kernel(place_ref, mine_ref, other_ref, embedded_ref, query_grad_ref, doc_grad_ref):
    core, first = place_ref[0], place_ref[1]

    @pl.when(core == 0)
    def _():
        gradients(mine_ref, other_ref, embedded_ref, first, query_grad_ref, doc_grad_ref)

    @pl.when(core == 1)
    def _():
        gradients(other_ref, mine_ref, embedded_ref, first, query_grad_ref, doc_grad_ref)


def route(tokens, routes, norm_gain, router_weight):
    rows, width = tokens.shape
    experts = router_weight.shape[1]
    return call(
        route_kernel,
        [
            jax.ShapeDtypeStruct((rows // 2 * experts, width), bf16),
            jax.ShapeDtypeStruct((rows, experts), f32),
            jax.ShapeDtypeStruct((rows, experts), f32),
        ],
        tokens, routes.T, norm_gain[None], router_weight.T,
    )


def combine(tokens, slots, weights, back, lengths):
    return call(
        combine_kernel,
        [
            jax.ShapeDtypeStruct(tokens.shape, bf16),
            jax.ShapeDtypeStruct((lengths.shape[1], tokens.shape[1]), f32),
        ],
        tokens, slots, weights, back, lengths,
    )


def info_nce(place, mine, other, embedded):
    out = jax.ShapeDtypeStruct((embedded.shape[0] // 2, embedded.shape[1]), f32)
    vmem = pl.BlockSpec(memory_space=pltpu.VMEM)
    return call(
        gradient_kernel, [out, out], place, mine, other, embedded,
        in_specs=[pl.BlockSpec(memory_space=pltpu.SMEM), vmem, vmem, vmem],
    )


def body(tokens, routes, lengths, norm_gain, router_weight, gate_weight, up_weight, down_weight):
    width = tokens.shape[1]
    experts = router_weight.shape[1]
    outgoing, slots, weights = route(tokens, routes, norm_gain, router_weight)
    outgoing = outgoing.reshape(experts, -1, width)
    incoming = lax.all_to_all(outgoing, "expert", split_axis=0, concat_axis=0, tiled=True)
    results = expert_rows(
        incoming.reshape(-1, width), gate_weight[0], up_weight[0], down_weight[0]
    )
    results = results.reshape(experts, -1, width)
    returned = lax.all_to_all(results, "expert", split_axis=0, concat_axis=0, tiled=True)
    hidden_out, embedded = combine(tokens, slots, weights, returned.reshape(-1, width), lengths)

    pairs = embedded.shape[0] // 2
    groups = lax.axis_size("dp")
    devices = groups * experts
    chips = devices // 2
    same_core = [[d for d in range(devices) if d // experts % 2 == core] for core in range(2)]
    swap = [(i, i ^ 1) for i in range(groups)]
    core = lax.axis_index("dp") % 2
    rounded = embedded.astype(bf16)
    kept = jnp.where(core == 0, rounded[:pairs], rounded[pairs:])
    given = jnp.where(core == 0, rounded[pairs:], rounded[:pairs])
    taken = lax.ppermute(given, "dp", swap)
    shard = jnp.concatenate(
        [jnp.where(core == 0, kept, taken), jnp.where(core == 0, taken, kept)]
    )
    copies = jnp.broadcast_to(shard[None], (chips,) + shard.shape)
    mine = lax.all_to_all(
        copies, ("dp", "expert"), split_axis=0, concat_axis=0, tiled=True, axis_index_groups=same_core
    ).reshape(-1, width)
    other = lax.ppermute(mine, "dp", swap)
    chip = lax.axis_index("dp") // 2 * experts + lax.axis_index("expert")
    place = jnp.stack([core, (chip * 2 + core) * pairs]).astype(jnp.int32)
    query_grad, doc_grad = info_nce(place, mine, other, embedded)
    return (hidden_out, query_grad, doc_grad)


def solution(mesh):
    placed = (
        P(("dp", "expert"), None),
        P(("dp", "expert"), None),
        P(("dp", "expert"), None),
        P(),
        P(),
        P("expert", None, None),
        P("expert", None, None),
        P("expert", None, None),
    )
    return jax.shard_map(
        body,
        mesh=mesh,
        in_specs=placed,
        out_specs=(P(("dp", "expert"), None), P(("dp", "expert"), None), P(("dp", "expert"), None)),
        check_vma=False,
    )
```

time: 1060 us -> 133 us (0.13)
  waiting for transfers between devices: 947 us -> 26.1 us
  matrix products: 41.2 us -> 0 us
  Pallas kernels: 0 us -> 34.8 us
  blocking collectives: 29.9 us -> 59.1 us
  between operations: 14.3 us -> 0.67 us
    reduce_scatter x1 -> x0, waiting for transfers between devices: 622 us -> none  [body(): lax.psum_scatter(partial_terms, ('dp', 'expert'), scatter_dimension=0, ti...]
    all_gather x1 -> x0, waiting for transfers between devices: 303 us -> none  [body(): all_docs = lax.all_gather(documents, ('dp', 'expert'), axis=0, tiled=True)]
    dot_general x8 -> x0, matrix products: 41.2 us -> none  [the longest x1 18.8 us: expert_rows(): jnp.dot(hidden, w_down, preferred_element_type=jnp.float32)]
    pallas_call x0 -> x4, Pallas kernels: none -> 34.8 us  [the longest x1 21.8 us: expert_rows(): pl.pallas_call(functools.partial(expert_kernel, chunk=chunk), out_shape=j...]
    all_to_all x0 -> x1, blocking collectives: none -> 28.9 us  [body(): lax.all_to_all(copies, ('dp', 'expert'), split_axis=0, concat_axis=0, til...]
  transfers between devices with their start and end apart: 3 -> 3, of which waited for: 3 -> 3; matrix products, arithmetic and copies ran while one was open for 1% -> 0% of each run, Pallas kernels for 0% -> 0%
where the time goes in v2:
time: 133 us
  blocking collectives  59.1 us (44%)
  Pallas kernels  34.8 us (26%)
  waiting for transfers between devices  26.1 us (20%)
  starting transfers between devices  7.01 us (5%)
  local copies, waits for them, and re-layouts  3.68 us (3%)
  other arithmetic  1.4 us (1%)
    all_to_all x1, blocking collectives, body(): lax.all_to_all(outgoing, 'expert', split_axis=0, concat_axis=0, tiled=True)  30.2 us
    all_to_all x1, blocking collectives, body(): lax.all_to_all(copies, ('dp', 'expert'), split_axis=0, concat_axis=0, til...  28.9 us
    all_to_all x1, waiting for transfers between devices, body(): lax.all_to_all(results, 'expert', split_axis=0, concat_axis=0, tiled=True)  22.8 us
    pallas_call x1, Pallas kernels, expert_rows(): pl.pallas_call(functools.partial(expert_kernel, chunk=chunk), out_shape=j...  21.8 us
    pallas_call x3, Pallas kernels, call(): pl.pallas_call(kernel, out_shape=outs, compiler_params=pltpu.CompilerPara...  13 us
    all_to_all x1, starting transfers between devices, body(): lax.all_to_all(results, 'expert', split_axis=0, concat_axis=0, tiled=True)  3.58 us
  transfers between devices with their start and end apart: 3, of which 3 were waited for; matrix products, arithmetic and copies ran while one was open for 0% of the time, Pallas kernels for 0%

profile of v2, /device:TPU:1, one launch (start us, length us, event | category | flops | bytes accessed | tf_op | source)
XLA Modules:
  0.0 132.9 jit_solution(12781199557477032749)
XLA Ops:
  0.6 1.3 broadcast_in_dim.4.gain_ref
  1.9 3.0 %shard_map.103 = (bf16[1024,768]{1,0:T(8,128)(2,1)}, f32[256,8]{1,0:T(8,128)}, f32[256,8]{1,0:T(8,128)}) custom-call(bf16[256,768]{1,0:T(8,128)(2,1)} %tokens_ref.3, s32[2,256]{1,0:T(2,128)} %bitcast.22, f32[1,768]{1,0:T(1,128)} %broadcast_in_dim.4.gain_ref, bf16[8,768]{1,0:T(8,128)(2,1)} %bitcast.21), custom_call_target="tpu_custom_call" | custom-call | tf_op jit(solution)/shard_map/pallas_call | solution.py:40
  4.9 30.2 %all_to_all.15 = bf16[8,128,768]{2,1,0:T(8,128)(2,1)} all-to-all(bf16[8,128,768]{2,1,0:T(8,128)(2,1)} %bitcast.20), channel_id=1, replica_groups=mesh['dp'=16,'expert'=8] {'expert'}, dimensions={0} | all-to-all | bytes 3145728 | tf_op jit(solution)/shard_map/all_to_all | solution.py:221
  35.1 21.8 %shard_map.104 = bf16[1024,768]{1,0:T(8,128)(2,1)} custom-call(bf16[1024,768]{1,0:T(8,128)(2,1)} %bitcast.14, bf16[768,3072]{1,0:T(8,128)(2,1)} %bitcast.17, bf16[768,3072]{1,0:T(8,128)(2,1)} %bitcast.18, bf16[3072,768]{1,0:T(8,128)(2,1)} %bitcast.19), custom_call_target="tpu_custom_call" | custom-call | tf_op jit(solution)/shard_map/pallas_call | solution.py:100
  56.9 3.6 %all-to-all-start.1 = ((bf16[8,128,768]{2,1,0:T(8,128)(2,1)}), bf16[8,128,768]{2,1,0:T(8,128)(2,1)S(1)}, u32[]{:S(2)}, u32[]{:S(2)}) async-start(bf16[8,128,768]{2,1,0:T(8,128)(2,1)} %bitcast.13), calls=%async_computation.1 | async-start | bytes 3145728 | tf_op jit(solution)/shard_map/all_to_all | solution.py:226
  60.5 22.8 %all-to-all-done.1 = bf16[8,128,768]{2,1,0:T(8,128)(2,1)S(1)} async-done(((bf16[8,128,768]{2,1,0:T(8,128)(2,1)}), bf16[8,128,768]{2,1,0:T(8,128)(2,1)S(1)}, u32[]{:S(2)}, u32[]{:S(2)}) %all-to-all-start.1) | async-done | bytes 1572896 | tf_op jit(solution)/shard_map/all_to_all | solution.py:226
  83.3 0.0 copy-start
  83.3 1.1 copy-done
  84.5 4.3 %shard_map.105 = (bf16[256,768]{1,0:T(8,128)(2,1)}, f32[16,768]{1,0:T(8,128)}) custom-call(bf16[256,768]{1,0:T(8,128)(2,1)} %tokens_ref.3, f32[256,8]{1,0:T(8,128)} %get-tuple-element.10.slots_ref, f32[256,8]{1,0:T(8,128)} %get-tuple-element.11.weights_ref, bf16[1024,768]{1,0:T(8,128)(2,1)} %bitcast.12, s32[1,16]{1,0:T(1,128)} %lengths_ref.1), custom_call_target="tpu_custom_call" | custom-call | tf_op jit(solution)/shard_map/pallas_call | solution.py:40
  88.8 0.8 convert_element_type.3
  89.6 0.9 collective-permute-start
  90.5 0.8 collective-permute-done
  91.4 0.1 broadcast_in_dim.10
  91.5 28.9 %all_to_all.16 = bf16[64,16,768]{2,1,0:T(8,128)(2,1)S(1)} all-to-all(bf16[64,16,768]{2,1,0:T(8,128)(2,1)S(1)} %broadcast_in_dim.10), channel_id=1, replica_groups={{0,1,2,3,4,5,6,7,16,17,18,19,20,21,22,23,32,33,34,35,36,37,38,39,48,49,..., dimensions={0} | all-to-all | bytes 3145728 | tf_op jit(solution)/shard_map/all_to_all | solution.py:244
  120.4 0.0 copy-start.1
  120.4 2.5 %collective-permute-start.1 = (bf16[1024,768]{1,0:T(8,128)(2,1)S(1)}, bf16[1024,768]{1,0:T(8,128)(2,1)S(1)}, u32[]{:S(2)}, u32[]{:S(2)}) collective-permute-start(bf16[1024,768]{1,0:T(8,128)(2,1)S(1)} %bitcast.15), channel_id=1, source_target_pairs={{0,8},{8,0},{16,24},{24,16},{32,40},{40,32},{48,56},{56,48},{64,72... | collective-permute-start | bytes 4718600 | tf_op jit(solution)/shard_map/ppermute | solution.py:247
  122.9 0.6 pad_add_fusion.place_ref
  123.5 2.5 %collective-permute-done.1.other_ref = bf16[1024,768]{1,0:T(8,128)(2,1)S(1)} collective-permute-done((bf16[1024,768]{1,0:T(8,128)(2,1)S(1)}, bf16[1024,768]{1,0:T(8,128)(2,1)S(1)}, u32[]{:S(2)}, u32[]{:S(2)}) %collective-permute-start.1) | collective-permute-done | bytes 1572896 | tf_op jit(solution)/shard_map/ppermute | solution.py:247
  126.0 0.0 copy-done.1
  126.0 0.0 copy-start.2
  126.0 1.2 copy-done.2
  127.1 5.7 %shard_map.106 = (f32[8,768]{1,0:T(8,128)}, f32[8,768]{1,0:T(8,128)}) custom-call(s32[2]{0:T(128)} %pad_add_fusion.place_ref, bf16[1024,768]{1,0:T(8,128)(2,1)} %bitcast.16, bf16[1024,768]{1,0:T(8,128)(2,1)} %copy-done.2, f32[16,768]{1,0:T(8,128)} %get-tuple-element.14.embedded_ref), custom_call_target="tpu_custom_call" | custom-call | tf_op jit(solution)/shard_map/pallas_call | solution.py:40
  (3 shorter events, 0.0 us)
Async XLA Ops:
  56.9 26.5 %all-to-all-start.1 = ((bf16[8,128,768]{2,1,0:T(8,128)(2,1)}), bf16[8,128,768]{2,1,0:T(8,128)(2,1)S(1)}, u32[]{:S(2)}, u32[]{:S(2)}) async-start(bf16[8,128,768]{2,1,0:T(8,128)(2,1)} %bitcast.13), calls=%async_computation.1 | async-start | bytes 3145728 | tf_op jit(solution)/shard_map/all_to_all | solution.py:226
  83.3 1.2 copy-start
  89.6 1.8 %collective-permute-start = (bf16[8,768]{1,0:T(8,128)(2,1)S(1)}, bf16[8,768]{1,0:T(8,128)(2,1)S(1)}, u32[]{:S(2)}, u32[]{:S(2)}) collective-permute-start(bf16[8,768]{1,0:T(8,128)(2,1)S(1)} %broadcast_select_fusion.2), channel_id=1, source_target_pairs={{0,8},{8,0},{16,24},{24,16},{32,40},{40,32},{48,56},{56,48},{64,72... | collective-permute-start | bytes 36872 | tf_op jit(solution)/shard_map/ppermute | solution.py:239
  120.4 5.5 %copy-start.1 = (bf16[64,16,768]{2,1,0:T(8,128)(2,1)}, bf16[64,16,768]{2,1,0:T(8,128)(2,1)S(1)}, u32[]{:S(2)}) copy-start(bf16[64,16,768]{2,1,0:T(8,128)(2,1)S(1)} %all_to_all.16) | copy-start | bytes 4718596
  120.4 5.5 %collective-permute-start.1 = (bf16[1024,768]{1,0:T(8,128)(2,1)S(1)}, bf16[1024,768]{1,0:T(8,128)(2,1)S(1)}, u32[]{:S(2)}, u32[]{:S(2)}) collective-permute-start(bf16[1024,768]{1,0:T(8,128)(2,1)S(1)} %bitcast.15), channel_id=1, source_target_pairs={{0,8},{8,0},{16,24},{24,16},{32,40},{40,32},{48,56},{56,48},{64,72... | collective-permute-start | bytes 4718600 | tf_op jit(solution)/shard_map/ppermute | solution.py:247
  126.0 1.2 copy-start.2

commit v3 on v2

--- a/solution.py
+++ b/solution.py
@@ -12,7 +12,7 @@
 pool_eps = 1e-06
 f32 = jnp.float32
 bf16 = jnp.bfloat16
-vmem_budget = 56 * 1024 * 1024
+mebibyte = 1024 * 1024
 
 
 def dot(a, b):
@@ -36,11 +36,14 @@
     return x[: x.shape[0] // 2] + x[x.shape[0] // 2 :]
 
 
-def call(kernel, outs, *operands, **options):
+def call(kernel, outs, *operands, budget=16, **options):
+    whole = pl.BlockSpec(memory_space=pltpu.VMEM)
     return pl.pallas_call(
         kernel,
         out_shape=outs,
-        compiler_params=pltpu.CompilerParams(vmem_limit_bytes=vmem_budget),
+        in_specs=[whole] * len(operands),
+        out_specs=jax.tree.map(lambda _: whole, outs),
+        compiler_params=pltpu.CompilerParams(vmem_limit_bytes=budget * mebibyte),
         **options,
     )(*operands)
 
@@ -70,50 +73,32 @@
     weights_ref[...] = hits_down / (1.0 + jnp.exp(both - 2.0 * logits))
 
 
-def expert_kernel(x_ref, gate_ref, up_ref, down_ref, out_ref, acc_ref, *, chunk):
-    step, last = pl.program_id(0), pl.num_programs(0) - 1
-    for at in range(0, x_ref.shape[0], chunk):
-        rows = pl.ds(at, chunk)
-        x = x_ref[rows, :]
-        gate_act = dot(x, gate_ref[...])
-        up_act = dot(x, up_ref[...])
-        hidden = (gate_act / (1.0 + jnp.exp(-gate_act)) * up_act).astype(bf16)
-        part = dot(hidden, down_ref[...])
-
-        @pl.when(step == 0)
-        def _():
-            acc_ref[rows, :] = part
-
-        @pl.when((step > 0) & (step < last))
-        def _():
-            acc_ref[rows, :] += part
-
-        @pl.when(step == last)
-        def _():
-            out_ref[rows, :] = (acc_ref[rows, :] + part).astype(bf16)
-
-
-def expert_rows(x, w_gate, w_up, w_down, block=512, chunk=1024):
-    rows, width = x.shape
-    hidden = w_gate.shape[1]
-    whole = pl.BlockSpec((rows, width), lambda i: (0, 0))
-    return pl.pallas_call(
-        functools.partial(expert_kernel, chunk=chunk),
-        out_shape=jax.ShapeDtypeStruct((rows, width), bf16),
-        grid=(hidden // block,),
-        in_specs=[
-            whole,
-            pl.BlockSpec((width, block), lambda i: (0, i)),
-            pl.BlockSpec((width, block), lambda i: (0, i)),
-            pl.BlockSpec((block, width), lambda i: (i, 0)),
-        ],
-        out_specs=whole,
-        scratch_shapes=[pltpu.VMEM((rows, width), f32)],
-        compiler_params=pltpu.CompilerParams(vmem_limit_bytes=vmem_budget),
-    )(x, w_gate, w_up, w_down)
-
-
-def combine_kernel(tokens_ref, slots_ref, weights_ref, back_ref, lengths_ref, hidden_ref, embedded_ref):
+def expert_kernel(x_ref, gate_ref, up_ref, down_ref, out_ref, hidden_ref, *, block):
+    def columns(step, carry):
+        part = pl.ds(pl.multiple_of(step * block, block), block)
+        x = x_ref[...]
+        gate_act = dot(x, gate_ref[:, part])
+        up_act = dot(x, up_ref[:, part])
+        hidden_ref[:, part] = (gate_act / (1.0 + jnp.exp(-gate_act)) * up_act).astype(bf16)
+        return carry
+
+    lax.fori_loop(0, hidden_ref.shape[1] // block, columns, 0)
+    out_ref[...] = dot(hidden_ref[...], down_ref[...]).astype(bf16)
+
+
+def expert_rows(x, w_gate, w_up, w_down, block=512):
+    return call(
+        functools.partial(expert_kernel, block=block),
+        jax.ShapeDtypeStruct(x.shape, bf16),
+        x, w_gate, w_up, w_down,
+        budget=36,
+        scratch_shapes=[pltpu.VMEM((x.shape[0], w_gate.shape[1]), bf16)],
+    )
+
+
+def combine_kernel(
+    tokens_ref, slots_ref, weights_ref, back_ref, lengths_ref, hidden_ref, embedded_ref, kept_ref, given_ref
+):
     rows = tokens_ref.shape[0]
     experts = slots_ref.shape[1]
     capacity = back_ref.shape[0] // experts
@@ -136,9 +121,12 @@
     first, rest = split(mixed)
     second, third = split(mixed - first.astype(f32))
     pooled = (dot(member, first) + dot(member, second) + dot(member, third)) / sizes
-    embedded_ref[...] = pooled * lax.rsqrt(
-        jnp.sum(pooled * pooled, axis=-1, keepdims=True) + pool_eps
-    )
+    embedded = pooled * lax.rsqrt(jnp.sum(pooled * pooled, axis=-1, keepdims=True) + pool_eps)
+    embedded_ref[...] = embedded
+    queries, documents = embedded[: count // 2], embedded[count // 2 :]
+    first_core = lax.axis_index("dp") % 2 == 0
+    kept_ref[...] = jnp.where(first_core, queries, documents).astype(bf16)
+    given_ref[...] = jnp.where(first_core, documents, queries).astype(bf16)
 
 
 def gradients(queries_ref, docs_ref, embedded_ref, first, query_grad_ref, doc_grad_ref):
@@ -167,8 +155,11 @@
     doc_grad_ref[...] = logit_scale * (fold(dot(likely, all_queries))[count:] + diagonal * queries)
 
 
-def gradient_kernel(place_ref, mine_ref, other_ref, embedded_ref, query_grad_ref, doc_grad_ref):
-    core, first = place_ref[0], place_ref[1]
+def gradient_kernel(mine_ref, other_ref, embedded_ref, query_grad_ref, doc_grad_ref):
+    dp = lax.axis_index("dp")
+    core = dp % 2
+    chip = dp // 2 * lax.axis_size("expert") + lax.axis_index("expert")
+    first = (chip * 2 + core) * (embedded_ref.shape[0] // 2)
 
     @pl.when(core == 0)
     def _():
@@ -189,28 +180,28 @@
             jax.ShapeDtypeStruct((rows, experts), f32),
             jax.ShapeDtypeStruct((rows, experts), f32),
         ],
-        tokens, routes.T, norm_gain[None], router_weight.T,
+        tokens, routes.T, norm_gain, router_weight.T,
     )
 
 
 def combine(tokens, slots, weights, back, lengths):
+    count, width = lengths.shape[1], tokens.shape[1]
+    half = jax.ShapeDtypeStruct((count // 2, width), bf16)
     return call(
         combine_kernel,
         [
             jax.ShapeDtypeStruct(tokens.shape, bf16),
-            jax.ShapeDtypeStruct((lengths.shape[1], tokens.shape[1]), f32),
+            jax.ShapeDtypeStruct((count, width), f32),
+            half,
+            half,
         ],
         tokens, slots, weights, back, lengths,
     )
 
 
-def info_nce(place, mine, other, embedded):
+def info_nce(mine, other, embedded):
     out = jax.ShapeDtypeStruct((embedded.shape[0] // 2, embedded.shape[1]), f32)
-    vmem = pl.BlockSpec(memory_space=pltpu.VMEM)
-    return call(
-        gradient_kernel, [out, out], place, mine, other, embedded,
-        in_specs=[pl.BlockSpec(memory_space=pltpu.SMEM), vmem, vmem, vmem],
-    )
+    return call(gradient_kernel, [out, out], mine, other, embedded)
 
 
 def body(tokens, routes, lengths, norm_gain, router_weight, gate_weight, up_weight, down_weight):
@@ -224,18 +215,16 @@
     )
     results = results.reshape(experts, -1, width)
     returned = lax.all_to_all(results, "expert", split_axis=0, concat_axis=0, tiled=True)
-    hidden_out, embedded = combine(tokens, slots, weights, returned.reshape(-1, width), lengths)
-
-    pairs = embedded.shape[0] // 2
+    hidden_out, embedded, kept, given = combine(
+        tokens, slots, weights, returned.reshape(-1, width), lengths
+    )
+
     groups = lax.axis_size("dp")
     devices = groups * experts
     chips = devices // 2
     same_core = [[d for d in range(devices) if d // experts % 2 == core] for core in range(2)]
     swap = [(i, i ^ 1) for i in range(groups)]
     core = lax.axis_index("dp") % 2
-    rounded = embedded.astype(bf16)
-    kept = jnp.where(core == 0, rounded[:pairs], rounded[pairs:])
-    given = jnp.where(core == 0, rounded[pairs:], rounded[:pairs])
     taken = lax.ppermute(given, "dp", swap)
     shard = jnp.concatenate(
         [jnp.where(core == 0, kept, taken), jnp.where(core == 0, taken, kept)]
@@ -245,9 +234,7 @@
         copies, ("dp", "expert"), split_axis=0, concat_axis=0, tiled=True, axis_index_groups=same_core
     ).reshape(-1, width)
     other = lax.ppermute(mine, "dp", swap)
-    chip = lax.axis_index("dp") // 2 * experts + lax.axis_index("expert")
-    place = jnp.stack([core, (chip * 2 + core) * pairs]).astype(jnp.int32)
-    query_grad, doc_grad = info_nce(place, mine, other, embedded)
+    query_grad, doc_grad = info_nce(mine, other, embedded)
     return (hidden_out, query_grad, doc_grad)
 
 

time: 133 us -> 126 us (0.947)
  blocking collectives: 59.1 us -> 82.1 us
  waiting for transfers between devices: 26.1 us -> 3.87 us
  Pallas kernels: 34.8 us -> 23.3 us
  local copies, waits for them, and re-layouts: 3.68 us -> 10.2 us
  other arithmetic: 1.4 us -> 0.01 us
    all_to_all x0 -> x1, blocking collectives: none -> 23.1 us  [body(): lax.all_to_all(results, 'expert', split_axis=0, concat_axis=0, tiled=True)]
    all_to_all x1 -> x0, waiting for transfers between devices: 22.8 us -> none  [body(): lax.all_to_all(results, 'expert', split_axis=0, concat_axis=0, tiled=True)]
    pallas_call x4, Pallas kernels: 34.8 us -> 23.3 us  [call(): pl.pallas_call(kernel, out_shape=outs, in_specs=[whole] * len(operands),...]
    unnamed x6 -> x18, local copies, waits for them, and re-layouts: 2.31 us -> 10.1 us
    all_to_all x1 -> x0, starting transfers between devices: 3.58 us -> none  [body(): lax.all_to_all(results, 'expert', split_axis=0, concat_axis=0, tiled=True)]
    ppermute x1, starting transfers between devices: 0.93 us -> 3.23 us  [body(): taken = lax.ppermute(given, 'dp', swap)]
  transfers between devices with their start and end apart: 3 -> 2, of which waited for: 3 -> 2; matrix products, arithmetic and copies ran while one was open for 0% -> 0% of each run, Pallas kernels for 0% -> 0%
where the time goes in v3:
time: 126 us
  blocking collectives  82.1 us (65%)
  Pallas kernels  23.3 us (18%)
  local copies, waits for them, and re-layouts  10.2 us (8%)
  starting transfers between devices  5.73 us (5%)
  waiting for transfers between devices  3.87 us (3%)
    all_to_all x1, blocking collectives, body(): lax.all_to_all(outgoing, 'expert', split_axis=0, concat_axis=0, tiled=True)  29.9 us
    all_to_all x1, blocking collectives, body(): lax.all_to_all(copies, ('dp', 'expert'), split_axis=0, concat_axis=0, til...  29.1 us
    pallas_call x4, Pallas kernels, call(): pl.pallas_call(kernel, out_shape=outs, in_specs=[whole] * len(operands),...  23.3 us
    all_to_all x1, blocking collectives, body(): lax.all_to_all(results, 'expert', split_axis=0, concat_axis=0, tiled=True)  23.1 us
    unnamed x18, local copies, waits for them, and re-layouts  10.1 us
    ppermute x1, starting transfers between devices, body(): taken = lax.ppermute(given, 'dp', swap)  3.23 us
    ppermute x1, waiting for transfers between devices, body(): other = lax.ppermute(mine, 'dp', swap)  3.04 us
  transfers between devices with their start and end apart: 2, of which 2 were waited for; matrix products, arithmetic and copies ran while one was open for 0% of the time, Pallas kernels for 0%

profile of v3, /device:TPU:1, one launch (start us, length us, event | category | flops | bytes accessed | tf_op | source)
XLA Modules:
  0.0 125.9 jit_solution(3544148845171554329)
XLA Ops:
  0.6 0.0 copy-start.3
  0.6 1.0 copy-done.3
  1.6 0.0 copy-start.5
  1.6 0.7 copy-done.5
  2.3 0.0 copy-start.6
  2.3 0.7 copy-done.6
  3.0 0.0 copy-start.7
  3.0 0.7 copy-done.7
  3.7 1.0 shard_map.103
  4.7 29.9 %all_to_all.15 = bf16[8,128,768]{2,1,0:T(8,128)(2,1)S(1)} all-to-all(bf16[8,128,768]{2,1,0:T(8,128)(2,1)S(1)} %bitcast.18), channel_id=1, replica_groups=mesh['dp'=16,'expert'=8] {'expert'}, dimensions={0} | all-to-all | bytes 3145728 | tf_op jit(solution)/shard_map/all_to_all | solution.py:212
  34.6 0.0 copy-start
  34.6 2.3 %copy-done = bf16[1,768,3072]{2,1,0:T(8,128)(2,1)S(1)} copy-done((bf16[1,768,3072]{2,1,0:T(8,128)(2,1)S(1)}, bf16[1,768,3072]{2,1,0:T(8,128)(2,1)}, u32[]{:S(2)}) %copy-start) | copy-done | bytes 4718616
  37.0 0.0 copy-start.1
  37.0 2.3 %copy-done.1 = bf16[1,768,3072]{2,1,0:T(8,128)(2,1)S(1)} copy-done((bf16[1,768,3072]{2,1,0:T(8,128)(2,1)S(1)}, bf16[1,768,3072]{2,1,0:T(8,128)(2,1)}, u32[]{:S(2)}) %copy-start.1) | copy-done | bytes 4718616
  39.3 0.0 copy-start.2
  39.3 2.3 %copy-done.2 = bf16[1,3072,768]{2,1,0:T(8,128)(2,1)S(1)} copy-done((bf16[1,3072,768]{2,1,0:T(8,128)(2,1)S(1)}, bf16[1,3072,768]{2,1,0:T(8,128)(2,1)}, u32[]{:S(2)}) %copy-start.2) | copy-done | bytes 4718616
  41.6 16.0 %shard_map.104 = bf16[1024,768]{1,0:T(8,128)(2,1)S(1)} custom-call(bf16[1024,768]{1,0:T(8,128)(2,1)S(1)} %bitcast.13, bf16[768,3072]{1,0:T(8,128)(2,1)S(1)} %bitcast.15, bf16[768,3072]{1,0:T(8,128)(2,1)S(1)} %bitcast.16, bf16[3072,768]{1,0:T(8,128)(2,1)S(1)} %bitcast.17), custom_call_target="tpu_custom_call" | custom-call | tf_op jit(solution)/shard_map/pallas_call | solution.py:41
  57.7 0.0 copy-start.4
  57.7 0.0 copy-start.8
  57.7 23.1 %all_to_all.16 = bf16[8,128,768]{2,1,0:T(8,128)(2,1)S(1)} all-to-all(bf16[8,128,768]{2,1,0:T(8,128)(2,1)S(1)} %bitcast.14), channel_id=1, replica_groups=mesh['dp'=16,'expert'=8] {'expert'}, dimensions={0} | all-to-all | bytes 3145728 | tf_op jit(solution)/shard_map/all_to_all | solution.py:217
  80.8 0.0 copy-done.4
  80.8 0.0 copy-done.8
  80.8 2.4 %shard_map.105 = (bf16[256,768]{1,0:T(8,128)(2,1)}, f32[16,768]{1,0:T(8,128)S(1)}, bf16[8,768]{1,0:T(8,128)(2,1)S(1)}, bf16[8,768]{1,0:T(8,128)(2,1)S(1)}) custom-call(bf16[256,768]{1,0:T(8,128)(2,1)S(1)} %copy-done.4, f32[256,8]{1,0:T(8,128)S(1)} %get-tuple-element.12.slots_ref, f32[256,8]{1,0:T(8,128)S(1)} %get-tuple-element.13.weights_ref, ...), custom_call_target="tpu_custom_call" | custom-call | tf_op jit(solution)/shard_map/pallas_call | solution.py:41
  83.3 3.2 %collective-permute-start = (bf16[8,768]{1,0:T(8,128)(2,1)S(1)}, bf16[8,768]{1,0:T(8,128)(2,1)S(1)}, u32[]{:S(2)}, u32[]{:S(2)}) collective-permute-start(bf16[8,768]{1,0:T(8,128)(2,1)S(1)} %get-tuple-element.17), channel_id=1, source_target_pairs={{0,8},{8,0},{16,24},{24,16},{32,40},{40,32},{48,56},{56,48},{64,72... | collective-permute-start | bytes 36872 | tf_op jit(solution)/shard_map/ppermute | solution.py:228
  86.5 0.8 collective-permute-done
  87.3 0.1 broadcast_in_dim.2
  87.4 29.1 %all_to_all.17 = bf16[64,16,768]{2,1,0:T(8,128)(2,1)S(1)} all-to-all(bf16[64,16,768]{2,1,0:T(8,128)(2,1)S(1)} %broadcast_in_dim.2), channel_id=1, replica_groups={{0,1,2,3,4,5,6,7,16,17,18,19,20,21,22,23,32,33,34,35,36,37,38,39,48,49,..., dimensions={0} | all-to-all | bytes 3145728 | tf_op jit(solution)/shard_map/all_to_all | solution.py:233
  116.6 2.5 %collective-permute-start.1 = (bf16[1024,768]{1,0:T(8,128)(2,1)S(1)}, bf16[1024,768]{1,0:T(8,128)(2,1)S(1)}, u32[]{:S(2)}, u32[]{:S(2)}) collective-permute-start(bf16[1024,768]{1,0:T(8,128)(2,1)S(1)} %bitcast.10), channel_id=1, source_target_pairs={{0,8},{8,0},{16,24},{24,16},{32,40},{40,32},{48,56},{56,48},{64,72... | collective-permute-start | bytes 4718600 | tf_op jit(solution)/shard_map/ppermute | solution.py:236
  119.1 3.0 %collective-permute-done.1.other_ref = bf16[1024,768]{1,0:T(8,128)(2,1)S(1)} collective-permute-done((bf16[1024,768]{1,0:T(8,128)(2,1)S(1)}, bf16[1024,768]{1,0:T(8,128)(2,1)S(1)}, u32[]{:S(2)}, u32[]{:S(2)}) %collective-permute-start.1) | collective-permute-done | bytes 1572896 | tf_op jit(solution)/shard_map/ppermute | solution.py:236
  122.1 3.8 %shard_map.106 = (f32[8,768]{1,0:T(8,128)}, f32[8,768]{1,0:T(8,128)}) custom-call(bf16[1024,768]{1,0:T(8,128)(2,1)S(1)} %bitcast.11, bf16[1024,768]{1,0:T(8,128)(2,1)S(1)} %collective-permute-done.1.other_ref, f32[16,768]{1,0:T(8,128)S(1)} %get-tuple-element.18.embedded_ref), custom_call_target="tpu_custom_call" | custom-call | tf_op jit(solution)/shard_map/pallas_call | solution.py:41
  (2 shorter events, 0.0 us)
Async XLA Ops:
  0.6 1.0 copy-start.3
  1.6 0.7 copy-start.5
  2.3 0.7 copy-start.6
  3.0 0.7 copy-start.7
  34.6 2.3 %copy-start = (bf16[1,768,3072]{2,1,0:T(8,128)(2,1)S(1)}, bf16[1,768,3072]{2,1,0:T(8,128)(2,1)}, u32[]{:S(2)}) copy-start(bf16[1,768,3072]{2,1,0:T(8,128)(2,1)} %param.13) | copy-start | bytes 14155780
  37.0 2.3 %copy-start.1 = (bf16[1,768,3072]{2,1,0:T(8,128)(2,1)S(1)}, bf16[1,768,3072]{2,1,0:T(8,128)(2,1)}, u32[]{:S(2)}) copy-start(bf16[1,768,3072]{2,1,0:T(8,128)(2,1)} %param.14) | copy-start | bytes 14155780
  39.3 2.3 %copy-start.2 = (bf16[1,3072,768]{2,1,0:T(8,128)(2,1)S(1)}, bf16[1,3072,768]{2,1,0:T(8,128)(2,1)}, u32[]{:S(2)}) copy-start(bf16[1,3072,768]{2,1,0:T(8,128)(2,1)} %param.15) | copy-start | bytes 14155780
  57.7 23.1 %copy-start.4 = (bf16[256,768]{1,0:T(8,128)(2,1)S(1)}, bf16[256,768]{1,0:T(8,128)(2,1)}, u32[]{:S(2)}) copy-start(bf16[256,768]{1,0:T(8,128)(2,1)} %tokens_ref.3) | copy-start | bytes 1179652
  57.7 23.1 %copy-start.8 = (s32[1,16]{1,0:T(1,128)S(1)}, s32[1,16]{1,0:T(1,128)}, u32[]{:S(2)}) copy-start(s32[1,16]{1,0:T(1,128)} %lengths_ref.1) | copy-start | bytes 196
  83.3 4.1 %collective-permute-start = (bf16[8,768]{1,0:T(8,128)(2,1)S(1)}, bf16[8,768]{1,0:T(8,128)(2,1)S(1)}, u32[]{:S(2)}, u32[]{:S(2)}) collective-permute-start(bf16[8,768]{1,0:T(8,128)(2,1)S(1)} %get-tuple-element.17), channel_id=1, source_target_pairs={{0,8},{8,0},{16,24},{24,16},{32,40},{40,32},{48,56},{56,48},{64,72... | collective-permute-start | bytes 36872 | tf_op jit(solution)/shard_map/ppermute | solution.py:228
  116.6 5.5 %collective-permute-start.1 = (bf16[1024,768]{1,0:T(8,128)(2,1)S(1)}, bf16[1024,768]{1,0:T(8,128)(2,1)S(1)}, u32[]{:S(2)}, u32[]{:S(2)}) collective-permute-start(bf16[1024,768]{1,0:T(8,128)(2,1)S(1)} %bitcast.10), channel_id=1, source_target_pairs={{0,8},{8,0},{16,24},{24,16},{32,40},{40,32},{48,56},{56,48},{64,72... | collective-permute-start | bytes 4718600 | tf_op jit(solution)/shard_map/ppermute | solution.py:236

commit v4 on v3

--- a/solution.py
+++ b/solution.py
@@ -36,19 +36,37 @@
     return x[: x.shape[0] // 2] + x[x.shape[0] // 2 :]
 
 
-def call(kernel, outs, *operands, budget=16, **options):
+def call(kernel, outs, *operands, budget=16, outside=(), **options):
     whole = pl.BlockSpec(memory_space=pltpu.VMEM)
+    left = pl.BlockSpec(memory_space=pltpu.HBM)
+    operands = [
+        pltpu.with_memory_space_constraint(x, pltpu.HBM) if at in outside else x
+        for at, x in enumerate(operands)
+    ]
     return pl.pallas_call(
         kernel,
         out_shape=outs,
-        in_specs=[whole] * len(operands),
+        in_specs=[left if at in outside else whole for at in range(len(operands))],
         out_specs=jax.tree.map(lambda _: whole, outs),
         compiler_params=pltpu.CompilerParams(vmem_limit_bytes=budget * mebibyte),
         **options,
     )(*operands)
 
 
-def route_kernel(tokens_ref, routes_ref, gain_ref, router_ref, out_ref, slots_ref, weights_ref):
+def route_kernel(
+    tokens_hbm, routes_hbm, gain_hbm, router_hbm, out_ref, slots_ref, weights_ref,
+    tokens_ref, routes_ref, gain_ref, router_ref, sems,
+):
+    copies = [
+        pltpu.make_async_copy(tokens_hbm, tokens_ref, sems.at[0]),
+        pltpu.make_async_copy(gain_hbm, gain_ref, sems.at[1]),
+        pltpu.make_async_copy(routes_hbm, routes_ref, sems.at[2]),
+        pltpu.make_async_copy(router_hbm, router_ref, sems.at[3]),
+    ]
+    for copy in copies:
+        copy.start()
+    for copy in copies:
+        copy.wait()
     rows = tokens_ref.shape[0]
     experts = router_ref.shape[0]
     capacity = out_ref.shape[0] // experts
@@ -73,26 +91,65 @@
     weights_ref[...] = hits_down / (1.0 + jnp.exp(both - 2.0 * logits))
 
 
-def expert_kernel(x_ref, gate_ref, up_ref, down_ref, out_ref, hidden_ref, *, block):
+def expert_kernel(
+    x_ref, gate_hbm, up_hbm, down_hbm, out_ref, gate_ref, up_ref, down_ref, hidden_ref, sems, *, block, ahead
+):
+    steps = hidden_ref.shape[1] // block
+
+    def part(step):
+        return pl.ds(pl.multiple_of(step * block, block), block)
+
+    def fetches(step):
+        at = part(step)
+        return (
+            pltpu.make_async_copy(gate_hbm.at[:, at], gate_ref.at[:, at], sems.at[0, step]),
+            pltpu.make_async_copy(up_hbm.at[:, at], up_ref.at[:, at], sems.at[1, step]),
+        )
+
+    def down_fetch(step):
+        at = part(step)
+        return pltpu.make_async_copy(down_hbm.at[at, :], down_ref.at[at, :], sems.at[2, step])
+
+    for step in range(ahead):
+        for copy in fetches(step):
+            copy.start()
+
     def columns(step, carry):
-        part = pl.ds(pl.multiple_of(step * block, block), block)
+        @pl.when(step + ahead < steps)
+        def _():
+            for copy in fetches(step + ahead):
+                copy.start()
+
+        down_fetch(step).start()
+        for copy in fetches(step):
+            copy.wait()
+        at = part(step)
         x = x_ref[...]
-        gate_act = dot(x, gate_ref[:, part])
-        up_act = dot(x, up_ref[:, part])
-        hidden_ref[:, part] = (gate_act / (1.0 + jnp.exp(-gate_act)) * up_act).astype(bf16)
+        gate_act = dot(x, gate_ref[:, at])
+        up_act = dot(x, up_ref[:, at])
+        hidden_ref[:, at] = (gate_act / (1.0 + jnp.exp(-gate_act)) * up_act).astype(bf16)
         return carry
 
-    lax.fori_loop(0, hidden_ref.shape[1] // block, columns, 0)
+    lax.fori_loop(0, steps, columns, 0)
+    lax.fori_loop(0, steps, lambda step, carry: (down_fetch(step).wait(), carry)[1], 0)
     out_ref[...] = dot(hidden_ref[...], down_ref[...]).astype(bf16)
 
 
-def expert_rows(x, w_gate, w_up, w_down, block=512):
+def expert_rows(x, w_gate, w_up, w_down, block=512, ahead=1):
+    hidden = w_gate.shape[1]
     return call(
-        functools.partial(expert_kernel, block=block),
+        functools.partial(expert_kernel, block=block, ahead=ahead),
         jax.ShapeDtypeStruct(x.shape, bf16),
         x, w_gate, w_up, w_down,
-        budget=36,
-        scratch_shapes=[pltpu.VMEM((x.shape[0], w_gate.shape[1]), bf16)],
+        budget=44,
+        outside=(1, 2, 3),
+        scratch_shapes=[
+            pltpu.VMEM(w_gate.shape, bf16),
+            pltpu.VMEM(w_up.shape, bf16),
+            pltpu.VMEM(w_down.shape, bf16),
+            pltpu.VMEM((x.shape[0], hidden), bf16),
+            pltpu.SemaphoreType.DMA((3, hidden // block)),
+        ],
     )
 
 
@@ -173,6 +230,7 @@
 def route(tokens, routes, norm_gain, router_weight):
     rows, width = tokens.shape
     experts = router_weight.shape[1]
+    operands = (tokens, routes.T, norm_gain, router_weight.T)
     return call(
         route_kernel,
         [
@@ -180,7 +238,10 @@
             jax.ShapeDtypeStruct((rows, experts), f32),
             jax.ShapeDtypeStruct((rows, experts), f32),
         ],
-        tokens, routes.T, norm_gain, router_weight.T,
+        *operands,
+        outside=(0, 1, 2, 3),
+        scratch_shapes=[pltpu.VMEM(x.shape, x.dtype) for x in operands]
+        + [pltpu.SemaphoreType.DMA((len(operands),))],
     )
 
 

time: 126 us -> 119 us (0.944)
  local copies, waits for them, and re-layouts: 10.2 us -> 0.12 us
  Pallas kernels: 23.3 us -> 25.9 us
    unnamed x18 -> x4, local copies, waits for them, and re-layouts: 10.1 us -> 0.01 us
    pallas_call x4, Pallas kernels: 23.3 us -> 25.9 us  [call(): pl.pallas_call(kernel, out_shape=outs, in_specs=[left if at in outside el...]
where the time goes in v4:
time: 119 us; the launch traced here: 118 us
  blocking collectives  82.2 us (69%)
  Pallas kernels  25.9 us (22%)
  starting transfers between devices  5.72 us (5%)
  waiting for transfers between devices  3.87 us (3%)
    all_to_all x1, blocking collectives, body(): lax.all_to_all(outgoing, 'expert', split_axis=0, concat_axis=0, tiled=True)  29.9 us
    all_to_all x1, blocking collectives, body(): lax.all_to_all(copies, ('dp', 'expert'), split_axis=0, concat_axis=0, til...  29.1 us
    pallas_call x4, Pallas kernels, call(): pl.pallas_call(kernel, out_shape=outs, in_specs=[left if at in outside el...  25.9 us
    all_to_all x1, blocking collectives, body(): lax.all_to_all(results, 'expert', split_axis=0, concat_axis=0, tiled=True)  23.1 us
    ppermute x1, starting transfers between devices, body(): taken = lax.ppermute(given, 'dp', swap)  3.22 us
    ppermute x1, waiting for transfers between devices, body(): other = lax.ppermute(mine, 'dp', swap)  3.04 us
    ppermute x1, starting transfers between devices, body(): other = lax.ppermute(mine, 'dp', swap)  2.5 us
  transfers between devices with their start and end apart: 2, of which 2 were waited for; matrix products, arithmetic and copies ran while one was open for 0% of the time, Pallas kernels for 0%

profile of v4, /device:TPU:1, one launch (start us, length us, event | category | flops | bytes accessed | tf_op | source)
XLA Modules:
  0.0 118.5 jit_solution(12729979705767686848)
XLA Ops:
  0.6 2.0 %shard_map.103 = (bf16[1024,768]{1,0:T(8,128)(2,1)S(1)}, f32[256,8]{1,0:T(8,128)S(1)}, f32[256,8]{1,0:T(8,128)S(1)}) custom-call(bf16[256,768]{1,0:T(8,128)(2,1)} %tokens_ref.1, s32[2,256]{1,0:T(2,128)} %bitcast.20, f32[768]{0:T(1024)} %gain_hbm.1, bf16[8,768]{1,0:T(8,128)(2,1)} %bitcast.19), custom_call_target="tpu_custom_call" | custom-call | tf_op jit(solution)/shard_map/pallas_call | solution.py:46
  2.7 29.9 %all_to_all.15 = bf16[8,128,768]{2,1,0:T(8,128)(2,1)S(1)} all-to-all(bf16[8,128,768]{2,1,0:T(8,128)(2,1)S(1)} %bitcast.15), channel_id=1, replica_groups=mesh['dp'=16,'expert'=8] {'expert'}, dimensions={0} | all-to-all | bytes 3145728 | tf_op jit(solution)/shard_map/all_to_all | solution.py:273
  32.6 17.6 %shard_map.104 = bf16[1024,768]{1,0:T(8,128)(2,1)S(1)} custom-call(bf16[1024,768]{1,0:T(8,128)(2,1)S(1)} %bitcast.13, bf16[768,3072]{1,0:T(8,128)(2,1)} %bitcast.16, bf16[768,3072]{1,0:T(8,128)(2,1)} %bitcast.17, bf16[3072,768]{1,0:T(8,128)(2,1)} %bitcast.18), custom_call_target="tpu_custom_call" | custom-call | tf_op jit(solution)/shard_map/pallas_call | solution.py:46
  50.2 0.0 copy-start
  50.2 0.0 copy-start.1
  50.2 23.1 %all_to_all.16 = bf16[8,128,768]{2,1,0:T(8,128)(2,1)S(1)} all-to-all(bf16[8,128,768]{2,1,0:T(8,128)(2,1)S(1)} %bitcast.14), channel_id=1, replica_groups=mesh['dp'=16,'expert'=8] {'expert'}, dimensions={0} | all-to-all | bytes 3145728 | tf_op jit(solution)/shard_map/all_to_all | solution.py:278
  73.4 0.0 copy-done
  73.4 0.0 copy-done.1
  73.4 2.4 %shard_map.105 = (bf16[256,768]{1,0:T(8,128)(2,1)}, f32[16,768]{1,0:T(8,128)S(1)}, bf16[8,768]{1,0:T(8,128)(2,1)S(1)}, bf16[8,768]{1,0:T(8,128)(2,1)S(1)}) custom-call(bf16[256,768]{1,0:T(8,128)(2,1)S(1)} %copy-done, f32[256,8]{1,0:T(8,128)S(1)} %get-tuple-element.12.slots_ref, f32[256,8]{1,0:T(8,128)S(1)} %get-tuple-element.13.weights_ref, ...), custom_call_target="tpu_custom_call" | custom-call | tf_op jit(solution)/shard_map/pallas_call | solution.py:46
  75.8 3.2 %collective-permute-start = (bf16[8,768]{1,0:T(8,128)(2,1)S(1)}, bf16[8,768]{1,0:T(8,128)(2,1)S(1)}, u32[]{:S(2)}, u32[]{:S(2)}) collective-permute-start(bf16[8,768]{1,0:T(8,128)(2,1)S(1)} %get-tuple-element.17), channel_id=1, source_target_pairs={{0,8},{8,0},{16,24},{24,16},{32,40},{40,32},{48,56},{56,48},{64,72... | collective-permute-start | bytes 36872 | tf_op jit(solution)/shard_map/ppermute | solution.py:289
  79.0 0.8 collective-permute-done
  79.9 0.1 broadcast_in_dim.2
  80.0 29.1 %all_to_all.17 = bf16[64,16,768]{2,1,0:T(8,128)(2,1)S(1)} all-to-all(bf16[64,16,768]{2,1,0:T(8,128)(2,1)S(1)} %broadcast_in_dim.2), channel_id=1, replica_groups={{0,1,2,3,4,5,6,7,16,17,18,19,20,21,22,23,32,33,34,35,36,37,38,39,48,49,..., dimensions={0} | all-to-all | bytes 3145728 | tf_op jit(solution)/shard_map/all_to_all | solution.py:294
  109.1 2.5 %collective-permute-start.1 = (bf16[1024,768]{1,0:T(8,128)(2,1)S(1)}, bf16[1024,768]{1,0:T(8,128)(2,1)S(1)}, u32[]{:S(2)}, u32[]{:S(2)}) collective-permute-start(bf16[1024,768]{1,0:T(8,128)(2,1)S(1)} %bitcast.10), channel_id=1, source_target_pairs={{0,8},{8,0},{16,24},{24,16},{32,40},{40,32},{48,56},{56,48},{64,72... | collective-permute-start | bytes 4718600 | tf_op jit(solution)/shard_map/ppermute | solution.py:297
  111.6 3.0 %collective-permute-done.1.other_ref = bf16[1024,768]{1,0:T(8,128)(2,1)S(1)} collective-permute-done((bf16[1024,768]{1,0:T(8,128)(2,1)S(1)}, bf16[1024,768]{1,0:T(8,128)(2,1)S(1)}, u32[]{:S(2)}, u32[]{:S(2)}) %collective-permute-start.1) | collective-permute-done | bytes 1572896 | tf_op jit(solution)/shard_map/ppermute | solution.py:297
  114.7 3.8 %shard_map.106 = (f32[8,768]{1,0:T(8,128)}, f32[8,768]{1,0:T(8,128)}) custom-call(bf16[1024,768]{1,0:T(8,128)(2,1)S(1)} %bitcast.11, bf16[1024,768]{1,0:T(8,128)(2,1)S(1)} %collective-permute-done.1.other_ref, f32[16,768]{1,0:T(8,128)S(1)} %get-tuple-element.18.embedded_ref), custom_call_target="tpu_custom_call" | custom-call | tf_op jit(solution)/shard_map/pallas_call | solution.py:46
  (2 shorter events, 0.0 us)
Async XLA Ops:
  50.2 23.2 %copy-start = (bf16[256,768]{1,0:T(8,128)(2,1)S(1)}, bf16[256,768]{1,0:T(8,128)(2,1)}, u32[]{:S(2)}) copy-start(bf16[256,768]{1,0:T(8,128)(2,1)} %tokens_ref.1) | copy-start | bytes 1179652
  50.2 23.1 %copy-start.1 = (s32[1,16]{1,0:T(1,128)S(1)}, s32[1,16]{1,0:T(1,128)}, u32[]{:S(2)}) copy-start(s32[1,16]{1,0:T(1,128)} %lengths_ref.1) | copy-start | bytes 196
  75.8 4.1 %collective-permute-start = (bf16[8,768]{1,0:T(8,128)(2,1)S(1)}, bf16[8,768]{1,0:T(8,128)(2,1)S(1)}, u32[]{:S(2)}, u32[]{:S(2)}) collective-permute-start(bf16[8,768]{1,0:T(8,128)(2,1)S(1)} %get-tuple-element.17), channel_id=1, source_target_pairs={{0,8},{8,0},{16,24},{24,16},{32,40},{40,32},{48,56},{56,48},{64,72... | collective-permute-start | bytes 36872 | tf_op jit(solution)/shard_map/ppermute | solution.py:289
  109.1 5.5 %collective-permute-start.1 = (bf16[1024,768]{1,0:T(8,128)(2,1)S(1)}, bf16[1024,768]{1,0:T(8,128)(2,1)S(1)}, u32[]{:S(2)}, u32[]{:S(2)}) collective-permute-start(bf16[1024,768]{1,0:T(8,128)(2,1)S(1)} %bitcast.10), channel_id=1, source_target_pairs={{0,8},{8,0},{16,24},{24,16},{32,40},{40,32},{48,56},{56,48},{64,72... | collective-permute-start | bytes 4718600 | tf_op jit(solution)/shard_map/ppermute | solution.py:297

commit v5 on v4

--- a/solution.py
+++ b/solution.py
@@ -13,6 +13,13 @@
 f32 = jnp.float32
 bf16 = jnp.bfloat16
 mebibyte = 1024 * 1024
+plane = 4
+move_groups = (
+    ((0, 0), (1, 0), (3, 0), (0, 1)),
+    ((2, 0), (1, 1)),
+    ((3, 1), (2, 1)),
+)
+moves = [move for group in move_groups for move in group]
 
 
 def dot(a, b):
@@ -21,6 +28,11 @@
 
 def dot_nt(a, b):
     return lax.dot_general(a, b, (((1,), (1,)), ((), ())), preferred_element_type=f32)
+
+
+def target(expert, move):
+    along, across = move
+    return (expert // plane + across) % 2 * plane + (expert % plane + along) % plane
 
 
 def iota(shape, axis):
@@ -36,11 +48,15 @@
     return x[: x.shape[0] // 2] + x[x.shape[0] // 2 :]
 
 
-def call(kernel, outs, *operands, budget=16, outside=(), **options):
+def call(kernel, outs, *operands, budget=16, outside=(), inside=(), **options):
     whole = pl.BlockSpec(memory_space=pltpu.VMEM)
     left = pl.BlockSpec(memory_space=pltpu.HBM)
     operands = [
-        pltpu.with_memory_space_constraint(x, pltpu.HBM) if at in outside else x
+        pltpu.with_memory_space_constraint(x, pltpu.HBM)
+        if at in outside
+        else pltpu.with_memory_space_constraint(x, pltpu.VMEM)
+        if at in inside
+        else x
         for at, x in enumerate(operands)
     ]
     return pl.pallas_call(
@@ -54,9 +70,9 @@
 
 
 def route_kernel(
-    tokens_hbm, routes_hbm, gain_hbm, router_hbm, out_ref, slots_ref, weights_ref,
-    tokens_ref, routes_ref, gain_ref, router_ref, sems,
+    tokens_hbm, routes_hbm, gain_hbm, router_hbm, *refs
 ):
+    *out_refs, slots_ref, weights_ref, tokens_ref, routes_ref, gain_ref, router_ref, sems = refs
     copies = [
         pltpu.make_async_copy(tokens_hbm, tokens_ref, sems.at[0]),
         pltpu.make_async_copy(gain_hbm, gain_ref, sems.at[1]),
@@ -69,11 +85,19 @@
         copy.wait()
     rows = tokens_ref.shape[0]
     experts = router_ref.shape[0]
-    capacity = out_ref.shape[0] // experts
+    capacity = out_refs[0].shape[0]
+    here = lax.axis_index("expert")
+
+    def ordered(shape):
+        place, labels = iota(shape, 0), jnp.zeros(shape, jnp.int32)
+        for at, move in enumerate(moves):
+            labels = jnp.where(place == at, target(here, move), labels)
+        return labels
+
     widened = tokens_ref[...].astype(f32)
     inverse = lax.rsqrt(jnp.mean(widened * widened, axis=-1, keepdims=True) + norm_eps)
     normed = (widened * inverse * gain_ref[...]).astype(bf16)
-    labels = iota((experts, rows), 0)
+    labels = ordered((experts, rows))
     hit = (routes_ref[0:1, :] == labels) | (routes_ref[1:2, :] == labels)
     hits = jnp.where(hit, 1.0, 0.0).astype(bf16)
     down, across = iota((rows, rows), 0), iota((rows, rows), 1)
@@ -82,18 +106,40 @@
     places = iota((capacity, rows), 0).astype(f32)
     for e in range(experts):
         chosen = jnp.where(places == ranks[e : e + 1, :], 1.0, 0.0).astype(bf16)
-        out_ref[e * capacity : (e + 1) * capacity, :] = dot(chosen, normed).astype(bf16)
+        out_refs[e][...] = dot(chosen, normed).astype(bf16)
     hits_down = dot_nt(jnp.where(down == across, 1.0, 0.0).astype(bf16), hits)
     ranks_down = dot_nt(jnp.where(across < down, 1.0, 0.0).astype(bf16), hits)
-    logits = dot_nt(normed, router_ref[...])
+    picks = ordered((experts, experts)) == iota((experts, experts), 1)
+    router = dot(jnp.where(picks, 1.0, 0.0).astype(bf16), router_ref[...]).astype(bf16)
+    logits = dot_nt(normed, router)
     both = jnp.sum(hits_down * logits, axis=-1, keepdims=True)
     slots_ref[...] = jnp.where(hits_down > 0.5, ranks_down, -1.0)
     weights_ref[...] = hits_down / (1.0 + jnp.exp(both - 2.0 * logits))
 
 
-def expert_kernel(
-    x_ref, gate_hbm, up_hbm, down_hbm, out_ref, gate_ref, up_ref, down_ref, hidden_ref, sems, *, block, ahead
-):
+def stack(x_refs, x_ref):
+    rows = x_refs[0].shape[0]
+    for at, ref in enumerate(x_refs):
+        x_ref[at * rows : (at + 1) * rows, :] = ref[...]
+
+
+def unstack(x, out_refs):
+    rows = out_refs[0].shape[0]
+    for at, ref in enumerate(out_refs):
+        ref[...] = x[at * rows : (at + 1) * rows, :]
+
+
+def hidden_block(x_ref, gate_ref, up_ref, hidden_ref, at):
+    x = x_ref[...]
+    gate_act = dot(x, gate_ref[:, at])
+    up_act = dot(x, up_ref[:, at])
+    hidden_ref[:, at] = (gate_act / (1.0 + jnp.exp(-gate_act)) * up_act).astype(bf16)
+
+
+def first_expert_kernel(*refs, blocks, block, ahead):
+    x_refs, out_refs = refs[:blocks], refs[blocks + 3 : 2 * blocks + 3]
+    gate_hbm, up_hbm, down_hbm = refs[blocks : blocks + 3]
+    gate_ref, up_ref, down_ref, x_ref, hidden_ref, sems = refs[2 * blocks + 3 :]
     steps = hidden_ref.shape[1] // block
 
     def part(step):
@@ -106,13 +152,11 @@
             pltpu.make_async_copy(up_hbm.at[:, at], up_ref.at[:, at], sems.at[1, step]),
         )
 
-    def down_fetch(step):
-        at = part(step)
-        return pltpu.make_async_copy(down_hbm.at[at, :], down_ref.at[at, :], sems.at[2, step])
-
+    down_fetch = pltpu.make_async_copy(down_hbm, down_ref, sems.at[2, 0])
     for step in range(ahead):
         for copy in fetches(step):
             copy.start()
+    stack(x_refs, x_ref)
 
     def columns(step, carry):
         @pl.when(step + ahead < steps)
@@ -120,53 +164,85 @@
             for copy in fetches(step + ahead):
                 copy.start()
 
-        down_fetch(step).start()
+        @pl.when(step + ahead == steps)
+        def _():
+            down_fetch.start()
+
         for copy in fetches(step):
             copy.wait()
-        at = part(step)
-        x = x_ref[...]
-        gate_act = dot(x, gate_ref[:, at])
-        up_act = dot(x, up_ref[:, at])
-        hidden_ref[:, at] = (gate_act / (1.0 + jnp.exp(-gate_act)) * up_act).astype(bf16)
+        hidden_block(x_ref, gate_ref, up_ref, hidden_ref, part(step))
         return carry
 
     lax.fori_loop(0, steps, columns, 0)
-    lax.fori_loop(0, steps, lambda step, carry: (down_fetch(step).wait(), carry)[1], 0)
-    out_ref[...] = dot(hidden_ref[...], down_ref[...]).astype(bf16)
-
-
-def expert_rows(x, w_gate, w_up, w_down, block=512, ahead=1):
-    hidden = w_gate.shape[1]
-    return call(
-        functools.partial(expert_kernel, block=block, ahead=ahead),
-        jax.ShapeDtypeStruct(x.shape, bf16),
-        x, w_gate, w_up, w_down,
-        budget=44,
-        outside=(1, 2, 3),
-        scratch_shapes=[
-            pltpu.VMEM(w_gate.shape, bf16),
-            pltpu.VMEM(w_up.shape, bf16),
-            pltpu.VMEM(w_down.shape, bf16),
-            pltpu.VMEM((x.shape[0], hidden), bf16),
-            pltpu.SemaphoreType.DMA((3, hidden // block)),
-        ],
-    )
-
-
-def combine_kernel(
-    tokens_ref, slots_ref, weights_ref, back_ref, lengths_ref, hidden_ref, embedded_ref, kept_ref, given_ref
-):
-    rows = tokens_ref.shape[0]
-    experts = slots_ref.shape[1]
-    capacity = back_ref.shape[0] // experts
-    lanes = iota((rows, capacity), 1).astype(f32)
+    down_fetch.wait()
+    unstack(dot(hidden_ref[...], down_ref[...]).astype(bf16), out_refs)
+
+
+def later_expert_kernel(*refs, blocks, block):
+    x_refs, out_refs = refs[:blocks], refs[blocks + 3 : 2 * blocks + 3]
+    gate_ref, up_ref, down_ref = refs[blocks : blocks + 3]
+    x_ref, hidden_ref = refs[2 * blocks + 3 :]
+    stack(x_refs, x_ref)
+
+    def columns(step, carry):
+        at = pl.ds(pl.multiple_of(step * block, block), block)
+        hidden_block(x_ref, gate_ref, up_ref, hidden_ref, at)
+        return carry
+
+    lax.fori_loop(0, hidden_ref.shape[1] // block, columns, 0)
+    unstack(dot(hidden_ref[...], down_ref[...]).astype(bf16), out_refs)
+
+
+def expert_rows(xs, weights, first, block=512, ahead=2):
+    rows, width = xs[0].shape
+    hidden = weights[0].shape[1]
+    blocks = len(xs)
+    places = range(blocks, blocks + 3)
+    results = [jax.ShapeDtypeStruct(x.shape, bf16) for x in xs]
+    scratch = [pltpu.VMEM((blocks * rows, width), bf16), pltpu.VMEM((blocks * rows, hidden), bf16)]
+    if first:
+        out = call(
+            functools.partial(first_expert_kernel, blocks=blocks, block=block, ahead=ahead),
+            results + [jax.ShapeDtypeStruct(w.shape, bf16) for w in weights],
+            *xs, *weights,
+            budget=20,
+            outside=places,
+            scratch_shapes=scratch + [pltpu.SemaphoreType.DMA((3, hidden // block))],
+        )
+        return out[:blocks], out[blocks:]
+    out = call(
+        functools.partial(later_expert_kernel, blocks=blocks, block=block),
+        results,
+        *xs, *weights,
+        budget=16,
+        inside=places,
+        scratch_shapes=scratch,
+    )
+    return out, weights
+
+
+def weighted_rows(slots_ref, weights_ref, back_refs, start):
+    shape = slots_ref.shape[0], back_refs[0].shape[0]
+    lanes = iota(shape, 1).astype(f32)
     terms = [
         jnp.where(lanes == slots_ref[:, e : e + 1], weights_ref[:, e : e + 1], 0.0)
-        for e in range(experts)
+        for e in range(start, start + len(back_refs))
     ]
     high, low = split(jnp.concatenate(terms, axis=1))
-    back = back_ref[...]
-    mixed = tokens_ref[...].astype(f32) + (dot(high, back) + dot(low, back))
+    back = jnp.concatenate([ref[...] for ref in back_refs], axis=0)
+    return dot(high, back) + dot(low, back)
+
+
+def early_combine_kernel(tokens_ref, slots_ref, weights_ref, *refs):
+    *back_refs, mixed_ref = refs
+    mixed_ref[...] = tokens_ref[...].astype(f32) + weighted_rows(slots_ref, weights_ref, back_refs, 0)
+
+
+def combine_kernel(early_ref, slots_ref, weights_ref, lengths_ref, *refs):
+    *back_refs, hidden_ref, embedded_ref, kept_ref, given_ref = refs
+    rows = early_ref.shape[0]
+    start = slots_ref.shape[1] - len(back_refs)
+    mixed = early_ref[...] + weighted_rows(slots_ref, weights_ref, back_refs, start)
     hidden_ref[...] = mixed.astype(bf16)
     count = lengths_ref.shape[1]
     spans = jnp.broadcast_to(lengths_ref[...], (count, count)).astype(f32)
@@ -234,7 +310,7 @@
     return call(
         route_kernel,
         [
-            jax.ShapeDtypeStruct((rows // 2 * experts, width), bf16),
+            *[jax.ShapeDtypeStruct((rows // 2, width), bf16) for _ in range(experts)],
             jax.ShapeDtypeStruct((rows, experts), f32),
             jax.ShapeDtypeStruct((rows, experts), f32),
         ],
@@ -245,9 +321,15 @@
     )
 
 
-def combine(tokens, slots, weights, back, lengths):
+def combine(tokens, slots, weights, backs, lengths):
     count, width = lengths.shape[1], tokens.shape[1]
     half = jax.ShapeDtypeStruct((count // 2, width), bf16)
+    early = len(backs) - len(move_groups[-1])
+    mixed = call(
+        early_combine_kernel,
+        jax.ShapeDtypeStruct(tokens.shape, f32),
+        tokens, slots, weights, *backs[:early],
+    )
     return call(
         combine_kernel,
         [
@@ -256,7 +338,7 @@
             half,
             half,
         ],
-        tokens, slots, weights, back, lengths,
+        mixed, slots, weights, lengths, *backs[early:],
     )
 
 
@@ -268,17 +350,22 @@
 def body(tokens, routes, lengths, norm_gain, router_weight, gate_weight, up_weight, down_weight):
     width = tokens.shape[1]
     experts = router_weight.shape[1]
-    outgoing, slots, weights = route(tokens, routes, norm_gain, router_weight)
-    outgoing = outgoing.reshape(experts, -1, width)
-    incoming = lax.all_to_all(outgoing, "expert", split_axis=0, concat_axis=0, tiled=True)
-    results = expert_rows(
-        incoming.reshape(-1, width), gate_weight[0], up_weight[0], down_weight[0]
-    )
-    results = results.reshape(experts, -1, width)
-    returned = lax.all_to_all(results, "expert", split_axis=0, concat_axis=0, tiled=True)
-    hidden_out, embedded, kept, given = combine(
-        tokens, slots, weights, returned.reshape(-1, width), lengths
-    )
+    *outgoing, slots, weights = route(tokens, routes, norm_gain, router_weight)
+
+    def pairs(move, back):
+        places = [(e, target(e, move)) for e in range(experts)]
+        return [(to, start) for start, to in places] if back else places
+
+    def send(x, move, back=False):
+        return x if move == (0, 0) else lax.ppermute(x, "expert", pairs(move, back))
+
+    incoming = {move: send(x, move) for move, x in zip(moves, outgoing)}
+    matrices = [gate_weight[0], up_weight[0], down_weight[0]]
+    backs = []
+    for at, group in enumerate(move_groups):
+        results, matrices = expert_rows([incoming[move] for move in group], matrices, at == 0)
+        backs += [send(x, move, back=True) for move, x in zip(group, results)]
+    hidden_out, embedded, kept, given = combine(tokens, slots, weights, backs, lengths)
 
     groups = lax.axis_size("dp")
     devices = groups * experts

time: 119 us -> 106 us (0.89)
  blocking collectives: 82.2 us -> 30.7 us
  starting transfers between devices: 5.72 us -> 35.9 us
  waiting for transfers between devices: 3.87 us -> 8.69 us
  Pallas kernels: 25.9 us -> 29.3 us
    all_to_all x2 -> x0, blocking collectives: 53 us -> none  [the longest x1 29.9 us: body(): lax.all_to_all(outgoing, 'expert', split_axis=0, concat_axis=0, tiled=True)]
    ppermute x0 -> x14, starting transfers between devices: none -> 27.3 us  [send(): return x if move == (0, 0) else lax.ppermute(x, 'expert', pairs(move, back))]
    ppermute x0 -> x14, waiting for transfers between devices: none -> 4.82 us  [send(): return x if move == (0, 0) else lax.ppermute(x, 'expert', pairs(move, back))]
    pallas_call x4 -> x7, Pallas kernels: 25.9 us -> 29.3 us  [call(): pl.pallas_call(kernel, out_shape=outs, in_specs=[left if at in outside el...]
    ppermute x1, starting transfers between devices: 3.22 us -> 6.13 us  [body(): taken = lax.ppermute(given, 'dp', swap)]
    all_to_all x1, blocking collectives: 29.1 us -> 30.7 us  [body(): lax.all_to_all(copies, ('dp', 'expert'), split_axis=0, concat_axis=0, til...]
  transfers between devices with their start and end apart: 2 -> 16, of which waited for: 2 -> 4; matrix products, arithmetic and copies ran while one was open for 0% -> 0% of each run, Pallas kernels for 0% -> 21%
where the time goes in v5:
time: 106 us
  starting transfers between devices  35.9 us (34%)
  blocking collectives  30.7 us (29%)
  Pallas kernels  29.3 us (28%)
  waiting for transfers between devices  8.69 us (8%)
    all_to_all x1, blocking collectives, body(): lax.all_to_all(copies, ('dp', 'expert'), split_axis=0, concat_axis=0, til...  30.7 us
    pallas_call x7, Pallas kernels, call(): pl.pallas_call(kernel, out_shape=outs, in_specs=[left if at in outside el...  29.3 us
    ppermute x14, starting transfers between devices, send(): return x if move == (0, 0) else lax.ppermute(x, 'expert', pairs(move, back))  27.3 us
    ppermute x1, starting transfers between devices, body(): taken = lax.ppermute(given, 'dp', swap)  6.13 us
    ppermute x14, waiting for transfers between devices, send(): return x if move == (0, 0) else lax.ppermute(x, 'expert', pairs(move, back))  4.82 us
    ppermute x1, waiting for transfers between devices, body(): other = lax.ppermute(mine, 'dp', swap)  3.04 us
    ppermute x1, starting transfers between devices, body(): other = lax.ppermute(mine, 'dp', swap)  2.5 us
  transfers between devices with their start and end apart: 16, of which 4 were waited for; matrix products, arithmetic and copies ran while one was open for 0% of the time, Pallas kernels for 21%

profile of v5, /device:TPU:1, one launch (start us, length us, event | category | flops | bytes accessed | tf_op | source)
XLA Modules:
  0.0 105.5 jit_solution(7495033306326769521)
XLA Ops:
  0.6 2.2 %shard_map.103 = (bf16[128,768]{1,0:T(8,128)(2,1)S(1)}, bf16[128,768]{1,0:T(8,128)(2,1)S(1)}, bf16[128,768]{1,0:T(8,128)(2,1)S(1)}, bf16[128,768]{1,0:T(8,128)(2...) custom-call(bf16[256,768]{1,0:T(8,128)(2,1)} %tokens_ref.1, ...), custom_call_target="tpu_custom_call" | custom-call | tf_op jit(solution)/shard_map/pallas_call | solution.py:62
  2.8 2.1 %collective-permute-start = (bf16[128,768]{1,0:T(8,128)(2,1)S(1)}, bf16[128,768]{1,0:T(8,128)(2,1)S(1)}, u32[]{:S(2)}, u32[]{:S(2)}) collective-permute-start(bf16[128,768]{1,0:T(8,128)(2,1)S(1)} %get-tuple-element.33), channel_id=1, source_target_pairs={{0,1},{1,2},{2,3},{3,0},{4,5},{5,6},{6,7},{7,4},{8,9},{9,10},{10,1... | collective-permute-start | bytes 589832 | tf_op jit(solution)/shard_map/ppermute | solution.py:360
  4.9 1.4 %collective-permute-start.1 = (bf16[128,768]{1,0:T(8,128)(2,1)S(1)}, bf16[128,768]{1,0:T(8,128)(2,1)S(1)}, u32[]{:S(2)}, u32[]{:S(2)}) collective-permute-start(bf16[128,768]{1,0:T(8,128)(2,1)S(1)} %get-tuple-element.34), channel_id=1, source_target_pairs={{0,3},{1,0},{2,1},{3,2},{4,7},{5,4},{6,5},{7,6},{8,11},{9,8},{10,9... | collective-permute-start | bytes 589832 | tf_op jit(solution)/shard_map/ppermute | solution.py:360
  6.3 3.7 %collective-permute-start.2 = (bf16[128,768]{1,0:T(8,128)(2,1)S(1)}, bf16[128,768]{1,0:T(8,128)(2,1)S(1)}, u32[]{:S(2)}, u32[]{:S(2)}) collective-permute-start(bf16[128,768]{1,0:T(8,128)(2,1)S(1)} %get-tuple-element.35), channel_id=1, source_target_pairs={{0,4},{1,5},{2,6},{3,7},{4,0},{5,1},{6,2},{7,3},{8,12},{9,13},{10,... | collective-permute-start | bytes 589832 | tf_op jit(solution)/shard_map/ppermute | solution.py:360
  10.0 1.5 %collective-permute-start.6 = (bf16[128,768]{1,0:T(8,128)(2,1)S(1)}, bf16[128,768]{1,0:T(8,128)(2,1)S(1)}, u32[]{:S(2)}, u32[]{:S(2)}) collective-permute-start(bf16[128,768]{1,0:T(8,128)(2,1)S(1)} %get-tuple-element.40), channel_id=1, source_target_pairs={{0,2},{1,3},{2,0},{3,1},{4,6},{5,7},{6,4},{7,5},{8,10},{9,11},{10,... | collective-permute-start | bytes 589832 | tf_op jit(solution)/shard_map/ppermute | solution.py:360
  11.5 0.0 collective-permute-start.7
  11.6 0.0 collective-permute-done.refs_1_
  11.6 5.0 %collective-permute-start.10 = (bf16[128,768]{1,0:T(8,128)(2,1)S(1)}, bf16[128,768]{1,0:T(8,128)(2,1)S(1)}, u32[]{:S(2)}, u32[]{:S(2)}) collective-permute-start(bf16[128,768]{1,0:T(8,128)(2,1)S(1)} %get-tuple-element.47), channel_id=1, source_target_pairs={{0,7},{1,4},{2,5},{3,6},{4,3},{5,0},{6,1},{7,2},{8,15},{9,12},{10,... | collective-permute-start | bytes 589832 | tf_op jit(solution)/shard_map/ppermute | solution.py:360
  16.6 10.7 %shard_map.104 = (bf16[128,768]{1,0:T(8,128)(2,1)S(1)}, bf16[128,768]{1,0:T(8,128)(2,1)S(1)}, bf16[128,768]{1,0:T(8,128)(2,1)S(1)}, bf16[128,768]{1,0:T(8,128)(2...) custom-call(bf16[128,768]{1,0:T(8,128)(2,1)S(1)} %get-tuple-element.32.refs_0_,, ...), custom_call_target="tpu_custom_call" | custom-call | tf_op jit(solution)/shard_map/pallas_call | solution.py:62
  27.4 5.0 %shard_map.105 = (bf16[128,768]{1,0:T(8,128)(2,1)S(1)}, bf16[128,768]{1,0:T(8,128)(2,1)S(1)}) custom-call(bf16[128,768]{1,0:T(8,128)(2,1)S(1)} %collective-permute-done.6.refs_0_, bf16[128,768]{1,0:T(8,128)(2,1)S(1)} %collective-permute-done.7.refs_1_, bf16[768,3072]{1,0:T(8,128)(2,1)S(1)} %get-tuple-element.42.refs_2_, ...), custom_call_target="tpu_custom_call" | custom-call | tf_op jit(solution)/shard_map/pallas_call | solution.py:62
  32.3 2.8 %collective-permute-start.8 = (bf16[128,768]{1,0:T(8,128)(2,1)S(1)}, bf16[128,768]{1,0:T(8,128)(2,1)S(1)}, u32[]{:S(2)}, u32[]{:S(2)}) collective-permute-start(bf16[128,768]{1,0:T(8,128)(2,1)S(1)} %get-tuple-element.45), channel_id=1, source_target_pairs={{2,0},{3,1},{0,2},{1,3},{6,4},{7,5},{4,6},{5,7},{10,8},{11,9},{8,1... | collective-permute-start | bytes 589832 | tf_op jit(solution)/shard_map/ppermute | solution.py:360
  35.1 2.3 %collective-permute-start.9 = (bf16[128,768]{1,0:T(8,128)(2,1)S(1)}, bf16[128,768]{1,0:T(8,128)(2,1)S(1)}, u32[]{:S(2)}, u32[]{:S(2)}) collective-permute-start(bf16[128,768]{1,0:T(8,128)(2,1)S(1)} %get-tuple-element.46), channel_id=1, source_target_pairs={{5,0},{6,1},{7,2},{4,3},{1,4},{2,5},{3,6},{0,7},{13,8},{14,9},{15,... | collective-permute-start | bytes 589832 | tf_op jit(solution)/shard_map/ppermute | solution.py:360
  37.4 2.1 %collective-permute-start.3 = (bf16[128,768]{1,0:T(8,128)(2,1)S(1)}, bf16[128,768]{1,0:T(8,128)(2,1)S(1)}, u32[]{:S(2)}, u32[]{:S(2)}) collective-permute-start(bf16[128,768]{1,0:T(8,128)(2,1)S(1)} %get-tuple-element.37), channel_id=1, source_target_pairs={{1,0},{2,1},{3,2},{0,3},{5,4},{6,5},{7,6},{4,7},{9,8},{10,9},{11,1... | collective-permute-start | bytes 589832 | tf_op jit(solution)/shard_map/ppermute | solution.py:360
  39.5 0.0 collective-permute-done.10.refs_0_
  39.5 0.0 copy-start
  39.5 0.0 copy-start.1
  39.5 0.1 collective-permute-start.5
  39.6 5.0 %shard_map.107 = (bf16[128,768]{1,0:T(8,128)(2,1)S(1)}, bf16[128,768]{1,0:T(8,128)(2,1)S(1)}) custom-call(bf16[128,768]{1,0:T(8,128)(2,1)S(1)} %collective-permute-done.10.refs_0_, bf16[128,768]{1,0:T(8,128)(2,1)S(1)} %collective-permute-done.11.refs_1_, bf16[768,3072]{1,0:T(8,128)(2,1)S(1)} %get-tuple-element.42.refs_2_, ...), custom_call_target="tpu_custom_call" | custom-call | tf_op jit(solution)/shard_map/pallas_call | solution.py:62
  44.6 3.8 %collective-permute-start.12 = (bf16[128,768]{1,0:T(8,128)(2,1)S(1)}, bf16[128,768]{1,0:T(8,128)(2,1)S(1)}, u32[]{:S(2)}, u32[]{:S(2)}) collective-permute-start(bf16[128,768]{1,0:T(8,128)(2,1)S(1)} %get-tuple-element.49), channel_id=1, source_target_pairs={{7,0},{4,1},{5,2},{6,3},{3,4},{0,5},{1,6},{2,7},{15,8},{12,9},{13,... | collective-permute-start | bytes 589832 | tf_op jit(solution)/shard_map/ppermute | solution.py:360
  48.5 2.4 %collective-permute-start.13 = (bf16[128,768]{1,0:T(8,128)(2,1)S(1)}, bf16[128,768]{1,0:T(8,128)(2,1)S(1)}, u32[]{:S(2)}, u32[]{:S(2)}) collective-permute-start(bf16[128,768]{1,0:T(8,128)(2,1)S(1)} %get-tuple-element.50), channel_id=1, source_target_pairs={{6,0},{7,1},{4,2},{5,3},{2,4},{3,5},{0,6},{1,7},{14,8},{15,9},{12,... | collective-permute-start | bytes 589832 | tf_op jit(solution)/shard_map/ppermute | solution.py:360
  50.8 0.0 collective-permute-done.3.refs_1_
  50.9 1.2 %shard_map.106.early_ref = f32[256,768]{1,0:T(8,128)S(1)} custom-call(bf16[256,768]{1,0:T(8,128)(2,1)S(1)} %copy-done, f32[256,8]{1,0:T(8,128)S(1)} %get-tuple-element.30.slots_ref, f32[256,8]{1,0:T(8,128)S(1)} %get-tuple-element.31.weights_ref, bf16[128,768]{1,0:T(8,128)(2,1)S(1)} %get-tuple-element.36.refs_0_, ...), custom_call_target="tpu_custom_call" | custom-call | tf_op jit(solution)/shard_map/pallas_call | solution.py:62
  52.1 0.9 collective-permute-done.12.refs_0_
  53.0 3.9 %collective-permute-done.13.refs_1_ = bf16[128,768]{1,0:T(8,128)(2,1)S(1)} collective-permute-done((bf16[128,768]{1,0:T(8,128)(2,1)S(1)}, bf16[128,768]{1,0:T(8,128)(2,1)S(1)}, u32[]{:S(2)}, u32[]{:S(2)}) %collective-permute-start.13) | collective-permute-done | bytes 196640 | tf_op jit(solution)/shard_map/ppermute | solution.py:360
  56.9 1.4 %shard_map.108 = (bf16[256,768]{1,0:T(8,128)(2,1)}, f32[16,768]{1,0:T(8,128)S(1)}, bf16[8,768]{1,0:T(8,128)(2,1)S(1)}, bf16[8,768]{1,0:T(8,128)(2,1)S(1)}) custom-call(f32[256,768]{1,0:T(8,128)S(1)} %shard_map.106.early_ref, f32[256,8]{1,0:T(8,128)S(1)} %get-tuple-element.30.slots_ref, f32[256,8]{1,0:T(8,128)S(1)} %get-tuple-element.31.weights_ref, ...), custom_call_target="tpu_custom_call" | custom-call | tf_op jit(solution)/shard_map/pallas_call | solution.py:62
  58.3 6.1 %collective-permute-start.14 = (bf16[8,768]{1,0:T(8,128)(2,1)S(1)}, bf16[8,768]{1,0:T(8,128)(2,1)S(1)}, u32[]{:S(2)}, u32[]{:S(2)}) collective-permute-start(bf16[8,768]{1,0:T(8,128)(2,1)S(1)} %get-tuple-element.53), channel_id=1, source_target_pairs={{0,8},{8,0},{16,24},{24,16},{32,40},{40,32},{48,56},{56,48},{64,72... | collective-permute-start | bytes 36872 | tf_op jit(solution)/shard_map/ppermute | solution.py:376
  64.4 0.8 collective-permute-done.14
  65.3 0.1 broadcast_in_dim.2
  65.4 30.7 %all_to_all.5 = bf16[64,16,768]{2,1,0:T(8,128)(2,1)S(1)} all-to-all(bf16[64,16,768]{2,1,0:T(8,128)(2,1)S(1)} %broadcast_in_dim.2), channel_id=1, replica_groups={{0,1,2,3,4,5,6,7,16,17,18,19,20,21,22,23,32,33,34,35,36,37,38,39,48,49,..., dimensions={0} | all-to-all | bytes 3145728 | tf_op jit(solution)/shard_map/all_to_all | solution.py:381
  96.1 2.5 %collective-permute-start.15 = (bf16[1024,768]{1,0:T(8,128)(2,1)S(1)}, bf16[1024,768]{1,0:T(8,128)(2,1)S(1)}, u32[]{:S(2)}, u32[]{:S(2)}) collective-permute-start(bf16[1024,768]{1,0:T(8,128)(2,1)S(1)} %bitcast.6), channel_id=1, source_target_pairs={{0,8},{8,0},{16,24},{24,16},{32,40},{40,32},{48,56},{56,48},{64,72... | collective-permute-start | bytes 4718600 | tf_op jit(solution)/shard_map/ppermute | solution.py:384
  98.6 3.0 %collective-permute-done.15.other_ref = bf16[1024,768]{1,0:T(8,128)(2,1)S(1)} collective-permute-done((bf16[1024,768]{1,0:T(8,128)(2,1)S(1)}, bf16[1024,768]{1,0:T(8,128)(2,1)S(1)}, u32[]{:S(2)}, u32[]{:S(2)}) %collective-permute-start.15) | collective-permute-done | bytes 1572896 | tf_op jit(solution)/shard_map/ppermute | solution.py:384
  101.7 3.8 %shard_map.109 = (f32[8,768]{1,0:T(8,128)}, f32[8,768]{1,0:T(8,128)}) custom-call(bf16[1024,768]{1,0:T(8,128)(2,1)S(1)} %bitcast.7, bf16[1024,768]{1,0:T(8,128)(2,1)S(1)} %collective-permute-done.15.other_ref, f32[16,768]{1,0:T(8,128)S(1)} %get-tuple-element.54.embedded_ref), custom_call_target="tpu_custom_call" | custom-call | tf_op jit(solution)/shard_map/pallas_call | solution.py:62
  (15 shorter events, 0.0 us)
Async XLA Ops:
  2.8 8.8 %collective-permute-start = (bf16[128,768]{1,0:T(8,128)(2,1)S(1)}, bf16[128,768]{1,0:T(8,128)(2,1)S(1)}, u32[]{:S(2)}, u32[]{:S(2)}) collective-permute-start(bf16[128,768]{1,0:T(8,128)(2,1)S(1)} %get-tuple-element.33), channel_id=1, source_target_pairs={{0,1},{1,2},{2,3},{3,0},{4,5},{5,6},{6,7},{7,4},{8,9},{9,10},{10,1... | collective-permute-start | bytes 589832 | tf_op jit(solution)/shard_map/ppermute | solution.py:360
  4.9 11.7 %collective-permute-start.1 = (bf16[128,768]{1,0:T(8,128)(2,1)S(1)}, bf16[128,768]{1,0:T(8,128)(2,1)S(1)}, u32[]{:S(2)}, u32[]{:S(2)}) collective-permute-start(bf16[128,768]{1,0:T(8,128)(2,1)S(1)} %get-tuple-element.34), channel_id=1, source_target_pairs={{0,3},{1,0},{2,1},{3,2},{4,7},{5,4},{6,5},{7,6},{8,11},{9,8},{10,9... | collective-permute-start | bytes 589832 | tf_op jit(solution)/shard_map/ppermute | solution.py:360
  6.3 10.3 %collective-permute-start.2 = (bf16[128,768]{1,0:T(8,128)(2,1)S(1)}, bf16[128,768]{1,0:T(8,128)(2,1)S(1)}, u32[]{:S(2)}, u32[]{:S(2)}) collective-permute-start(bf16[128,768]{1,0:T(8,128)(2,1)S(1)} %get-tuple-element.35), channel_id=1, source_target_pairs={{0,4},{1,5},{2,6},{3,7},{4,0},{5,1},{6,2},{7,3},{8,12},{9,13},{10,... | collective-permute-start | bytes 589832 | tf_op jit(solution)/shard_map/ppermute | solution.py:360
  10.0 17.4 %collective-permute-start.6 = (bf16[128,768]{1,0:T(8,128)(2,1)S(1)}, bf16[128,768]{1,0:T(8,128)(2,1)S(1)}, u32[]{:S(2)}, u32[]{:S(2)}) collective-permute-start(bf16[128,768]{1,0:T(8,128)(2,1)S(1)} %get-tuple-element.40), channel_id=1, source_target_pairs={{0,2},{1,3},{2,0},{3,1},{4,6},{5,7},{6,4},{7,5},{8,10},{9,11},{10,... | collective-permute-start | bytes 589832 | tf_op jit(solution)/shard_map/ppermute | solution.py:360
  11.5 15.8 %collective-permute-start.7 = (bf16[128,768]{1,0:T(8,128)(2,1)S(1)}, bf16[128,768]{1,0:T(8,128)(2,1)S(1)}, u32[]{:S(2)}, u32[]{:S(2)}) collective-permute-start(bf16[128,768]{1,0:T(8,128)(2,1)S(1)} %get-tuple-element.41), channel_id=1, source_target_pairs={{0,5},{1,6},{2,7},{3,4},{4,1},{5,2},{6,3},{7,0},{8,13},{9,14},{10,... | collective-permute-start | bytes 589832 | tf_op jit(solution)/shard_map/ppermute | solution.py:360
  11.6 27.9 %collective-permute-start.10 = (bf16[128,768]{1,0:T(8,128)(2,1)S(1)}, bf16[128,768]{1,0:T(8,128)(2,1)S(1)}, u32[]{:S(2)}, u32[]{:S(2)}) collective-permute-start(bf16[128,768]{1,0:T(8,128)(2,1)S(1)} %get-tuple-element.47), channel_id=1, source_target_pairs={{0,7},{1,4},{2,5},{3,6},{4,3},{5,0},{6,1},{7,2},{8,15},{9,12},{10,... | collective-permute-start | bytes 589832 | tf_op jit(solution)/shard_map/ppermute | solution.py:360
  16.6 22.9 %collective-permute-start.11 = (bf16[128,768]{1,0:T(8,128)(2,1)S(1)}, bf16[128,768]{1,0:T(8,128)(2,1)S(1)}, u32[]{:S(2)}, u32[]{:S(2)}) collective-permute-start(bf16[128,768]{1,0:T(8,128)(2,1)S(1)} %get-tuple-element.48), channel_id=1, source_target_pairs={{0,6},{1,7},{2,4},{3,5},{4,2},{5,3},{6,0},{7,1},{8,14},{9,15},{10,... | collective-permute-start | bytes 589832 | tf_op jit(solution)/shard_map/ppermute | solution.py:360
  32.3 12.3 %collective-permute-start.8 = (bf16[128,768]{1,0:T(8,128)(2,1)S(1)}, bf16[128,768]{1,0:T(8,128)(2,1)S(1)}, u32[]{:S(2)}, u32[]{:S(2)}) collective-permute-start(bf16[128,768]{1,0:T(8,128)(2,1)S(1)} %get-tuple-element.45), channel_id=1, source_target_pairs={{2,0},{3,1},{0,2},{1,3},{6,4},{7,5},{4,6},{5,7},{10,8},{11,9},{8,1... | collective-permute-start | bytes 589832 | tf_op jit(solution)/shard_map/ppermute | solution.py:360
  35.1 13.4 %collective-permute-start.9 = (bf16[128,768]{1,0:T(8,128)(2,1)S(1)}, bf16[128,768]{1,0:T(8,128)(2,1)S(1)}, u32[]{:S(2)}, u32[]{:S(2)}) collective-permute-start(bf16[128,768]{1,0:T(8,128)(2,1)S(1)} %get-tuple-element.46), channel_id=1, source_target_pairs={{5,0},{6,1},{7,2},{4,3},{1,4},{2,5},{3,6},{0,7},{13,8},{14,9},{15,... | collective-permute-start | bytes 589832 | tf_op jit(solution)/shard_map/ppermute | solution.py:360
  37.4 13.4 %collective-permute-start.3 = (bf16[128,768]{1,0:T(8,128)(2,1)S(1)}, bf16[128,768]{1,0:T(8,128)(2,1)S(1)}, u32[]{:S(2)}, u32[]{:S(2)}) collective-permute-start(bf16[128,768]{1,0:T(8,128)(2,1)S(1)} %get-tuple-element.37), channel_id=1, source_target_pairs={{1,0},{2,1},{3,2},{0,3},{5,4},{6,5},{7,6},{4,7},{9,8},{10,9},{11,1... | collective-permute-start | bytes 589832 | tf_op jit(solution)/shard_map/ppermute | solution.py:360
  39.5 11.3 %collective-permute-start.4 = (bf16[128,768]{1,0:T(8,128)(2,1)S(1)}, bf16[128,768]{1,0:T(8,128)(2,1)S(1)}, u32[]{:S(2)}, u32[]{:S(2)}) collective-permute-start(bf16[128,768]{1,0:T(8,128)(2,1)S(1)} %get-tuple-element.38), channel_id=1, source_target_pairs={{3,0},{0,1},{1,2},{2,3},{7,4},{4,5},{5,6},{6,7},{11,8},{8,9},{9,10... | collective-permute-start | bytes 589832 | tf_op jit(solution)/shard_map/ppermute | solution.py:360
  39.5 11.3 %copy-start = (bf16[256,768]{1,0:T(8,128)(2,1)S(1)}, bf16[256,768]{1,0:T(8,128)(2,1)}, u32[]{:S(2)}) copy-start(bf16[256,768]{1,0:T(8,128)(2,1)} %tokens_ref.1) | copy-start | bytes 1179652
  39.5 17.4 %copy-start.1 = (s32[1,16]{1,0:T(1,128)S(1)}, s32[1,16]{1,0:T(1,128)}, u32[]{:S(2)}) copy-start(s32[1,16]{1,0:T(1,128)} %lengths_ref.1) | copy-start | bytes 196
  39.5 11.3 %collective-permute-start.5 = (bf16[128,768]{1,0:T(8,128)(2,1)S(1)}, bf16[128,768]{1,0:T(8,128)(2,1)S(1)}, u32[]{:S(2)}, u32[]{:S(2)}) collective-permute-start(bf16[128,768]{1,0:T(8,128)(2,1)S(1)} %get-tuple-element.39), channel_id=1, source_target_pairs={{4,0},{5,1},{6,2},{7,3},{0,4},{1,5},{2,6},{3,7},{12,8},{13,9},{14,... | collective-permute-start | bytes 589832 | tf_op jit(solution)/shard_map/ppermute | solution.py:360
  44.6 8.4 %collective-permute-start.12 = (bf16[128,768]{1,0:T(8,128)(2,1)S(1)}, bf16[128,768]{1,0:T(8,128)(2,1)S(1)}, u32[]{:S(2)}, u32[]{:S(2)}) collective-permute-start(bf16[128,768]{1,0:T(8,128)(2,1)S(1)} %get-tuple-element.49), channel_id=1, source_target_pairs={{7,0},{4,1},{5,2},{6,3},{3,4},{0,5},{1,6},{2,7},{15,8},{12,9},{13,... | collective-permute-start | bytes 589832 | tf_op jit(solution)/shard_map/ppermute | solution.py:360
  48.5 8.4 %collective-permute-start.13 = (bf16[128,768]{1,0:T(8,128)(2,1)S(1)}, bf16[128,768]{1,0:T(8,128)(2,1)S(1)}, u32[]{:S(2)}, u32[]{:S(2)}) collective-permute-start(bf16[128,768]{1,0:T(8,128)(2,1)S(1)} %get-tuple-element.50), channel_id=1, source_target_pairs={{6,0},{7,1},{4,2},{5,3},{2,4},{3,5},{0,6},{1,7},{14,8},{15,9},{12,... | collective-permute-start | bytes 589832 | tf_op jit(solution)/shard_map/ppermute | solution.py:360
  58.3 7.0 %collective-permute-start.14 = (bf16[8,768]{1,0:T(8,128)(2,1)S(1)}, bf16[8,768]{1,0:T(8,128)(2,1)S(1)}, u32[]{:S(2)}, u32[]{:S(2)}) collective-permute-start(bf16[8,768]{1,0:T(8,128)(2,1)S(1)} %get-tuple-element.53), channel_id=1, source_target_pairs={{0,8},{8,0},{16,24},{24,16},{32,40},{40,32},{48,56},{56,48},{64,72... | collective-permute-start | bytes 36872 | tf_op jit(solution)/shard_map/ppermute | solution.py:376
  96.1 5.5 %collective-permute-start.15 = (bf16[1024,768]{1,0:T(8,128)(2,1)S(1)}, bf16[1024,768]{1,0:T(8,128)(2,1)S(1)}, u32[]{:S(2)}, u32[]{:S(2)}) collective-permute-start(bf16[1024,768]{1,0:T(8,128)(2,1)S(1)} %bitcast.6), channel_id=1, source_target_pairs={{0,8},{8,0},{16,24},{24,16},{32,40},{40,32},{48,56},{56,48},{64,72... | collective-permute-start | bytes 4718600 | tf_op jit(solution)/shard_map/ppermute | solution.py:384

commit v6 on v5

--- a/solution.py
+++ b/solution.py
@@ -14,6 +14,8 @@
 bf16 = jnp.bfloat16
 mebibyte = 1024 * 1024
 plane = 4
+block = 512
+head = 1024
 move_groups = (
     ((0, 0), (1, 0), (3, 0), (0, 1)),
     ((2, 0), (1, 1)),
@@ -70,9 +72,9 @@
 
 
 def route_kernel(
-    tokens_hbm, routes_hbm, gain_hbm, router_hbm, *refs
+    tokens_hbm, routes_hbm, gain_hbm, router_hbm, gate_hbm, up_hbm, *refs, head
 ):
-    *out_refs, slots_ref, weights_ref, tokens_ref, routes_ref, gain_ref, router_ref, sems = refs
+    *out_refs, slots_ref, weights_ref, gate_ref, up_ref, tokens_ref, routes_ref, gain_ref, router_ref, sems = refs
     copies = [
         pltpu.make_async_copy(tokens_hbm, tokens_ref, sems.at[0]),
         pltpu.make_async_copy(gain_hbm, gain_ref, sems.at[1]),
@@ -81,8 +83,14 @@
     ]
     for copy in copies:
         copy.start()
+    heads = [
+        pltpu.make_async_copy(gate_hbm.at[:, :head], gate_ref.at[:, :head], sems.at[4]),
+        pltpu.make_async_copy(up_hbm.at[:, :head], up_ref.at[:, :head], sems.at[5]),
+    ]
     for copy in copies:
         copy.wait()
+    for copy in heads:
+        copy.start()
     rows = tokens_ref.shape[0]
     experts = router_ref.shape[0]
     capacity = out_refs[0].shape[0]
@@ -115,6 +123,8 @@
     both = jnp.sum(hits_down * logits, axis=-1, keepdims=True)
     slots_ref[...] = jnp.where(hits_down > 0.5, ranks_down, -1.0)
     weights_ref[...] = hits_down / (1.0 + jnp.exp(both - 2.0 * logits))
+    for copy in heads:
+        copy.wait()
 
 
 def stack(x_refs, x_ref):
@@ -136,10 +146,10 @@
     hidden_ref[:, at] = (gate_act / (1.0 + jnp.exp(-gate_act)) * up_act).astype(bf16)
 
 
-def first_expert_kernel(*refs, blocks, block, ahead):
-    x_refs, out_refs = refs[:blocks], refs[blocks + 3 : 2 * blocks + 3]
+def first_expert_kernel(*refs, blocks, block, present, ahead):
+    x_refs, out_refs = refs[:blocks], refs[blocks + 5 : 2 * blocks + 5]
     gate_hbm, up_hbm, down_hbm = refs[blocks : blocks + 3]
-    gate_ref, up_ref, down_ref, x_ref, hidden_ref, sems = refs[2 * blocks + 3 :]
+    gate_ref, up_ref, down_ref, x_ref, hidden_ref, sems = refs[2 * blocks + 5 :]
     steps = hidden_ref.shape[1] // block
 
     def part(step):
@@ -153,7 +163,7 @@
         )
 
     down_fetch = pltpu.make_async_copy(down_hbm, down_ref, sems.at[2, 0])
-    for step in range(ahead):
+    for step in range(present, ahead):
         for copy in fetches(step):
             copy.start()
     stack(x_refs, x_ref)
@@ -168,8 +178,11 @@
         def _():
             down_fetch.start()
 
-        for copy in fetches(step):
-            copy.wait()
+        @pl.when(step >= present)
+        def _():
+            for copy in fetches(step):
+                copy.wait()
+
         hidden_block(x_ref, gate_ref, up_ref, hidden_ref, part(step))
         return carry
 
@@ -193,20 +206,24 @@
     unstack(dot(hidden_ref[...], down_ref[...]).astype(bf16), out_refs)
 
 
-def expert_rows(xs, weights, first, block=512, ahead=2):
+def expert_rows(xs, weights, heads, ahead=3):
     rows, width = xs[0].shape
     hidden = weights[0].shape[1]
     blocks = len(xs)
     places = range(blocks, blocks + 3)
     results = [jax.ShapeDtypeStruct(x.shape, bf16) for x in xs]
     scratch = [pltpu.VMEM((blocks * rows, width), bf16), pltpu.VMEM((blocks * rows, hidden), bf16)]
-    if first:
+    if heads:
         out = call(
-            functools.partial(first_expert_kernel, blocks=blocks, block=block, ahead=ahead),
+            functools.partial(
+                first_expert_kernel, blocks=blocks, block=block, present=head // block, ahead=ahead
+            ),
             results + [jax.ShapeDtypeStruct(w.shape, bf16) for w in weights],
-            *xs, *weights,
+            *xs, *weights, *heads,
             budget=20,
             outside=places,
+            inside=range(blocks + 3, blocks + 5),
+            input_output_aliases={blocks + 3: blocks, blocks + 4: blocks + 1},
             scratch_shapes=scratch + [pltpu.SemaphoreType.DMA((3, hidden // block))],
         )
         return out[:blocks], out[blocks:]
@@ -303,20 +320,22 @@
         gradients(other_ref, mine_ref, embedded_ref, first, query_grad_ref, doc_grad_ref)
 
 
-def route(tokens, routes, norm_gain, router_weight):
+def route(tokens, routes, norm_gain, router_weight, gate, up):
     rows, width = tokens.shape
     experts = router_weight.shape[1]
-    operands = (tokens, routes.T, norm_gain, router_weight.T)
+    operands = (tokens, routes.T, norm_gain, router_weight.T, gate, up)
     return call(
-        route_kernel,
+        functools.partial(route_kernel, head=head),
         [
             *[jax.ShapeDtypeStruct((rows // 2, width), bf16) for _ in range(experts)],
             jax.ShapeDtypeStruct((rows, experts), f32),
             jax.ShapeDtypeStruct((rows, experts), f32),
+            jax.ShapeDtypeStruct(gate.shape, bf16),
+            jax.ShapeDtypeStruct(up.shape, bf16),
         ],
         *operands,
-        outside=(0, 1, 2, 3),
-        scratch_shapes=[pltpu.VMEM(x.shape, x.dtype) for x in operands]
+        outside=range(6),
+        scratch_shapes=[pltpu.VMEM(x.shape, x.dtype) for x in operands[:4]]
         + [pltpu.SemaphoreType.DMA((len(operands),))],
     )
 
@@ -350,7 +369,10 @@
 def body(tokens, routes, lengths, norm_gain, router_weight, gate_weight, up_weight, down_weight):
     width = tokens.shape[1]
     experts = router_weight.shape[1]
-    *outgoing, slots, weights = route(tokens, routes, norm_gain, router_weight)
+    matrices = [gate_weight[0], up_weight[0], down_weight[0]]
+    *outgoing, slots, weights, gate, up = route(
+        tokens, routes, norm_gain, router_weight, *matrices[:2]
+    )
 
     def pairs(move, back):
         places = [(e, target(e, move)) for e in range(experts)]
@@ -360,10 +382,10 @@
         return x if move == (0, 0) else lax.ppermute(x, "expert", pairs(move, back))
 
     incoming = {move: send(x, move) for move, x in zip(moves, outgoing)}
-    matrices = [gate_weight[0], up_weight[0], down_weight[0]]
-    backs = []
-    for at, group in enumerate(move_groups):
-        results, matrices = expert_rows([incoming[move] for move in group], matrices, at == 0)
+    backs, heads = [], [gate, up]
+    for group in move_groups:
+        results, matrices = expert_rows([incoming[move] for move in group], matrices, heads)
+        heads = []
         backs += [send(x, move, back=True) for move, x in zip(group, results)]
     hidden_out, embedded, kept, given = combine(tokens, slots, weights, backs, lengths)
 

time: 106 us -> 106 us (level)
  transfers between devices with their start and end apart: 16 -> 16, of which waited for: 4 -> 5; matrix products, arithmetic and copies ran while one was open for 0% -> 0% of each run, Pallas kernels for 21% -> 19%
where the time goes in v6:
time: 106 us
  starting transfers between devices  36.6 us (35%)
  blocking collectives  30.1 us (28%)
  Pallas kernels  29 us (27%)
  waiting for transfers between devices  9.53 us (9%)
    all_to_all x1, blocking collectives, body(): lax.all_to_all(copies, ('dp', 'expert'), split_axis=0, concat_axis=0, til...  30.1 us
    pallas_call x7, Pallas kernels, call(): pl.pallas_call(kernel, out_shape=outs, in_specs=[left if at in outside el...  29 us
    ppermute x14, starting transfers between devices, send(): return x if move == (0, 0) else lax.ppermute(x, 'expert', pairs(move, back))  27.3 us
    ppermute x1, starting transfers between devices, body(): taken = lax.ppermute(given, 'dp', swap)  6.76 us
    ppermute x14, waiting for transfers between devices, send(): return x if move == (0, 0) else lax.ppermute(x, 'expert', pairs(move, back))  5.66 us
    ppermute x1, waiting for transfers between devices, body(): other = lax.ppermute(mine, 'dp', swap)  3.04 us
    ppermute x1, starting transfers between devices, body(): other = lax.ppermute(mine, 'dp', swap)  2.5 us
  transfers between devices with their start and end apart: 16, of which 5 were waited for; matrix products, arithmetic and copies ran while one was open for 0% of the time, Pallas kernels for 19%

profile of v6, /device:TPU:1, one launch (start us, length us, event | category | flops | bytes accessed | tf_op | source)
XLA Modules:
  0.0 106.1 jit_solution(10363849130905126974)
XLA Ops:
  0.6 3.6 %shard_map.103 = (bf16[128,768]{1,0:T(8,128)(2,1)S(1)}, bf16[128,768]{1,0:T(8,128)(2,1)S(1)}, bf16[128,768]{1,0:T(8,128)(2,1)S(1)}, bf16[128,768]{1,0:T(8,128)(2...) custom-call(bf16[256,768]{1,0:T(8,128)(2,1)} %tokens_ref.1, ...), custom_call_target="tpu_custom_call" | custom-call | tf_op jit(solution)/shard_map/pallas_call | solution.py:64
  4.2 2.1 %collective-permute-start = (bf16[128,768]{1,0:T(8,128)(2,1)S(1)}, bf16[128,768]{1,0:T(8,128)(2,1)S(1)}, u32[]{:S(2)}, u32[]{:S(2)}) collective-permute-start(bf16[128,768]{1,0:T(8,128)(2,1)S(1)} %get-tuple-element.35), channel_id=1, source_target_pairs={{0,1},{1,2},{2,3},{3,0},{4,5},{5,6},{6,7},{7,4},{8,9},{9,10},{10,1... | collective-permute-start | bytes 589832 | tf_op jit(solution)/shard_map/ppermute | solution.py:382
  6.3 1.3 %collective-permute-start.1 = (bf16[128,768]{1,0:T(8,128)(2,1)S(1)}, bf16[128,768]{1,0:T(8,128)(2,1)S(1)}, u32[]{:S(2)}, u32[]{:S(2)}) collective-permute-start(bf16[128,768]{1,0:T(8,128)(2,1)S(1)} %get-tuple-element.36), channel_id=1, source_target_pairs={{0,3},{1,0},{2,1},{3,2},{4,7},{5,4},{6,5},{7,6},{8,11},{9,8},{10,9... | collective-permute-start | bytes 589832 | tf_op jit(solution)/shard_map/ppermute | solution.py:382
  7.7 3.7 %collective-permute-start.2 = (bf16[128,768]{1,0:T(8,128)(2,1)S(1)}, bf16[128,768]{1,0:T(8,128)(2,1)S(1)}, u32[]{:S(2)}, u32[]{:S(2)}) collective-permute-start(bf16[128,768]{1,0:T(8,128)(2,1)S(1)} %get-tuple-element.37), channel_id=1, source_target_pairs={{0,4},{1,5},{2,6},{3,7},{4,0},{5,1},{6,2},{7,3},{8,12},{9,13},{10,... | collective-permute-start | bytes 589832 | tf_op jit(solution)/shard_map/ppermute | solution.py:382
  11.4 1.5 %collective-permute-start.6 = (bf16[128,768]{1,0:T(8,128)(2,1)S(1)}, bf16[128,768]{1,0:T(8,128)(2,1)S(1)}, u32[]{:S(2)}, u32[]{:S(2)}) collective-permute-start(bf16[128,768]{1,0:T(8,128)(2,1)S(1)} %get-tuple-element.44), channel_id=1, source_target_pairs={{0,2},{1,3},{2,0},{3,1},{4,6},{5,7},{6,4},{7,5},{8,10},{9,11},{10,... | collective-permute-start | bytes 589832 | tf_op jit(solution)/shard_map/ppermute | solution.py:382
  12.9 0.0 collective-permute-start.7
  13.0 0.0 collective-permute-done.refs_1_
  13.0 5.1 %collective-permute-start.10 = (bf16[128,768]{1,0:T(8,128)(2,1)S(1)}, bf16[128,768]{1,0:T(8,128)(2,1)S(1)}, u32[]{:S(2)}, u32[]{:S(2)}) collective-permute-start(bf16[128,768]{1,0:T(8,128)(2,1)S(1)} %get-tuple-element.51), channel_id=1, source_target_pairs={{0,7},{1,4},{2,5},{3,6},{4,3},{5,0},{6,1},{7,2},{8,15},{9,12},{10,... | collective-permute-start | bytes 589832 | tf_op jit(solution)/shard_map/ppermute | solution.py:382
  18.0 0.0 collective-permute-done.2.refs_3_
  18.0 9.0 %shard_map.104 = (bf16[128,768]{1,0:T(8,128)(2,1)S(1)}, bf16[128,768]{1,0:T(8,128)(2,1)S(1)}, bf16[128,768]{1,0:T(8,128)(2,1)S(1)}, bf16[128,768]{1,0:T(8,128)(2...) custom-call(bf16[128,768]{1,0:T(8,128)(2,1)S(1)} %get-tuple-element., ...), custom_call_target="tpu_custom_call", output_to_operand_aliasing={{4}: (7, {}), {5}: (8, {})} | custom-call | tf_op jit(solution)/shard_map/pallas_call | solution.py:64
  27.1 1.7 %collective-permute-done.7.refs_1_ = bf16[128,768]{1,0:T(8,128)(2,1)S(1)} collective-permute-done((bf16[128,768]{1,0:T(8,128)(2,1)S(1)}, bf16[128,768]{1,0:T(8,128)(2,1)S(1)}, u32[]{:S(2)}, u32[]{:S(2)}) %collective-permute-start.7) | collective-permute-done | bytes 196640 | tf_op jit(solution)/shard_map/ppermute | solution.py:382
  28.8 4.9 %shard_map.105 = (bf16[128,768]{1,0:T(8,128)(2,1)S(1)}, bf16[128,768]{1,0:T(8,128)(2,1)S(1)}) custom-call(bf16[128,768]{1,0:T(8,128)(2,1)S(1)} %collective-permute-done.6.refs_0_, bf16[128,768]{1,0:T(8,128)(2,1)S(1)} %collective-permute-done.7.refs_1_, bf16[768,3072]{1,0:T(8,128)(2,1)S(1)} %get-tuple-element.46.refs_2_, ...), custom_call_target="tpu_custom_call" | custom-call | tf_op jit(solution)/shard_map/pallas_call | solution.py:64
  33.7 1.1 %collective-permute-start.8 = (bf16[128,768]{1,0:T(8,128)(2,1)S(1)}, bf16[128,768]{1,0:T(8,128)(2,1)S(1)}, u32[]{:S(2)}, u32[]{:S(2)}) collective-permute-start(bf16[128,768]{1,0:T(8,128)(2,1)S(1)} %get-tuple-element.49), channel_id=1, source_target_pairs={{2,0},{3,1},{0,2},{1,3},{6,4},{7,5},{4,6},{5,7},{10,8},{11,9},{8,1... | collective-permute-start | bytes 589832 | tf_op jit(solution)/shard_map/ppermute | solution.py:382
  34.8 2.3 %collective-permute-start.9 = (bf16[128,768]{1,0:T(8,128)(2,1)S(1)}, bf16[128,768]{1,0:T(8,128)(2,1)S(1)}, u32[]{:S(2)}, u32[]{:S(2)}) collective-permute-start(bf16[128,768]{1,0:T(8,128)(2,1)S(1)} %get-tuple-element.50), channel_id=1, source_target_pairs={{5,0},{6,1},{7,2},{4,3},{1,4},{2,5},{3,6},{0,7},{13,8},{14,9},{15,... | collective-permute-start | bytes 589832 | tf_op jit(solution)/shard_map/ppermute | solution.py:382
  37.2 3.8 %collective-permute-start.3 = (bf16[128,768]{1,0:T(8,128)(2,1)S(1)}, bf16[128,768]{1,0:T(8,128)(2,1)S(1)}, u32[]{:S(2)}, u32[]{:S(2)}) collective-permute-start(bf16[128,768]{1,0:T(8,128)(2,1)S(1)} %get-tuple-element.41), channel_id=1, source_target_pairs={{1,0},{2,1},{3,2},{0,3},{5,4},{6,5},{7,6},{4,7},{9,8},{10,9},{11,1... | collective-permute-start | bytes 589832 | tf_op jit(solution)/shard_map/ppermute | solution.py:382
  40.9 0.0 copy-start
  41.0 0.0 copy-start.1
  41.0 0.1 collective-permute-start.5
  41.1 5.0 %shard_map.107 = (bf16[128,768]{1,0:T(8,128)(2,1)S(1)}, bf16[128,768]{1,0:T(8,128)(2,1)S(1)}) custom-call(bf16[128,768]{1,0:T(8,128)(2,1)S(1)} %collective-permute-done.10.refs_0_, bf16[128,768]{1,0:T(8,128)(2,1)S(1)} %collective-permute-done.11.refs_1_, bf16[768,3072]{1,0:T(8,128)(2,1)S(1)} %get-tuple-element.46.refs_2_, ...), custom_call_target="tpu_custom_call" | custom-call | tf_op jit(solution)/shard_map/pallas_call | solution.py:64
  46.0 2.4 %collective-permute-start.12 = (bf16[128,768]{1,0:T(8,128)(2,1)S(1)}, bf16[128,768]{1,0:T(8,128)(2,1)S(1)}, u32[]{:S(2)}, u32[]{:S(2)}) collective-permute-start(bf16[128,768]{1,0:T(8,128)(2,1)S(1)} %get-tuple-element.53), channel_id=1, source_target_pairs={{7,0},{4,1},{5,2},{6,3},{3,4},{0,5},{1,6},{2,7},{15,8},{12,9},{13,... | collective-permute-start | bytes 589832 | tf_op jit(solution)/shard_map/ppermute | solution.py:382
  48.4 3.8 %collective-permute-start.13 = (bf16[128,768]{1,0:T(8,128)(2,1)S(1)}, bf16[128,768]{1,0:T(8,128)(2,1)S(1)}, u32[]{:S(2)}, u32[]{:S(2)}) collective-permute-start(bf16[128,768]{1,0:T(8,128)(2,1)S(1)} %get-tuple-element.54), channel_id=1, source_target_pairs={{6,0},{7,1},{4,2},{5,3},{2,4},{3,5},{0,6},{1,7},{14,8},{15,9},{12,... | collective-permute-start | bytes 589832 | tf_op jit(solution)/shard_map/ppermute | solution.py:382
  52.3 1.2 %shard_map.106.early_ref = f32[256,768]{1,0:T(8,128)S(1)} custom-call(bf16[256,768]{1,0:T(8,128)(2,1)S(1)} %copy-done, f32[256,8]{1,0:T(8,128)S(1)} %get-tuple-element.32.slots_ref, f32[256,8]{1,0:T(8,128)S(1)} %get-tuple-element.33.weights_ref, bf16[128,768]{1,0:T(8,128)(2,1)S(1)} %get-tuple-element.40.refs_0_, ...), custom_call_target="tpu_custom_call" | custom-call | tf_op jit(solution)/shard_map/pallas_call | solution.py:64
  53.5 0.8 collective-permute-done.12.refs_0_
  54.4 3.1 %collective-permute-done.13.refs_1_ = bf16[128,768]{1,0:T(8,128)(2,1)S(1)} collective-permute-done((bf16[128,768]{1,0:T(8,128)(2,1)S(1)}, bf16[128,768]{1,0:T(8,128)(2,1)S(1)}, u32[]{:S(2)}, u32[]{:S(2)}) %collective-permute-start.13) | collective-permute-done | bytes 196640 | tf_op jit(solution)/shard_map/ppermute | solution.py:382
  57.5 1.4 %shard_map.108 = (bf16[256,768]{1,0:T(8,128)(2,1)}, f32[16,768]{1,0:T(8,128)S(1)}, bf16[8,768]{1,0:T(8,128)(2,1)S(1)}, bf16[8,768]{1,0:T(8,128)(2,1)S(1)}) custom-call(f32[256,768]{1,0:T(8,128)S(1)} %shard_map.106.early_ref, f32[256,8]{1,0:T(8,128)S(1)} %get-tuple-element.32.slots_ref, f32[256,8]{1,0:T(8,128)S(1)} %get-tuple-element.33.weights_ref, ...), custom_call_target="tpu_custom_call" | custom-call | tf_op jit(solution)/shard_map/pallas_call | solution.py:64
  58.9 6.8 %collective-permute-start.14 = (bf16[8,768]{1,0:T(8,128)(2,1)S(1)}, bf16[8,768]{1,0:T(8,128)(2,1)S(1)}, u32[]{:S(2)}, u32[]{:S(2)}) collective-permute-start(bf16[8,768]{1,0:T(8,128)(2,1)S(1)} %get-tuple-element.57), channel_id=1, source_target_pairs={{0,8},{8,0},{16,24},{24,16},{32,40},{40,32},{48,56},{56,48},{64,72... | collective-permute-start | bytes 36872 | tf_op jit(solution)/shard_map/ppermute | solution.py:398
  65.7 0.8 collective-permute-done.14
  66.5 0.1 broadcast_in_dim.2
  66.6 30.1 %all_to_all.5 = bf16[64,16,768]{2,1,0:T(8,128)(2,1)S(1)} all-to-all(bf16[64,16,768]{2,1,0:T(8,128)(2,1)S(1)} %broadcast_in_dim.2), channel_id=1, replica_groups={{0,1,2,3,4,5,6,7,16,17,18,19,20,21,22,23,32,33,34,35,36,37,38,39,48,49,..., dimensions={0} | all-to-all | bytes 3145728 | tf_op jit(solution)/shard_map/all_to_all | solution.py:403
  96.7 2.5 %collective-permute-start.15 = (bf16[1024,768]{1,0:T(8,128)(2,1)S(1)}, bf16[1024,768]{1,0:T(8,128)(2,1)S(1)}, u32[]{:S(2)}, u32[]{:S(2)}) collective-permute-start(bf16[1024,768]{1,0:T(8,128)(2,1)S(1)} %bitcast.6), channel_id=1, source_target_pairs={{0,8},{8,0},{16,24},{24,16},{32,40},{40,32},{48,56},{56,48},{64,72... | collective-permute-start | bytes 4718600 | tf_op jit(solution)/shard_map/ppermute | solution.py:406
  99.2 3.0 %collective-permute-done.15.other_ref = bf16[1024,768]{1,0:T(8,128)(2,1)S(1)} collective-permute-done((bf16[1024,768]{1,0:T(8,128)(2,1)S(1)}, bf16[1024,768]{1,0:T(8,128)(2,1)S(1)}, u32[]{:S(2)}, u32[]{:S(2)}) %collective-permute-start.15) | collective-permute-done | bytes 1572896 | tf_op jit(solution)/shard_map/ppermute | solution.py:406
  102.3 3.8 %shard_map.109 = (f32[8,768]{1,0:T(8,128)}, f32[8,768]{1,0:T(8,128)}) custom-call(bf16[1024,768]{1,0:T(8,128)(2,1)S(1)} %bitcast.7, bf16[1024,768]{1,0:T(8,128)(2,1)S(1)} %collective-permute-done.15.other_ref, f32[16,768]{1,0:T(8,128)S(1)} %get-tuple-element.58.embedded_ref), custom_call_target="tpu_custom_call" | custom-call | tf_op jit(solution)/shard_map/pallas_call | solution.py:64
  (15 shorter events, 0.0 us)
Async XLA Ops:
  4.2 8.7 %collective-permute-start = (bf16[128,768]{1,0:T(8,128)(2,1)S(1)}, bf16[128,768]{1,0:T(8,128)(2,1)S(1)}, u32[]{:S(2)}, u32[]{:S(2)}) collective-permute-start(bf16[128,768]{1,0:T(8,128)(2,1)S(1)} %get-tuple-element.35), channel_id=1, source_target_pairs={{0,1},{1,2},{2,3},{3,0},{4,5},{5,6},{6,7},{7,4},{8,9},{9,10},{10,1... | collective-permute-start | bytes 589832 | tf_op jit(solution)/shard_map/ppermute | solution.py:382
  6.3 11.7 %collective-permute-start.1 = (bf16[128,768]{1,0:T(8,128)(2,1)S(1)}, bf16[128,768]{1,0:T(8,128)(2,1)S(1)}, u32[]{:S(2)}, u32[]{:S(2)}) collective-permute-start(bf16[128,768]{1,0:T(8,128)(2,1)S(1)} %get-tuple-element.36), channel_id=1, source_target_pairs={{0,3},{1,0},{2,1},{3,2},{4,7},{5,4},{6,5},{7,6},{8,11},{9,8},{10,9... | collective-permute-start | bytes 589832 | tf_op jit(solution)/shard_map/ppermute | solution.py:382
  7.7 10.3 %collective-permute-start.2 = (bf16[128,768]{1,0:T(8,128)(2,1)S(1)}, bf16[128,768]{1,0:T(8,128)(2,1)S(1)}, u32[]{:S(2)}, u32[]{:S(2)}) collective-permute-start(bf16[128,768]{1,0:T(8,128)(2,1)S(1)} %get-tuple-element.37), channel_id=1, source_target_pairs={{0,4},{1,5},{2,6},{3,7},{4,0},{5,1},{6,2},{7,3},{8,12},{9,13},{10,... | collective-permute-start | bytes 589832 | tf_op jit(solution)/shard_map/ppermute | solution.py:382
  11.4 15.7 %collective-permute-start.6 = (bf16[128,768]{1,0:T(8,128)(2,1)S(1)}, bf16[128,768]{1,0:T(8,128)(2,1)S(1)}, u32[]{:S(2)}, u32[]{:S(2)}) collective-permute-start(bf16[128,768]{1,0:T(8,128)(2,1)S(1)} %get-tuple-element.44), channel_id=1, source_target_pairs={{0,2},{1,3},{2,0},{3,1},{4,6},{5,7},{6,4},{7,5},{8,10},{9,11},{10,... | collective-permute-start | bytes 589832 | tf_op jit(solution)/shard_map/ppermute | solution.py:382
  12.9 15.8 %collective-permute-start.7 = (bf16[128,768]{1,0:T(8,128)(2,1)S(1)}, bf16[128,768]{1,0:T(8,128)(2,1)S(1)}, u32[]{:S(2)}, u32[]{:S(2)}) collective-permute-start(bf16[128,768]{1,0:T(8,128)(2,1)S(1)} %get-tuple-element.45), channel_id=1, source_target_pairs={{0,5},{1,6},{2,7},{3,4},{4,1},{5,2},{6,3},{7,0},{8,13},{9,14},{10,... | collective-permute-start | bytes 589832 | tf_op jit(solution)/shard_map/ppermute | solution.py:382
  13.0 28.0 %collective-permute-start.10 = (bf16[128,768]{1,0:T(8,128)(2,1)S(1)}, bf16[128,768]{1,0:T(8,128)(2,1)S(1)}, u32[]{:S(2)}, u32[]{:S(2)}) collective-permute-start(bf16[128,768]{1,0:T(8,128)(2,1)S(1)} %get-tuple-element.51), channel_id=1, source_target_pairs={{0,7},{1,4},{2,5},{3,6},{4,3},{5,0},{6,1},{7,2},{8,15},{9,12},{10,... | collective-permute-start | bytes 589832 | tf_op jit(solution)/shard_map/ppermute | solution.py:382
  18.0 22.9 %collective-permute-start.11 = (bf16[128,768]{1,0:T(8,128)(2,1)S(1)}, bf16[128,768]{1,0:T(8,128)(2,1)S(1)}, u32[]{:S(2)}, u32[]{:S(2)}) collective-permute-start(bf16[128,768]{1,0:T(8,128)(2,1)S(1)} %get-tuple-element.52), channel_id=1, source_target_pairs={{0,6},{1,7},{2,4},{3,5},{4,2},{5,3},{6,0},{7,1},{8,14},{9,15},{10,... | collective-permute-start | bytes 589832 | tf_op jit(solution)/shard_map/ppermute | solution.py:382
  33.7 12.3 %collective-permute-start.8 = (bf16[128,768]{1,0:T(8,128)(2,1)S(1)}, bf16[128,768]{1,0:T(8,128)(2,1)S(1)}, u32[]{:S(2)}, u32[]{:S(2)}) collective-permute-start(bf16[128,768]{1,0:T(8,128)(2,1)S(1)} %get-tuple-element.49), channel_id=1, source_target_pairs={{2,0},{3,1},{0,2},{1,3},{6,4},{7,5},{4,6},{5,7},{10,8},{11,9},{8,1... | collective-permute-start | bytes 589832 | tf_op jit(solution)/shard_map/ppermute | solution.py:382
  34.8 13.6 %collective-permute-start.9 = (bf16[128,768]{1,0:T(8,128)(2,1)S(1)}, bf16[128,768]{1,0:T(8,128)(2,1)S(1)}, u32[]{:S(2)}, u32[]{:S(2)}) collective-permute-start(bf16[128,768]{1,0:T(8,128)(2,1)S(1)} %get-tuple-element.50), channel_id=1, source_target_pairs={{5,0},{6,1},{7,2},{4,3},{1,4},{2,5},{3,6},{0,7},{13,8},{14,9},{15,... | collective-permute-start | bytes 589832 | tf_op jit(solution)/shard_map/ppermute | solution.py:382
  37.2 15.1 %collective-permute-start.3 = (bf16[128,768]{1,0:T(8,128)(2,1)S(1)}, bf16[128,768]{1,0:T(8,128)(2,1)S(1)}, u32[]{:S(2)}, u32[]{:S(2)}) collective-permute-start(bf16[128,768]{1,0:T(8,128)(2,1)S(1)} %get-tuple-element.41), channel_id=1, source_target_pairs={{1,0},{2,1},{3,2},{0,3},{5,4},{6,5},{7,6},{4,7},{9,8},{10,9},{11,1... | collective-permute-start | bytes 589832 | tf_op jit(solution)/shard_map/ppermute | solution.py:382
  40.9 11.4 %collective-permute-start.4 = (bf16[128,768]{1,0:T(8,128)(2,1)S(1)}, bf16[128,768]{1,0:T(8,128)(2,1)S(1)}, u32[]{:S(2)}, u32[]{:S(2)}) collective-permute-start(bf16[128,768]{1,0:T(8,128)(2,1)S(1)} %get-tuple-element.42), channel_id=1, source_target_pairs={{3,0},{0,1},{1,2},{2,3},{7,4},{4,5},{5,6},{6,7},{11,8},{8,9},{9,10... | collective-permute-start | bytes 589832 | tf_op jit(solution)/shard_map/ppermute | solution.py:382
  40.9 11.4 %copy-start = (bf16[256,768]{1,0:T(8,128)(2,1)S(1)}, bf16[256,768]{1,0:T(8,128)(2,1)}, u32[]{:S(2)}) copy-start(bf16[256,768]{1,0:T(8,128)(2,1)} %tokens_ref.1) | copy-start | bytes 1179652
  41.0 16.6 %copy-start.1 = (s32[1,16]{1,0:T(1,128)S(1)}, s32[1,16]{1,0:T(1,128)}, u32[]{:S(2)}) copy-start(s32[1,16]{1,0:T(1,128)} %lengths_ref.1) | copy-start | bytes 196
  41.0 11.3 %collective-permute-start.5 = (bf16[128,768]{1,0:T(8,128)(2,1)S(1)}, bf16[128,768]{1,0:T(8,128)(2,1)S(1)}, u32[]{:S(2)}, u32[]{:S(2)}) collective-permute-start(bf16[128,768]{1,0:T(8,128)(2,1)S(1)} %get-tuple-element.43), channel_id=1, source_target_pairs={{4,0},{5,1},{6,2},{7,3},{0,4},{1,5},{2,6},{3,7},{12,8},{13,9},{14,... | collective-permute-start | bytes 589832 | tf_op jit(solution)/shard_map/ppermute | solution.py:382
  46.0 8.3 %collective-permute-start.12 = (bf16[128,768]{1,0:T(8,128)(2,1)S(1)}, bf16[128,768]{1,0:T(8,128)(2,1)S(1)}, u32[]{:S(2)}, u32[]{:S(2)}) collective-permute-start(bf16[128,768]{1,0:T(8,128)(2,1)S(1)} %get-tuple-element.53), channel_id=1, source_target_pairs={{7,0},{4,1},{5,2},{6,3},{3,4},{0,5},{1,6},{2,7},{15,8},{12,9},{13,... | collective-permute-start | bytes 589832 | tf_op jit(solution)/shard_map/ppermute | solution.py:382
  48.4 9.1 %collective-permute-start.13 = (bf16[128,768]{1,0:T(8,128)(2,1)S(1)}, bf16[128,768]{1,0:T(8,128)(2,1)S(1)}, u32[]{:S(2)}, u32[]{:S(2)}) collective-permute-start(bf16[128,768]{1,0:T(8,128)(2,1)S(1)} %get-tuple-element.54), channel_id=1, source_target_pairs={{6,0},{7,1},{4,2},{5,3},{2,4},{3,5},{0,6},{1,7},{14,8},{15,9},{12,... | collective-permute-start | bytes 589832 | tf_op jit(solution)/shard_map/ppermute | solution.py:382
  58.9 7.6 %collective-permute-start.14 = (bf16[8,768]{1,0:T(8,128)(2,1)S(1)}, bf16[8,768]{1,0:T(8,128)(2,1)S(1)}, u32[]{:S(2)}, u32[]{:S(2)}) collective-permute-start(bf16[8,768]{1,0:T(8,128)(2,1)S(1)} %get-tuple-element.57), channel_id=1, source_target_pairs={{0,8},{8,0},{16,24},{24,16},{32,40},{40,32},{48,56},{56,48},{64,72... | collective-permute-start | bytes 36872 | tf_op jit(solution)/shard_map/ppermute | solution.py:398
  96.7 5.5 %collective-permute-start.15 = (bf16[1024,768]{1,0:T(8,128)(2,1)S(1)}, bf16[1024,768]{1,0:T(8,128)(2,1)S(1)}, u32[]{:S(2)}, u32[]{:S(2)}) collective-permute-start(bf16[1024,768]{1,0:T(8,128)(2,1)S(1)} %bitcast.6), channel_id=1, source_target_pairs={{0,8},{8,0},{16,24},{24,16},{32,40},{40,32},{48,56},{56,48},{64,72... | collective-permute-start | bytes 4718600 | tf_op jit(solution)/shard_map/ppermute | solution.py:406

commit v7 on v5

--- a/solution.py
+++ b/solution.py
@@ -14,6 +14,7 @@
 bf16 = jnp.bfloat16
 mebibyte = 1024 * 1024
 plane = 4
+line = 4
 move_groups = (
     ((0, 0), (1, 0), (3, 0), (0, 1)),
     ((2, 0), (1, 1)),
@@ -291,8 +292,8 @@
 def gradient_kernel(mine_ref, other_ref, embedded_ref, query_grad_ref, doc_grad_ref):
     dp = lax.axis_index("dp")
     core = dp % 2
-    chip = dp // 2 * lax.axis_size("expert") + lax.axis_index("expert")
-    first = (chip * 2 + core) * (embedded_ref.shape[0] // 2)
+    rank = dp // 2 * (lax.axis_size("expert") // plane) + lax.axis_index("expert") // plane
+    first = (rank * 2 + core) * (embedded_ref.shape[0] // 2)
 
     @pl.when(core == 0)
     def _():
@@ -368,20 +369,28 @@
     hidden_out, embedded, kept, given = combine(tokens, slots, weights, backs, lengths)
 
     groups = lax.axis_size("dp")
-    devices = groups * experts
-    chips = devices // 2
-    same_core = [[d for d in range(devices) if d // experts % 2 == core] for core in range(2)]
     swap = [(i, i ^ 1) for i in range(groups)]
     core = lax.axis_index("dp") % 2
     taken = lax.ppermute(given, "dp", swap)
     shard = jnp.concatenate(
         [jnp.where(core == 0, kept, taken), jnp.where(core == 0, taken, kept)]
     )
-    copies = jnp.broadcast_to(shard[None], (chips,) + shard.shape)
-    mine = lax.all_to_all(
-        copies, ("dp", "expert"), split_axis=0, concat_axis=0, tiled=True, axis_index_groups=same_core
+    colours = [[] for _ in range(2 * plane)]
+    for device in range(groups * experts):
+        dp, expert = divmod(device, experts)
+        colours[(expert + 2 * (dp // line)) % plane * 2 + dp % 2].append(device)
+    copies = jnp.broadcast_to(shard[None], (len(colours[0]),) + shard.shape)
+    own = lax.all_to_all(
+        copies, ("dp", "expert"), split_axis=0, concat_axis=0, tiled=True, axis_index_groups=colours
     ).reshape(-1, width)
-    other = lax.ppermute(mine, "dp", swap)
+    blocks = [
+        own,
+        lax.ppermute(own, "expert", pairs((3, 0), False)),
+        lax.ppermute(own, "dp", [(i, (i - line) % groups) for i in range(groups)]),
+        lax.ppermute(own, "expert", pairs((1, 0), False)),
+    ]
+    mine = jnp.concatenate(blocks)
+    other = jnp.concatenate([lax.ppermute(x, "dp", swap) for x in blocks])
     query_grad, doc_grad = info_nce(mine, other, embedded)
     return (hidden_out, query_grad, doc_grad)
 

time: 106 us -> 102 us (0.962)
  blocking collectives: 30.7 us -> 16.7 us
  starting transfers between devices: 35.9 us -> 44.8 us
  waiting for transfers between devices: 8.69 us -> 10.3 us
    all_to_all x1, blocking collectives: 30.7 us -> 16.7 us  [body(): lax.all_to_all(copies, ('dp', 'expert'), split_axis=0, concat_axis=0, til...]
    ppermute x1 -> x7, starting transfers between devices: 2.5 us -> 11.4 us  [the longest x4 9.36 us: body(): other = jnp.concatenate([lax.ppermute(x, 'dp', swap) for x in blocks])]
    ppermute x1 -> x7, waiting for transfers between devices: 3.04 us -> 4.59 us  [the longest x1 3.37 us: body(): lax.ppermute(own, 'expert', pairs((3, 0), False))]
  transfers between devices with their start and end apart: 16 -> 22, of which waited for: 4 -> 5; matrix products, arithmetic and copies ran while one was open for 0% -> 0% of each run, Pallas kernels for 21% -> 21%
where the time goes in v7:
time: 102 us
  starting transfers between devices  44.8 us (44%)
  Pallas kernels  29.3 us (29%)
  blocking collectives  16.7 us (16%)
  waiting for transfers between devices  10.3 us (10%)
    pallas_call x7, Pallas kernels, call(): pl.pallas_call(kernel, out_shape=outs, in_specs=[left if at in outside el...  29.3 us
    ppermute x14, starting transfers between devices, send(): return x if move == (0, 0) else lax.ppermute(x, 'expert', pairs(move, back))  27.3 us
    all_to_all x1, blocking collectives, body(): lax.all_to_all(copies, ('dp', 'expert'), split_axis=0, concat_axis=0, til...  16.7 us
    ppermute x4, starting transfers between devices, body(): other = jnp.concatenate([lax.ppermute(x, 'dp', swap) for x in blocks])  9.36 us
    ppermute x1, starting transfers between devices, body(): taken = lax.ppermute(given, 'dp', swap)  6.13 us
    ppermute x14, waiting for transfers between devices, send(): return x if move == (0, 0) else lax.ppermute(x, 'expert', pairs(move, back))  4.82 us
    ppermute x1, waiting for transfers between devices, body(): lax.ppermute(own, 'expert', pairs((3, 0), False))  3.37 us
  transfers between devices with their start and end apart: 22, of which 5 were waited for; matrix products, arithmetic and copies ran while one was open for 0% of the time, Pallas kernels for 21%

profile of v7, /device:TPU:1, one launch (start us, length us, event | category | flops | bytes accessed | tf_op | source)
XLA Modules:
  0.0 102.2 jit_solution(9060096775308286202)
XLA Ops:
  0.6 2.2 %shard_map.103 = (bf16[128,768]{1,0:T(8,128)(2,1)S(1)}, bf16[128,768]{1,0:T(8,128)(2,1)S(1)}, bf16[128,768]{1,0:T(8,128)(2,1)S(1)}, bf16[128,768]{1,0:T(8,128)(2...) custom-call(bf16[256,768]{1,0:T(8,128)(2,1)} %tokens_ref.1, ...), custom_call_target="tpu_custom_call" | custom-call | tf_op jit(solution)/shard_map/pallas_call | solution.py:63
  2.8 2.1 %collective-permute-start = (bf16[128,768]{1,0:T(8,128)(2,1)S(1)}, bf16[128,768]{1,0:T(8,128)(2,1)S(1)}, u32[]{:S(2)}, u32[]{:S(2)}) collective-permute-start(bf16[128,768]{1,0:T(8,128)(2,1)S(1)} %get-tuple-element.33), channel_id=1, source_target_pairs={{0,1},{1,2},{2,3},{3,0},{4,5},{5,6},{6,7},{7,4},{8,9},{9,10},{10,1... | collective-permute-start | bytes 589832 | tf_op jit(solution)/shard_map/ppermute | solution.py:361
  4.9 1.4 %collective-permute-start.1 = (bf16[128,768]{1,0:T(8,128)(2,1)S(1)}, bf16[128,768]{1,0:T(8,128)(2,1)S(1)}, u32[]{:S(2)}, u32[]{:S(2)}) collective-permute-start(bf16[128,768]{1,0:T(8,128)(2,1)S(1)} %get-tuple-element.34), channel_id=1, source_target_pairs={{0,3},{1,0},{2,1},{3,2},{4,7},{5,4},{6,5},{7,6},{8,11},{9,8},{10,9... | collective-permute-start | bytes 589832 | tf_op jit(solution)/shard_map/ppermute | solution.py:361
  6.3 3.7 %collective-permute-start.2 = (bf16[128,768]{1,0:T(8,128)(2,1)S(1)}, bf16[128,768]{1,0:T(8,128)(2,1)S(1)}, u32[]{:S(2)}, u32[]{:S(2)}) collective-permute-start(bf16[128,768]{1,0:T(8,128)(2,1)S(1)} %get-tuple-element.35), channel_id=1, source_target_pairs={{0,4},{1,5},{2,6},{3,7},{4,0},{5,1},{6,2},{7,3},{8,12},{9,13},{10,... | collective-permute-start | bytes 589832 | tf_op jit(solution)/shard_map/ppermute | solution.py:361
  10.0 1.5 %collective-permute-start.6 = (bf16[128,768]{1,0:T(8,128)(2,1)S(1)}, bf16[128,768]{1,0:T(8,128)(2,1)S(1)}, u32[]{:S(2)}, u32[]{:S(2)}) collective-permute-start(bf16[128,768]{1,0:T(8,128)(2,1)S(1)} %get-tuple-element.40), channel_id=1, source_target_pairs={{0,2},{1,3},{2,0},{3,1},{4,6},{5,7},{6,4},{7,5},{8,10},{9,11},{10,... | collective-permute-start | bytes 589832 | tf_op jit(solution)/shard_map/ppermute | solution.py:361
  11.6 5.0 %collective-permute-start.10 = (bf16[128,768]{1,0:T(8,128)(2,1)S(1)}, bf16[128,768]{1,0:T(8,128)(2,1)S(1)}, u32[]{:S(2)}, u32[]{:S(2)}) collective-permute-start(bf16[128,768]{1,0:T(8,128)(2,1)S(1)} %get-tuple-element.47), channel_id=1, source_target_pairs={{0,7},{1,4},{2,5},{3,6},{4,3},{5,0},{6,1},{7,2},{8,15},{9,12},{10,... | collective-permute-start | bytes 589832 | tf_op jit(solution)/shard_map/ppermute | solution.py:361
  16.6 10.7 %shard_map.104 = (bf16[128,768]{1,0:T(8,128)(2,1)S(1)}, bf16[128,768]{1,0:T(8,128)(2,1)S(1)}, bf16[128,768]{1,0:T(8,128)(2,1)S(1)}, bf16[128,768]{1,0:T(8,128)(2...) custom-call(bf16[128,768]{1,0:T(8,128)(2,1)S(1)} %get-tuple-element.32.refs_0_,, ...), custom_call_target="tpu_custom_call" | custom-call | tf_op jit(solution)/shard_map/pallas_call | solution.py:63
  27.4 5.0 %shard_map.105 = (bf16[128,768]{1,0:T(8,128)(2,1)S(1)}, bf16[128,768]{1,0:T(8,128)(2,1)S(1)}) custom-call(bf16[128,768]{1,0:T(8,128)(2,1)S(1)} %collective-permute-done.6.refs_0_, bf16[128,768]{1,0:T(8,128)(2,1)S(1)} %collective-permute-done.7.refs_1_, bf16[768,3072]{1,0:T(8,128)(2,1)S(1)} %get-tuple-element.42.refs_2_, ...), custom_call_target="tpu_custom_call" | custom-call | tf_op jit(solution)/shard_map/pallas_call | solution.py:63
  32.3 2.8 %collective-permute-start.8 = (bf16[128,768]{1,0:T(8,128)(2,1)S(1)}, bf16[128,768]{1,0:T(8,128)(2,1)S(1)}, u32[]{:S(2)}, u32[]{:S(2)}) collective-permute-start(bf16[128,768]{1,0:T(8,128)(2,1)S(1)} %get-tuple-element.45), channel_id=1, source_target_pairs={{2,0},{3,1},{0,2},{1,3},{6,4},{7,5},{4,6},{5,7},{10,8},{11,9},{8,1... | collective-permute-start | bytes 589832 | tf_op jit(solution)/shard_map/ppermute | solution.py:361
  35.1 2.3 %collective-permute-start.9 = (bf16[128,768]{1,0:T(8,128)(2,1)S(1)}, bf16[128,768]{1,0:T(8,128)(2,1)S(1)}, u32[]{:S(2)}, u32[]{:S(2)}) collective-permute-start(bf16[128,768]{1,0:T(8,128)(2,1)S(1)} %get-tuple-element.46), channel_id=1, source_target_pairs={{5,0},{6,1},{7,2},{4,3},{1,4},{2,5},{3,6},{0,7},{13,8},{14,9},{15,... | collective-permute-start | bytes 589832 | tf_op jit(solution)/shard_map/ppermute | solution.py:361
  37.4 2.1 %collective-permute-start.3 = (bf16[128,768]{1,0:T(8,128)(2,1)S(1)}, bf16[128,768]{1,0:T(8,128)(2,1)S(1)}, u32[]{:S(2)}, u32[]{:S(2)}) collective-permute-start(bf16[128,768]{1,0:T(8,128)(2,1)S(1)} %get-tuple-element.37), channel_id=1, source_target_pairs={{1,0},{2,1},{3,2},{0,3},{5,4},{6,5},{7,6},{4,7},{9,8},{10,9},{11,1... | collective-permute-start | bytes 589832 | tf_op jit(solution)/shard_map/ppermute | solution.py:361
  39.6 5.0 %shard_map.107 = (bf16[128,768]{1,0:T(8,128)(2,1)S(1)}, bf16[128,768]{1,0:T(8,128)(2,1)S(1)}) custom-call(bf16[128,768]{1,0:T(8,128)(2,1)S(1)} %collective-permute-done.10.refs_0_, bf16[128,768]{1,0:T(8,128)(2,1)S(1)} %collective-permute-done.11.refs_1_, bf16[768,3072]{1,0:T(8,128)(2,1)S(1)} %get-tuple-element.42.refs_2_, ...), custom_call_target="tpu_custom_call" | custom-call | tf_op jit(solution)/shard_map/pallas_call | solution.py:63
  44.6 3.8 %collective-permute-start.12 = (bf16[128,768]{1,0:T(8,128)(2,1)S(1)}, bf16[128,768]{1,0:T(8,128)(2,1)S(1)}, u32[]{:S(2)}, u32[]{:S(2)}) collective-permute-start(bf16[128,768]{1,0:T(8,128)(2,1)S(1)} %get-tuple-element.49), channel_id=1, source_target_pairs={{7,0},{4,1},{5,2},{6,3},{3,4},{0,5},{1,6},{2,7},{15,8},{12,9},{13,... | collective-permute-start | bytes 589832 | tf_op jit(solution)/shard_map/ppermute | solution.py:361
  48.5 2.4 %collective-permute-start.13 = (bf16[128,768]{1,0:T(8,128)(2,1)S(1)}, bf16[128,768]{1,0:T(8,128)(2,1)S(1)}, u32[]{:S(2)}, u32[]{:S(2)}) collective-permute-start(bf16[128,768]{1,0:T(8,128)(2,1)S(1)} %get-tuple-element.50), channel_id=1, source_target_pairs={{6,0},{7,1},{4,2},{5,3},{2,4},{3,5},{0,6},{1,7},{14,8},{15,9},{12,... | collective-permute-start | bytes 589832 | tf_op jit(solution)/shard_map/ppermute | solution.py:361
  50.9 1.2 %shard_map.106.early_ref = f32[256,768]{1,0:T(8,128)S(1)} custom-call(bf16[256,768]{1,0:T(8,128)(2,1)S(1)} %copy-done, f32[256,8]{1,0:T(8,128)S(1)} %get-tuple-element.30.slots_ref, f32[256,8]{1,0:T(8,128)S(1)} %get-tuple-element.31.weights_ref, bf16[128,768]{1,0:T(8,128)(2,1)S(1)} %get-tuple-element.36.refs_0_, ...), custom_call_target="tpu_custom_call" | custom-call | tf_op jit(solution)/shard_map/pallas_call | solution.py:63
  52.1 0.9 collective-permute-done.12.refs_0_
  53.0 3.9 %collective-permute-done.13.refs_1_ = bf16[128,768]{1,0:T(8,128)(2,1)S(1)} collective-permute-done((bf16[128,768]{1,0:T(8,128)(2,1)S(1)}, bf16[128,768]{1,0:T(8,128)(2,1)S(1)}, u32[]{:S(2)}, u32[]{:S(2)}) %collective-permute-start.13) | collective-permute-done | bytes 196640 | tf_op jit(solution)/shard_map/ppermute | solution.py:361
  56.9 1.4 %shard_map.108 = (bf16[256,768]{1,0:T(8,128)(2,1)}, f32[16,768]{1,0:T(8,128)S(1)}, bf16[8,768]{1,0:T(8,128)(2,1)S(1)}, bf16[8,768]{1,0:T(8,128)(2,1)S(1)}) custom-call(f32[256,768]{1,0:T(8,128)S(1)} %shard_map.106.early_ref, f32[256,8]{1,0:T(8,128)S(1)} %get-tuple-element.30.slots_ref, f32[256,8]{1,0:T(8,128)S(1)} %get-tuple-element.31.weights_ref, ...), custom_call_target="tpu_custom_call" | custom-call | tf_op jit(solution)/shard_map/pallas_call | solution.py:63
  58.3 6.1 %collective-permute-start.14 = (bf16[8,768]{1,0:T(8,128)(2,1)S(1)}, bf16[8,768]{1,0:T(8,128)(2,1)S(1)}, u32[]{:S(2)}, u32[]{:S(2)}) collective-permute-start(bf16[8,768]{1,0:T(8,128)(2,1)S(1)} %get-tuple-element.53), channel_id=1, source_target_pairs={{0,8},{8,0},{16,24},{24,16},{32,40},{40,32},{48,56},{56,48},{64,72... | collective-permute-start | bytes 36872 | tf_op jit(solution)/shard_map/ppermute | solution.py:374
  64.4 0.8 collective-permute-done.14
  65.3 16.7 %all_to_all.5 = bf16[16,16,768]{2,1,0:T(8,128)(2,1)S(1)} all-to-all(bf16[16,16,768]{2,1,0:T(8,128)(2,1)S(1)} %broadcast_in_dim.2), channel_id=1, replica_groups={{0,4,16,20,34,38,50,54,64,68,80,84,98,102,114,118},{8,12,24,28,42,46,58..., dimensions={0} | all-to-all | bytes 786432 | tf_op jit(solution)/shard_map/all_to_all | solution.py:383
  82.1 0.6 collective-permute-start.15
  82.7 1.4 %collective-permute-start.16 = (bf16[256,768]{1,0:T(8,128)(2,1)S(1)}, bf16[256,768]{1,0:T(8,128)(2,1)S(1)}, u32[]{:S(2)}, u32[]{:S(2)}) collective-permute-start(bf16[256,768]{1,0:T(8,128)(2,1)S(1)} %bitcast.10), channel_id=1, source_target_pairs={{0,96},{8,104},{16,112},{24,120},{32,0},{40,8},{48,16},{56,24},{64... | collective-permute-start | bytes 1179656 | tf_op jit(solution)/shard_map/ppermute | solution.py:389
  84.1 3.1 %collective-permute-start.18 = (bf16[256,768]{1,0:T(8,128)(2,1)S(1)}, bf16[256,768]{1,0:T(8,128)(2,1)S(1)}, u32[]{:S(2)}, u32[]{:S(2)}) collective-permute-start(bf16[256,768]{1,0:T(8,128)(2,1)S(1)} %bitcast.12), channel_id=1, source_target_pairs={{0,8},{8,0},{16,24},{24,16},{32,40},{40,32},{48,56},{56,48},{64,72... | collective-permute-start | bytes 1179656 | tf_op jit(solution)/shard_map/ppermute | solution.py:393
  87.2 3.4 %collective-permute-done.15 = bf16[256,768]{1,0:T(8,128)(2,1)S(1)} collective-permute-done((bf16[256,768]{1,0:T(8,128)(2,1)S(1)}, bf16[256,768]{1,0:T(8,128)(2,1)S(1)}, u32[]{:S(2)}, u32[]{:S(2)}) %collective-permute-start.15) | collective-permute-done | bytes 393248 | tf_op jit(solution)/shard_map/ppermute | solution.py:388
  90.6 3.0 %collective-permute-start.19 = (bf16[256,768]{1,0:T(8,128)(2,1)S(1)}, bf16[256,768]{1,0:T(8,128)(2,1)S(1)}, u32[]{:S(2)}, u32[]{:S(2)}) collective-permute-start(bf16[256,768]{1,0:T(8,128)(2,1)S(1)} %collective-permute-done.15), channel_id=1, source_target_pairs={{0,8},{8,0},{16,24},{24,16},{32,40},{40,32},{48,56},{56,48},{64,72... | collective-permute-start | bytes 1179656 | tf_op jit(solution)/shard_map/ppermute | solution.py:393
  93.6 0.6 collective-permute-start.20
  94.2 2.6 %collective-permute-start.21 = (bf16[256,768]{1,0:T(8,128)(2,1)S(1)}, bf16[256,768]{1,0:T(8,128)(2,1)S(1)}, u32[]{:S(2)}, u32[]{:S(2)}) collective-permute-start(bf16[256,768]{1,0:T(8,128)(2,1)S(1)} %collective-permute-done.17), channel_id=1, source_target_pairs={{0,8},{8,0},{16,24},{24,16},{32,40},{40,32},{48,56},{56,48},{64,72... | collective-permute-start | bytes 1179656 | tf_op jit(solution)/shard_map/ppermute | solution.py:393
  96.9 0.1 pad_maximum_fusion.mine_ref
  97.0 1.2 %collective-permute-done.21 = bf16[256,768]{1,0:T(8,128)(2,1)S(1)} collective-permute-done((bf16[256,768]{1,0:T(8,128)(2,1)S(1)}, bf16[256,768]{1,0:T(8,128)(2,1)S(1)}, u32[]{:S(2)}, u32[]{:S(2)}) %collective-permute-start.21) | collective-permute-done | bytes 393248 | tf_op jit(solution)/shard_map/ppermute | solution.py:393
  98.2 0.1 pad_maximum_fusion.1.other_ref
  98.3 3.9 %shard_map.109 = (f32[8,768]{1,0:T(8,128)}, f32[8,768]{1,0:T(8,128)}) custom-call(bf16[1024,768]{1,0:T(8,128)(2,1)S(1)} %pad_maximum_fusion.mine_ref, bf16[1024,768]{1,0:T(8,128)(2,1)S(1)} %pad_maximum_fusion.1.other_ref, f32[16,768]{1,0:T(8,128)S(1)} %get-tuple-element.54.embedded_ref), custom_call_target="tpu_custom_call" | custom-call | tf_op jit(solution)/shard_map/pallas_call | solution.py:63
  (29 shorter events, 0.2 us)
Async XLA Ops:
  2.8 8.8 %collective-permute-start = (bf16[128,768]{1,0:T(8,128)(2,1)S(1)}, bf16[128,768]{1,0:T(8,128)(2,1)S(1)}, u32[]{:S(2)}, u32[]{:S(2)}) collective-permute-start(bf16[128,768]{1,0:T(8,128)(2,1)S(1)} %get-tuple-element.33), channel_id=1, source_target_pairs={{0,1},{1,2},{2,3},{3,0},{4,5},{5,6},{6,7},{7,4},{8,9},{9,10},{10,1... | collective-permute-start | bytes 589832 | tf_op jit(solution)/shard_map/ppermute | solution.py:361
  4.9 11.7 %collective-permute-start.1 = (bf16[128,768]{1,0:T(8,128)(2,1)S(1)}, bf16[128,768]{1,0:T(8,128)(2,1)S(1)}, u32[]{:S(2)}, u32[]{:S(2)}) collective-permute-start(bf16[128,768]{1,0:T(8,128)(2,1)S(1)} %get-tuple-element.34), channel_id=1, source_target_pairs={{0,3},{1,0},{2,1},{3,2},{4,7},{5,4},{6,5},{7,6},{8,11},{9,8},{10,9... | collective-permute-start | bytes 589832 | tf_op jit(solution)/shard_map/ppermute | solution.py:361
  6.3 10.3 %collective-permute-start.2 = (bf16[128,768]{1,0:T(8,128)(2,1)S(1)}, bf16[128,768]{1,0:T(8,128)(2,1)S(1)}, u32[]{:S(2)}, u32[]{:S(2)}) collective-permute-start(bf16[128,768]{1,0:T(8,128)(2,1)S(1)} %get-tuple-element.35), channel_id=1, source_target_pairs={{0,4},{1,5},{2,6},{3,7},{4,0},{5,1},{6,2},{7,3},{8,12},{9,13},{10,... | collective-permute-start | bytes 589832 | tf_op jit(solution)/shard_map/ppermute | solution.py:361
  10.0 17.4 %collective-permute-start.6 = (bf16[128,768]{1,0:T(8,128)(2,1)S(1)}, bf16[128,768]{1,0:T(8,128)(2,1)S(1)}, u32[]{:S(2)}, u32[]{:S(2)}) collective-permute-start(bf16[128,768]{1,0:T(8,128)(2,1)S(1)} %get-tuple-element.40), channel_id=1, source_target_pairs={{0,2},{1,3},{2,0},{3,1},{4,6},{5,7},{6,4},{7,5},{8,10},{9,11},{10,... | collective-permute-start | bytes 589832 | tf_op jit(solution)/shard_map/ppermute | solution.py:361
  11.5 15.8 %collective-permute-start.7 = (bf16[128,768]{1,0:T(8,128)(2,1)S(1)}, bf16[128,768]{1,0:T(8,128)(2,1)S(1)}, u32[]{:S(2)}, u32[]{:S(2)}) collective-permute-start(bf16[128,768]{1,0:T(8,128)(2,1)S(1)} %get-tuple-element.41), channel_id=1, source_target_pairs={{0,5},{1,6},{2,7},{3,4},{4,1},{5,2},{6,3},{7,0},{8,13},{9,14},{10,... | collective-permute-start | bytes 589832 | tf_op jit(solution)/shard_map/ppermute | solution.py:361
  11.6 27.9 %collective-permute-start.10 = (bf16[128,768]{1,0:T(8,128)(2,1)S(1)}, bf16[128,768]{1,0:T(8,128)(2,1)S(1)}, u32[]{:S(2)}, u32[]{:S(2)}) collective-permute-start(bf16[128,768]{1,0:T(8,128)(2,1)S(1)} %get-tuple-element.47), channel_id=1, source_target_pairs={{0,7},{1,4},{2,5},{3,6},{4,3},{5,0},{6,1},{7,2},{8,15},{9,12},{10,... | collective-permute-start | bytes 589832 | tf_op jit(solution)/shard_map/ppermute | solution.py:361
  16.6 22.9 %collective-permute-start.11 = (bf16[128,768]{1,0:T(8,128)(2,1)S(1)}, bf16[128,768]{1,0:T(8,128)(2,1)S(1)}, u32[]{:S(2)}, u32[]{:S(2)}) collective-permute-start(bf16[128,768]{1,0:T(8,128)(2,1)S(1)} %get-tuple-element.48), channel_id=1, source_target_pairs={{0,6},{1,7},{2,4},{3,5},{4,2},{5,3},{6,0},{7,1},{8,14},{9,15},{10,... | collective-permute-start | bytes 589832 | tf_op jit(solution)/shard_map/ppermute | solution.py:361
  32.3 12.3 %collective-permute-start.8 = (bf16[128,768]{1,0:T(8,128)(2,1)S(1)}, bf16[128,768]{1,0:T(8,128)(2,1)S(1)}, u32[]{:S(2)}, u32[]{:S(2)}) collective-permute-start(bf16[128,768]{1,0:T(8,128)(2,1)S(1)} %get-tuple-element.45), channel_id=1, source_target_pairs={{2,0},{3,1},{0,2},{1,3},{6,4},{7,5},{4,6},{5,7},{10,8},{11,9},{8,1... | collective-permute-start | bytes 589832 | tf_op jit(solution)/shard_map/ppermute | solution.py:361
  35.1 13.4 %collective-permute-start.9 = (bf16[128,768]{1,0:T(8,128)(2,1)S(1)}, bf16[128,768]{1,0:T(8,128)(2,1)S(1)}, u32[]{:S(2)}, u32[]{:S(2)}) collective-permute-start(bf16[128,768]{1,0:T(8,128)(2,1)S(1)} %get-tuple-element.46), channel_id=1, source_target_pairs={{5,0},{6,1},{7,2},{4,3},{1,4},{2,5},{3,6},{0,7},{13,8},{14,9},{15,... | collective-permute-start | bytes 589832 | tf_op jit(solution)/shard_map/ppermute | solution.py:361
  37.4 13.4 %collective-permute-start.3 = (bf16[128,768]{1,0:T(8,128)(2,1)S(1)}, bf16[128,768]{1,0:T(8,128)(2,1)S(1)}, u32[]{:S(2)}, u32[]{:S(2)}) collective-permute-start(bf16[128,768]{1,0:T(8,128)(2,1)S(1)} %get-tuple-element.37), channel_id=1, source_target_pairs={{1,0},{2,1},{3,2},{0,3},{5,4},{6,5},{7,6},{4,7},{9,8},{10,9},{11,1... | collective-permute-start | bytes 589832 | tf_op jit(solution)/shard_map/ppermute | solution.py:361
  39.5 11.3 %collective-permute-start.4 = (bf16[128,768]{1,0:T(8,128)(2,1)S(1)}, bf16[128,768]{1,0:T(8,128)(2,1)S(1)}, u32[]{:S(2)}, u32[]{:S(2)}) collective-permute-start(bf16[128,768]{1,0:T(8,128)(2,1)S(1)} %get-tuple-element.38), channel_id=1, source_target_pairs={{3,0},{0,1},{1,2},{2,3},{7,4},{4,5},{5,6},{6,7},{11,8},{8,9},{9,10... | collective-permute-start | bytes 589832 | tf_op jit(solution)/shard_map/ppermute | solution.py:361
  39.5 11.3 %copy-start = (bf16[256,768]{1,0:T(8,128)(2,1)S(1)}, bf16[256,768]{1,0:T(8,128)(2,1)}, u32[]{:S(2)}) copy-start(bf16[256,768]{1,0:T(8,128)(2,1)} %tokens_ref.1) | copy-start | bytes 1179652
  39.5 17.4 %copy-start.1 = (s32[1,16]{1,0:T(1,128)S(1)}, s32[1,16]{1,0:T(1,128)}, u32[]{:S(2)}) copy-start(s32[1,16]{1,0:T(1,128)} %lengths_ref.1) | copy-start | bytes 196
  39.5 11.3 %collective-permute-start.5 = (bf16[128,768]{1,0:T(8,128)(2,1)S(1)}, bf16[128,768]{1,0:T(8,128)(2,1)S(1)}, u32[]{:S(2)}, u32[]{:S(2)}) collective-permute-start(bf16[128,768]{1,0:T(8,128)(2,1)S(1)} %get-tuple-element.39), channel_id=1, source_target_pairs={{4,0},{5,1},{6,2},{7,3},{0,4},{1,5},{2,6},{3,7},{12,8},{13,9},{14,... | collective-permute-start | bytes 589832 | tf_op jit(solution)/shard_map/ppermute | solution.py:361
  44.6 8.4 %collective-permute-start.12 = (bf16[128,768]{1,0:T(8,128)(2,1)S(1)}, bf16[128,768]{1,0:T(8,128)(2,1)S(1)}, u32[]{:S(2)}, u32[]{:S(2)}) collective-permute-start(bf16[128,768]{1,0:T(8,128)(2,1)S(1)} %get-tuple-element.49), channel_id=1, source_target_pairs={{7,0},{4,1},{5,2},{6,3},{3,4},{0,5},{1,6},{2,7},{15,8},{12,9},{13,... | collective-permute-start | bytes 589832 | tf_op jit(solution)/shard_map/ppermute | solution.py:361
  48.5 8.4 %collective-permute-start.13 = (bf16[128,768]{1,0:T(8,128)(2,1)S(1)}, bf16[128,768]{1,0:T(8,128)(2,1)S(1)}, u32[]{:S(2)}, u32[]{:S(2)}) collective-permute-start(bf16[128,768]{1,0:T(8,128)(2,1)S(1)} %get-tuple-element.50), channel_id=1, source_target_pairs={{6,0},{7,1},{4,2},{5,3},{2,4},{3,5},{0,6},{1,7},{14,8},{15,9},{12,... | collective-permute-start | bytes 589832 | tf_op jit(solution)/shard_map/ppermute | solution.py:361
  58.3 7.0 %collective-permute-start.14 = (bf16[8,768]{1,0:T(8,128)(2,1)S(1)}, bf16[8,768]{1,0:T(8,128)(2,1)S(1)}, u32[]{:S(2)}, u32[]{:S(2)}) collective-permute-start(bf16[8,768]{1,0:T(8,128)(2,1)S(1)} %get-tuple-element.53), channel_id=1, source_target_pairs={{0,8},{8,0},{16,24},{24,16},{32,40},{40,32},{48,56},{56,48},{64,72... | collective-permute-start | bytes 36872 | tf_op jit(solution)/shard_map/ppermute | solution.py:374
  82.1 8.5 %collective-permute-start.15 = (bf16[256,768]{1,0:T(8,128)(2,1)S(1)}, bf16[256,768]{1,0:T(8,128)(2,1)S(1)}, u32[]{:S(2)}, u32[]{:S(2)}) collective-permute-start(bf16[256,768]{1,0:T(8,128)(2,1)S(1)} %bitcast.9), channel_id=1, source_target_pairs={{0,3},{1,0},{2,1},{3,2},{4,7},{5,4},{6,5},{7,6},{8,11},{9,8},{10,9... | collective-permute-start | bytes 1179656 | tf_op jit(solution)/shard_map/ppermute | solution.py:388
  82.7 10.9 %collective-permute-start.16 = (bf16[256,768]{1,0:T(8,128)(2,1)S(1)}, bf16[256,768]{1,0:T(8,128)(2,1)S(1)}, u32[]{:S(2)}, u32[]{:S(2)}) collective-permute-start(bf16[256,768]{1,0:T(8,128)(2,1)S(1)} %bitcast.10), channel_id=1, source_target_pairs={{0,96},{8,104},{16,112},{24,120},{32,0},{40,8},{48,16},{56,24},{64... | collective-permute-start | bytes 1179656 | tf_op jit(solution)/shard_map/ppermute | solution.py:389
  84.1 10.1 %collective-permute-start.17 = (bf16[256,768]{1,0:T(8,128)(2,1)S(1)}, bf16[256,768]{1,0:T(8,128)(2,1)S(1)}, u32[]{:S(2)}, u32[]{:S(2)}) collective-permute-start(bf16[256,768]{1,0:T(8,128)(2,1)S(1)} %bitcast.11), channel_id=1, source_target_pairs={{0,1},{1,2},{2,3},{3,0},{4,5},{5,6},{6,7},{7,4},{8,9},{9,10},{10,1... | collective-permute-start | bytes 1179656 | tf_op jit(solution)/shard_map/ppermute | solution.py:390
  84.1 12.8 %collective-permute-start.18 = (bf16[256,768]{1,0:T(8,128)(2,1)S(1)}, bf16[256,768]{1,0:T(8,128)(2,1)S(1)}, u32[]{:S(2)}, u32[]{:S(2)}) collective-permute-start(bf16[256,768]{1,0:T(8,128)(2,1)S(1)} %bitcast.12), channel_id=1, source_target_pairs={{0,8},{8,0},{16,24},{24,16},{32,40},{40,32},{48,56},{56,48},{64,72... | collective-permute-start | bytes 1179656 | tf_op jit(solution)/shard_map/ppermute | solution.py:393
  90.6 6.4 %collective-permute-start.19 = (bf16[256,768]{1,0:T(8,128)(2,1)S(1)}, bf16[256,768]{1,0:T(8,128)(2,1)S(1)}, u32[]{:S(2)}, u32[]{:S(2)}) collective-permute-start(bf16[256,768]{1,0:T(8,128)(2,1)S(1)} %collective-permute-done.15), channel_id=1, source_target_pairs={{0,8},{8,0},{16,24},{24,16},{32,40},{40,32},{48,56},{56,48},{64,72... | collective-permute-start | bytes 1179656 | tf_op jit(solution)/shard_map/ppermute | solution.py:393
  93.6 3.4 %collective-permute-start.20 = (bf16[256,768]{1,0:T(8,128)(2,1)S(1)}, bf16[256,768]{1,0:T(8,128)(2,1)S(1)}, u32[]{:S(2)}, u32[]{:S(2)}) collective-permute-start(bf16[256,768]{1,0:T(8,128)(2,1)S(1)} %collective-permute-done.16), channel_id=1, source_target_pairs={{0,8},{8,0},{16,24},{24,16},{32,40},{40,32},{48,56},{56,48},{64,72... | collective-permute-start | bytes 1179656 | tf_op jit(solution)/shard_map/ppermute | solution.py:393
  94.2 4.0 %collective-permute-start.21 = (bf16[256,768]{1,0:T(8,128)(2,1)S(1)}, bf16[256,768]{1,0:T(8,128)(2,1)S(1)}, u32[]{:S(2)}, u32[]{:S(2)}) collective-permute-start(bf16[256,768]{1,0:T(8,128)(2,1)S(1)} %collective-permute-done.17), channel_id=1, source_target_pairs={{0,8},{8,0},{16,24},{24,16},{32,40},{40,32},{48,56},{56,48},{64,72... | collective-permute-start | bytes 1179656 | tf_op jit(solution)/shard_map/ppermute | solution.py:393

commit v8 on v7

--- a/solution.py
+++ b/solution.py
@@ -240,7 +240,7 @@
 
 
 def combine_kernel(early_ref, slots_ref, weights_ref, lengths_ref, *refs):
-    *back_refs, hidden_ref, embedded_ref, kept_ref, given_ref = refs
+    *back_refs, hidden_ref, embedded_ref, rounded_ref = refs
     rows = early_ref.shape[0]
     start = slots_ref.shape[1] - len(back_refs)
     mixed = early_ref[...] + weighted_rows(slots_ref, weights_ref, back_refs, start)
@@ -257,13 +257,12 @@
     pooled = (dot(member, first) + dot(member, second) + dot(member, third)) / sizes
     embedded = pooled * lax.rsqrt(jnp.sum(pooled * pooled, axis=-1, keepdims=True) + pool_eps)
     embedded_ref[...] = embedded
-    queries, documents = embedded[: count // 2], embedded[count // 2 :]
-    first_core = lax.axis_index("dp") % 2 == 0
-    kept_ref[...] = jnp.where(first_core, queries, documents).astype(bf16)
-    given_ref[...] = jnp.where(first_core, documents, queries).astype(bf16)
-
-
-def gradients(queries_ref, docs_ref, embedded_ref, first, query_grad_ref, doc_grad_ref):
+    rounded_ref[...] = embedded.astype(bf16)
+
+
+def gradient_kernel(queries_ref, docs_ref, embedded_ref, query_grad_ref, doc_grad_ref):
+    rank = lax.axis_index("dp") // 2 * (lax.axis_size("expert") // plane) + lax.axis_index("expert") // plane
+    first = rank * (embedded_ref.shape[0] // 2)
     embedded = embedded_ref[...]
     count = embedded.shape[0] // 2
     total = queries_ref.shape[0]
@@ -289,21 +288,6 @@
     doc_grad_ref[...] = logit_scale * (fold(dot(likely, all_queries))[count:] + diagonal * queries)
 
 
-def gradient_kernel(mine_ref, other_ref, embedded_ref, query_grad_ref, doc_grad_ref):
-    dp = lax.axis_index("dp")
-    core = dp % 2
-    rank = dp // 2 * (lax.axis_size("expert") // plane) + lax.axis_index("expert") // plane
-    first = (rank * 2 + core) * (embedded_ref.shape[0] // 2)
-
-    @pl.when(core == 0)
-    def _():
-        gradients(mine_ref, other_ref, embedded_ref, first, query_grad_ref, doc_grad_ref)
-
-    @pl.when(core == 1)
-    def _():
-        gradients(other_ref, mine_ref, embedded_ref, first, query_grad_ref, doc_grad_ref)
-
-
 def route(tokens, routes, norm_gain, router_weight):
     rows, width = tokens.shape
     experts = router_weight.shape[1]
@@ -324,7 +308,6 @@
 
 def combine(tokens, slots, weights, backs, lengths):
     count, width = lengths.shape[1], tokens.shape[1]
-    half = jax.ShapeDtypeStruct((count // 2, width), bf16)
     early = len(backs) - len(move_groups[-1])
     mixed = call(
         early_combine_kernel,
@@ -336,16 +319,15 @@
         [
             jax.ShapeDtypeStruct(tokens.shape, bf16),
             jax.ShapeDtypeStruct((count, width), f32),
-            half,
-            half,
+            jax.ShapeDtypeStruct((count, width), bf16),
         ],
         mixed, slots, weights, lengths, *backs[early:],
     )
 
 
-def info_nce(mine, other, embedded):
+def info_nce(queries, docs, embedded):
     out = jax.ShapeDtypeStruct((embedded.shape[0] // 2, embedded.shape[1]), f32)
-    return call(gradient_kernel, [out, out], mine, other, embedded)
+    return call(gradient_kernel, [out, out], queries, docs, embedded)
 
 
 def body(tokens, routes, lengths, norm_gain, router_weight, gate_weight, up_weight, down_weight):
@@ -366,32 +348,29 @@
     for at, group in enumerate(move_groups):
         results, matrices = expert_rows([incoming[move] for move in group], matrices, at == 0)
         backs += [send(x, move, back=True) for move, x in zip(group, results)]
-    hidden_out, embedded, kept, given = combine(tokens, slots, weights, backs, lengths)
+    hidden_out, embedded, rounded = combine(tokens, slots, weights, backs, lengths)
 
     groups = lax.axis_size("dp")
     swap = [(i, i ^ 1) for i in range(groups)]
-    core = lax.axis_index("dp") % 2
-    taken = lax.ppermute(given, "dp", swap)
-    shard = jnp.concatenate(
-        [jnp.where(core == 0, kept, taken), jnp.where(core == 0, taken, kept)]
-    )
     colours = [[] for _ in range(2 * plane)]
     for device in range(groups * experts):
         dp, expert = divmod(device, experts)
         colours[(expert + 2 * (dp // line)) % plane * 2 + dp % 2].append(device)
-    copies = jnp.broadcast_to(shard[None], (len(colours[0]),) + shard.shape)
+    copies = jnp.broadcast_to(rounded[None], (len(colours[0]),) + rounded.shape)
     own = lax.all_to_all(
         copies, ("dp", "expert"), split_axis=0, concat_axis=0, tiled=True, axis_index_groups=colours
-    ).reshape(-1, width)
+    )
     blocks = [
         own,
         lax.ppermute(own, "expert", pairs((3, 0), False)),
         lax.ppermute(own, "dp", [(i, (i - line) % groups) for i in range(groups)]),
         lax.ppermute(own, "expert", pairs((1, 0), False)),
     ]
-    mine = jnp.concatenate(blocks)
-    other = jnp.concatenate([lax.ppermute(x, "dp", swap) for x in blocks])
-    query_grad, doc_grad = info_nce(mine, other, embedded)
+    blocks += [lax.ppermute(x, "dp", swap) for x in blocks]
+    half = rounded.shape[0] // 2
+    queries = jnp.concatenate([x[:, :half] for x in blocks]).reshape(-1, width)
+    docs = jnp.concatenate([x[:, half:] for x in blocks]).reshape(-1, width)
+    query_grad, doc_grad = info_nce(queries, docs, embedded)
     return (hidden_out, query_grad, doc_grad)
 
 

time: 102 us -> 98.8 us (0.969)
  waiting for transfers between devices: 10.3 us -> 6.63 us
  blocking collectives: 16.7 us -> 18.6 us
  starting transfers between devices: 44.8 us -> 42.9 us
    ppermute x1, waiting for transfers between devices: 3.37 us -> 0.01 us  [body(): lax.ppermute(own, 'expert', pairs((3, 0), False))]
    ppermute x5 -> x4, starting transfers between devices: 15.5 us -> 13 us  [body(): blocks += [lax.ppermute(x, 'dp', swap) for x in blocks]]
    ppermute x1, starting transfers between devices: 0.62 us -> 2.67 us  [body(): lax.ppermute(own, 'expert', pairs((3, 0), False))]
    all_to_all x1, blocking collectives: 16.7 us -> 18.6 us  [body(): lax.all_to_all(copies, ('dp', 'expert'), split_axis=0, concat_axis=0, til...]
    ppermute x1, starting transfers between devices: 1.43 us -> 0.01 us  [body(): lax.ppermute(own, 'dp', [(i, (i - line) % groups) for i in range(groups)])]
    ppermute x5 -> x4, waiting for transfers between devices: 2.05 us -> 1.81 us  [body(): blocks += [lax.ppermute(x, 'dp', swap) for x in blocks]]
  transfers between devices with their start and end apart: 22 -> 21, of which waited for: 5 -> 3; matrix products, arithmetic and copies ran while one was open for 0% -> 0% of each run, Pallas kernels for 21% -> 22%
where the time goes in v8:
time: 98.8 us; the launch traced here: 98.6 us
  starting transfers between devices  42.9 us (43%)
  Pallas kernels  29.3 us (30%)
  blocking collectives  18.6 us (19%)
  waiting for transfers between devices  6.63 us (7%)
    pallas_call x7, Pallas kernels, call(): pl.pallas_call(kernel, out_shape=outs, in_specs=[left if at in outside el...  29.3 us
    ppermute x14, starting transfers between devices, send(): return x if move == (0, 0) else lax.ppermute(x, 'expert', pairs(move, back))  27.3 us
    all_to_all x1, blocking collectives, body(): lax.all_to_all(copies, ('dp', 'expert'), split_axis=0, concat_axis=0, til...  18.6 us
    ppermute x4, starting transfers between devices, body(): blocks += [lax.ppermute(x, 'dp', swap) for x in blocks]  13 us
    ppermute x14, waiting for transfers between devices, send(): return x if move == (0, 0) else lax.ppermute(x, 'expert', pairs(move, back))  4.81 us
    ppermute x1, starting transfers between devices, body(): lax.ppermute(own, 'expert', pairs((3, 0), False))  2.67 us
  transfers between devices with their start and end apart: 21, of which 3 were waited for; matrix products, arithmetic and copies ran while one was open for 0% of the time, Pallas kernels for 22%

profile of v8, /device:TPU:1, one launch (start us, length us, event | category | flops | bytes accessed | tf_op | source)
XLA Modules:
  0.0 98.6 jit_solution(17609003989001520916)
XLA Ops:
  0.6 2.2 %shard_map.103 = (bf16[128,768]{1,0:T(8,128)(2,1)S(1)}, bf16[128,768]{1,0:T(8,128)(2,1)S(1)}, bf16[128,768]{1,0:T(8,128)(2,1)S(1)}, bf16[128,768]{1,0:T(8,128)(2...) custom-call(bf16[256,768]{1,0:T(8,128)(2,1)} %tokens_ref.1, ...), custom_call_target="tpu_custom_call" | custom-call | tf_op jit(solution)/shard_map/pallas_call | solution.py:63
  2.8 2.1 %collective-permute-start = (bf16[128,768]{1,0:T(8,128)(2,1)S(1)}, bf16[128,768]{1,0:T(8,128)(2,1)S(1)}, u32[]{:S(2)}, u32[]{:S(2)}) collective-permute-start(bf16[128,768]{1,0:T(8,128)(2,1)S(1)} %get-tuple-element.32), channel_id=1, source_target_pairs={{0,1},{1,2},{2,3},{3,0},{4,5},{5,6},{6,7},{7,4},{8,9},{9,10},{10,1... | collective-permute-start | bytes 589832 | tf_op jit(solution)/shard_map/ppermute | solution.py:343
  4.9 1.4 %collective-permute-start.1 = (bf16[128,768]{1,0:T(8,128)(2,1)S(1)}, bf16[128,768]{1,0:T(8,128)(2,1)S(1)}, u32[]{:S(2)}, u32[]{:S(2)}) collective-permute-start(bf16[128,768]{1,0:T(8,128)(2,1)S(1)} %get-tuple-element.33), channel_id=1, source_target_pairs={{0,3},{1,0},{2,1},{3,2},{4,7},{5,4},{6,5},{7,6},{8,11},{9,8},{10,9... | collective-permute-start | bytes 589832 | tf_op jit(solution)/shard_map/ppermute | solution.py:343
  6.3 3.7 %collective-permute-start.2 = (bf16[128,768]{1,0:T(8,128)(2,1)S(1)}, bf16[128,768]{1,0:T(8,128)(2,1)S(1)}, u32[]{:S(2)}, u32[]{:S(2)}) collective-permute-start(bf16[128,768]{1,0:T(8,128)(2,1)S(1)} %get-tuple-element.34), channel_id=1, source_target_pairs={{0,4},{1,5},{2,6},{3,7},{4,0},{5,1},{6,2},{7,3},{8,12},{9,13},{10,... | collective-permute-start | bytes 589832 | tf_op jit(solution)/shard_map/ppermute | solution.py:343
  10.0 1.5 %collective-permute-start.6 = (bf16[128,768]{1,0:T(8,128)(2,1)S(1)}, bf16[128,768]{1,0:T(8,128)(2,1)S(1)}, u32[]{:S(2)}, u32[]{:S(2)}) collective-permute-start(bf16[128,768]{1,0:T(8,128)(2,1)S(1)} %get-tuple-element.39), channel_id=1, source_target_pairs={{0,2},{1,3},{2,0},{3,1},{4,6},{5,7},{6,4},{7,5},{8,10},{9,11},{10,... | collective-permute-start | bytes 589832 | tf_op jit(solution)/shard_map/ppermute | solution.py:343
  11.5 0.0 collective-permute-start.7
  11.6 5.0 %collective-permute-start.10 = (bf16[128,768]{1,0:T(8,128)(2,1)S(1)}, bf16[128,768]{1,0:T(8,128)(2,1)S(1)}, u32[]{:S(2)}, u32[]{:S(2)}) collective-permute-start(bf16[128,768]{1,0:T(8,128)(2,1)S(1)} %get-tuple-element.46), channel_id=1, source_target_pairs={{0,7},{1,4},{2,5},{3,6},{4,3},{5,0},{6,1},{7,2},{8,15},{9,12},{10,... | collective-permute-start | bytes 589832 | tf_op jit(solution)/shard_map/ppermute | solution.py:343
  16.6 0.0 collective-permute-done.1.refs_2_
  16.6 0.0 collective-permute-start.11
  16.6 10.7 %shard_map.104 = (bf16[128,768]{1,0:T(8,128)(2,1)S(1)}, bf16[128,768]{1,0:T(8,128)(2,1)S(1)}, bf16[128,768]{1,0:T(8,128)(2,1)S(1)}, bf16[128,768]{1,0:T(8,128)(2...) custom-call(bf16[128,768]{1,0:T(8,128)(2,1)S(1)} %get-tuple-element.31.refs_0_,, ...), custom_call_target="tpu_custom_call" | custom-call | tf_op jit(solution)/shard_map/pallas_call | solution.py:63
  27.4 5.0 %shard_map.105 = (bf16[128,768]{1,0:T(8,128)(2,1)S(1)}, bf16[128,768]{1,0:T(8,128)(2,1)S(1)}) custom-call(bf16[128,768]{1,0:T(8,128)(2,1)S(1)} %collective-permute-done.6.refs_0_, bf16[128,768]{1,0:T(8,128)(2,1)S(1)} %collective-permute-done.7.refs_1_, bf16[768,3072]{1,0:T(8,128)(2,1)S(1)} %get-tuple-element.41.refs_2_, ...), custom_call_target="tpu_custom_call" | custom-call | tf_op jit(solution)/shard_map/pallas_call | solution.py:63
  32.3 2.8 %collective-permute-start.8 = (bf16[128,768]{1,0:T(8,128)(2,1)S(1)}, bf16[128,768]{1,0:T(8,128)(2,1)S(1)}, u32[]{:S(2)}, u32[]{:S(2)}) collective-permute-start(bf16[128,768]{1,0:T(8,128)(2,1)S(1)} %get-tuple-element.44), channel_id=1, source_target_pairs={{2,0},{3,1},{0,2},{1,3},{6,4},{7,5},{4,6},{5,7},{10,8},{11,9},{8,1... | collective-permute-start | bytes 589832 | tf_op jit(solution)/shard_map/ppermute | solution.py:343
  35.1 2.3 %collective-permute-start.9 = (bf16[128,768]{1,0:T(8,128)(2,1)S(1)}, bf16[128,768]{1,0:T(8,128)(2,1)S(1)}, u32[]{:S(2)}, u32[]{:S(2)}) collective-permute-start(bf16[128,768]{1,0:T(8,128)(2,1)S(1)} %get-tuple-element.45), channel_id=1, source_target_pairs={{5,0},{6,1},{7,2},{4,3},{1,4},{2,5},{3,6},{0,7},{13,8},{14,9},{15,... | collective-permute-start | bytes 589832 | tf_op jit(solution)/shard_map/ppermute | solution.py:343
  37.4 2.1 %collective-permute-start.3 = (bf16[128,768]{1,0:T(8,128)(2,1)S(1)}, bf16[128,768]{1,0:T(8,128)(2,1)S(1)}, u32[]{:S(2)}, u32[]{:S(2)}) collective-permute-start(bf16[128,768]{1,0:T(8,128)(2,1)S(1)} %get-tuple-element.36), channel_id=1, source_target_pairs={{1,0},{2,1},{3,2},{0,3},{5,4},{6,5},{7,6},{4,7},{9,8},{10,9},{11,1... | collective-permute-start | bytes 589832 | tf_op jit(solution)/shard_map/ppermute | solution.py:343
  39.5 0.0 copy-start
  39.5 0.1 collective-permute-start.5
  39.6 5.0 %shard_map.107 = (bf16[128,768]{1,0:T(8,128)(2,1)S(1)}, bf16[128,768]{1,0:T(8,128)(2,1)S(1)}) custom-call(bf16[128,768]{1,0:T(8,128)(2,1)S(1)} %collective-permute-done.10.refs_0_, bf16[128,768]{1,0:T(8,128)(2,1)S(1)} %collective-permute-done.11.refs_1_, bf16[768,3072]{1,0:T(8,128)(2,1)S(1)} %get-tuple-element.41.refs_2_, ...), custom_call_target="tpu_custom_call" | custom-call | tf_op jit(solution)/shard_map/pallas_call | solution.py:63
  44.6 0.0 copy-start.1
  44.6 3.8 %collective-permute-start.12 = (bf16[128,768]{1,0:T(8,128)(2,1)S(1)}, bf16[128,768]{1,0:T(8,128)(2,1)S(1)}, u32[]{:S(2)}, u32[]{:S(2)}) collective-permute-start(bf16[128,768]{1,0:T(8,128)(2,1)S(1)} %get-tuple-element.48), channel_id=1, source_target_pairs={{7,0},{4,1},{5,2},{6,3},{3,4},{0,5},{1,6},{2,7},{15,8},{12,9},{13,... | collective-permute-start | bytes 589832 | tf_op jit(solution)/shard_map/ppermute | solution.py:343
  48.5 2.4 %collective-permute-start.13 = (bf16[128,768]{1,0:T(8,128)(2,1)S(1)}, bf16[128,768]{1,0:T(8,128)(2,1)S(1)}, u32[]{:S(2)}, u32[]{:S(2)}) collective-permute-start(bf16[128,768]{1,0:T(8,128)(2,1)S(1)} %get-tuple-element.49), channel_id=1, source_target_pairs={{6,0},{7,1},{4,2},{5,3},{2,4},{3,5},{0,6},{1,7},{14,8},{15,9},{12,... | collective-permute-start | bytes 589832 | tf_op jit(solution)/shard_map/ppermute | solution.py:343
  50.9 1.2 %shard_map.106.early_ref = f32[256,768]{1,0:T(8,128)S(1)} custom-call(bf16[256,768]{1,0:T(8,128)(2,1)S(1)} %copy-done, f32[256,8]{1,0:T(8,128)S(1)} %get-tuple-element.29.slots_ref, f32[256,8]{1,0:T(8,128)S(1)} %get-tuple-element.30.weights_ref, bf16[128,768]{1,0:T(8,128)(2,1)S(1)} %get-tuple-element.35.refs_0_, ...), custom_call_target="tpu_custom_call" | custom-call | tf_op jit(solution)/shard_map/pallas_call | solution.py:63
  52.1 0.8 collective-permute-done.12.refs_0_
  53.0 3.9 %collective-permute-done.13.refs_1_ = bf16[128,768]{1,0:T(8,128)(2,1)S(1)} collective-permute-done((bf16[128,768]{1,0:T(8,128)(2,1)S(1)}, bf16[128,768]{1,0:T(8,128)(2,1)S(1)}, u32[]{:S(2)}, u32[]{:S(2)}) %collective-permute-start.13) | collective-permute-done | bytes 196640 | tf_op jit(solution)/shard_map/ppermute | solution.py:343
  56.9 1.4 %shard_map.108 = (bf16[256,768]{1,0:T(8,128)(2,1)}, f32[16,768]{1,0:T(8,128)S(1)}, bf16[16,768]{1,0:T(8,128)(2,1)S(1)}) custom-call(f32[256,768]{1,0:T(8,128)S(1)} %shard_map.106.early_ref, f32[256,8]{1,0:T(8,128)S(1)} %get-tuple-element.29.slots_ref, f32[256,8]{1,0:T(8,128)S(1)} %get-tuple-element.30.weights_ref, s32[1,16]{1,0:T(1,128)S(1)} %copy-done.1, ...), custom_call_target="tpu_custom_call" | custom-call | tf_op jit(solution)/shard_map/pallas_call | solution.py:63
  58.3 18.6 %all_to_all.5 = bf16[16,16,768]{2,1,0:T(8,128)(2,1)S(1)} all-to-all(bf16[16,16,768]{2,1,0:T(8,128)(2,1)S(1)} %broadcast_in_dim.2), channel_id=1, replica_groups={{0,4,16,20,34,38,50,54,64,68,80,84,98,102,114,118},{8,12,24,28,42,46,58..., dimensions={0} | all-to-all | bytes 786432 | tf_op jit(solution)/shard_map/all_to_all | solution.py:360
  77.0 2.7 %collective-permute-start.14 = (bf16[16,16,768]{2,1,0:T(8,128)(2,1)S(1)}, bf16[16,16,768]{2,1,0:T(8,128)(2,1)S(1)}, u32[]{:S(2)}, u32[]{:S(2)}) collective-permute-start(bf16[16,16,768]{2,1,0:T(8,128)(2,1)S(1)} %all_to_all.5), channel_id=1, source_target_pairs={{0,3},{1,0},{2,1},{3,2},{4,7},{5,4},{6,5},{7,6},{8,11},{9,8},{10,9... | collective-permute-start | bytes 1179656 | tf_op jit(solution)/shard_map/ppermute | solution.py:365
  79.6 6.7 %collective-permute-start.17 = (bf16[16,16,768]{2,1,0:T(8,128)(2,1)S(1)}, bf16[16,16,768]{2,1,0:T(8,128)(2,1)S(1)}, u32[]{:S(2)}, u32[]{:S(2)}) collective-permute-start(bf16[16,16,768]{2,1,0:T(8,128)(2,1)S(1)} %all_to_all.5), channel_id=1, source_target_pairs={{0,8},{8,0},{16,24},{24,16},{32,40},{40,32},{48,56},{56,48},{64,72... | collective-permute-start | bytes 1179656 | tf_op jit(solution)/shard_map/ppermute | solution.py:369
  86.4 5.7 %collective-permute-start.20 = (bf16[16,16,768]{2,1,0:T(8,128)(2,1)S(1)}, bf16[16,16,768]{2,1,0:T(8,128)(2,1)S(1)}, u32[]{:S(2)}, u32[]{:S(2)}) collective-permute-start(bf16[16,16,768]{2,1,0:T(8,128)(2,1)S(1)} %collective-permute-done.16), channel_id=1, source_target_pairs={{0,8},{8,0},{16,24},{24,16},{32,40},{40,32},{48,56},{56,48},{64,72... | collective-permute-start | bytes 1179656 | tf_op jit(solution)/shard_map/ppermute | solution.py:369
  92.1 0.0 collective-permute-start.19
  92.2 0.5 collective-permute-start.18
  92.8 1.8 %collective-permute-done.18 = bf16[16,16,768]{2,1,0:T(8,128)(2,1)S(1)} collective-permute-done((bf16[16,16,768]{2,1,0:T(8,128)(2,1)S(1)}, bf16[16,16,768]{2,1,0:T(8,128)(2,1)S(1)}, u32[]{:S(2)}, u32[]{:S(2)}) %collective-permute-start.18) | collective-permute-done | bytes 393248 | tf_op jit(solution)/shard_map/ppermute | solution.py:369
  94.7 3.8 %shard_map.109 = (f32[8,768]{1,0:T(8,128)}, f32[8,768]{1,0:T(8,128)}) custom-call(bf16[1024,768]{1,0:T(8,128)(2,1)S(1)} %bitcast.8, bf16[1024,768]{1,0:T(8,128)(2,1)S(1)} %bitcast.7, f32[16,768]{1,0:T(8,128)S(1)} %get-tuple-element.52.embedded_ref), custom_call_target="tpu_custom_call" | custom-call | tf_op jit(solution)/shard_map/pallas_call | solution.py:63
  (31 shorter events, 0.3 us)
Async XLA Ops:
  2.8 8.8 %collective-permute-start = (bf16[128,768]{1,0:T(8,128)(2,1)S(1)}, bf16[128,768]{1,0:T(8,128)(2,1)S(1)}, u32[]{:S(2)}, u32[]{:S(2)}) collective-permute-start(bf16[128,768]{1,0:T(8,128)(2,1)S(1)} %get-tuple-element.32), channel_id=1, source_target_pairs={{0,1},{1,2},{2,3},{3,0},{4,5},{5,6},{6,7},{7,4},{8,9},{9,10},{10,1... | collective-permute-start | bytes 589832 | tf_op jit(solution)/shard_map/ppermute | solution.py:343
  4.9 11.7 %collective-permute-start.1 = (bf16[128,768]{1,0:T(8,128)(2,1)S(1)}, bf16[128,768]{1,0:T(8,128)(2,1)S(1)}, u32[]{:S(2)}, u32[]{:S(2)}) collective-permute-start(bf16[128,768]{1,0:T(8,128)(2,1)S(1)} %get-tuple-element.33), channel_id=1, source_target_pairs={{0,3},{1,0},{2,1},{3,2},{4,7},{5,4},{6,5},{7,6},{8,11},{9,8},{10,9... | collective-permute-start | bytes 589832 | tf_op jit(solution)/shard_map/ppermute | solution.py:343
  6.3 10.3 %collective-permute-start.2 = (bf16[128,768]{1,0:T(8,128)(2,1)S(1)}, bf16[128,768]{1,0:T(8,128)(2,1)S(1)}, u32[]{:S(2)}, u32[]{:S(2)}) collective-permute-start(bf16[128,768]{1,0:T(8,128)(2,1)S(1)} %get-tuple-element.34), channel_id=1, source_target_pairs={{0,4},{1,5},{2,6},{3,7},{4,0},{5,1},{6,2},{7,3},{8,12},{9,13},{10,... | collective-permute-start | bytes 589832 | tf_op jit(solution)/shard_map/ppermute | solution.py:343
  10.0 17.4 %collective-permute-start.6 = (bf16[128,768]{1,0:T(8,128)(2,1)S(1)}, bf16[128,768]{1,0:T(8,128)(2,1)S(1)}, u32[]{:S(2)}, u32[]{:S(2)}) collective-permute-start(bf16[128,768]{1,0:T(8,128)(2,1)S(1)} %get-tuple-element.39), channel_id=1, source_target_pairs={{0,2},{1,3},{2,0},{3,1},{4,6},{5,7},{6,4},{7,5},{8,10},{9,11},{10,... | collective-permute-start | bytes 589832 | tf_op jit(solution)/shard_map/ppermute | solution.py:343
  11.5 15.8 %collective-permute-start.7 = (bf16[128,768]{1,0:T(8,128)(2,1)S(1)}, bf16[128,768]{1,0:T(8,128)(2,1)S(1)}, u32[]{:S(2)}, u32[]{:S(2)}) collective-permute-start(bf16[128,768]{1,0:T(8,128)(2,1)S(1)} %get-tuple-element.40), channel_id=1, source_target_pairs={{0,5},{1,6},{2,7},{3,4},{4,1},{5,2},{6,3},{7,0},{8,13},{9,14},{10,... | collective-permute-start | bytes 589832 | tf_op jit(solution)/shard_map/ppermute | solution.py:343
  11.6 27.9 %collective-permute-start.10 = (bf16[128,768]{1,0:T(8,128)(2,1)S(1)}, bf16[128,768]{1,0:T(8,128)(2,1)S(1)}, u32[]{:S(2)}, u32[]{:S(2)}) collective-permute-start(bf16[128,768]{1,0:T(8,128)(2,1)S(1)} %get-tuple-element.46), channel_id=1, source_target_pairs={{0,7},{1,4},{2,5},{3,6},{4,3},{5,0},{6,1},{7,2},{8,15},{9,12},{10,... | collective-permute-start | bytes 589832 | tf_op jit(solution)/shard_map/ppermute | solution.py:343
  16.6 22.9 %collective-permute-start.11 = (bf16[128,768]{1,0:T(8,128)(2,1)S(1)}, bf16[128,768]{1,0:T(8,128)(2,1)S(1)}, u32[]{:S(2)}, u32[]{:S(2)}) collective-permute-start(bf16[128,768]{1,0:T(8,128)(2,1)S(1)} %get-tuple-element.47), channel_id=1, source_target_pairs={{0,6},{1,7},{2,4},{3,5},{4,2},{5,3},{6,0},{7,1},{8,14},{9,15},{10,... | collective-permute-start | bytes 589832 | tf_op jit(solution)/shard_map/ppermute | solution.py:343
  32.3 12.3 %collective-permute-start.8 = (bf16[128,768]{1,0:T(8,128)(2,1)S(1)}, bf16[128,768]{1,0:T(8,128)(2,1)S(1)}, u32[]{:S(2)}, u32[]{:S(2)}) collective-permute-start(bf16[128,768]{1,0:T(8,128)(2,1)S(1)} %get-tuple-element.44), channel_id=1, source_target_pairs={{2,0},{3,1},{0,2},{1,3},{6,4},{7,5},{4,6},{5,7},{10,8},{11,9},{8,1... | collective-permute-start | bytes 589832 | tf_op jit(solution)/shard_map/ppermute | solution.py:343
  35.1 13.4 %collective-permute-start.9 = (bf16[128,768]{1,0:T(8,128)(2,1)S(1)}, bf16[128,768]{1,0:T(8,128)(2,1)S(1)}, u32[]{:S(2)}, u32[]{:S(2)}) collective-permute-start(bf16[128,768]{1,0:T(8,128)(2,1)S(1)} %get-tuple-element.45), channel_id=1, source_target_pairs={{5,0},{6,1},{7,2},{4,3},{1,4},{2,5},{3,6},{0,7},{13,8},{14,9},{15,... | collective-permute-start | bytes 589832 | tf_op jit(solution)/shard_map/ppermute | solution.py:343
  37.4 13.4 %collective-permute-start.3 = (bf16[128,768]{1,0:T(8,128)(2,1)S(1)}, bf16[128,768]{1,0:T(8,128)(2,1)S(1)}, u32[]{:S(2)}, u32[]{:S(2)}) collective-permute-start(bf16[128,768]{1,0:T(8,128)(2,1)S(1)} %get-tuple-element.36), channel_id=1, source_target_pairs={{1,0},{2,1},{3,2},{0,3},{5,4},{6,5},{7,6},{4,7},{9,8},{10,9},{11,1... | collective-permute-start | bytes 589832 | tf_op jit(solution)/shard_map/ppermute | solution.py:343
  39.5 11.4 %collective-permute-start.4 = (bf16[128,768]{1,0:T(8,128)(2,1)S(1)}, bf16[128,768]{1,0:T(8,128)(2,1)S(1)}, u32[]{:S(2)}, u32[]{:S(2)}) collective-permute-start(bf16[128,768]{1,0:T(8,128)(2,1)S(1)} %get-tuple-element.37), channel_id=1, source_target_pairs={{3,0},{0,1},{1,2},{2,3},{7,4},{4,5},{5,6},{6,7},{11,8},{8,9},{9,10... | collective-permute-start | bytes 589832 | tf_op jit(solution)/shard_map/ppermute | solution.py:343
  39.5 11.4 %copy-start = (bf16[256,768]{1,0:T(8,128)(2,1)S(1)}, bf16[256,768]{1,0:T(8,128)(2,1)}, u32[]{:S(2)}) copy-start(bf16[256,768]{1,0:T(8,128)(2,1)} %tokens_ref.1) | copy-start | bytes 1179652
  39.5 11.3 %collective-permute-start.5 = (bf16[128,768]{1,0:T(8,128)(2,1)S(1)}, bf16[128,768]{1,0:T(8,128)(2,1)S(1)}, u32[]{:S(2)}, u32[]{:S(2)}) collective-permute-start(bf16[128,768]{1,0:T(8,128)(2,1)S(1)} %get-tuple-element.38), channel_id=1, source_target_pairs={{4,0},{5,1},{6,2},{7,3},{0,4},{1,5},{2,6},{3,7},{12,8},{13,9},{14,... | collective-permute-start | bytes 589832 | tf_op jit(solution)/shard_map/ppermute | solution.py:343
  44.6 12.3 %copy-start.1 = (s32[1,16]{1,0:T(1,128)S(1)}, s32[1,16]{1,0:T(1,128)}, u32[]{:S(2)}) copy-start(s32[1,16]{1,0:T(1,128)} %lengths_ref.1) | copy-start | bytes 196
  44.6 8.3 %collective-permute-start.12 = (bf16[128,768]{1,0:T(8,128)(2,1)S(1)}, bf16[128,768]{1,0:T(8,128)(2,1)S(1)}, u32[]{:S(2)}, u32[]{:S(2)}) collective-permute-start(bf16[128,768]{1,0:T(8,128)(2,1)S(1)} %get-tuple-element.48), channel_id=1, source_target_pairs={{7,0},{4,1},{5,2},{6,3},{3,4},{0,5},{1,6},{2,7},{15,8},{12,9},{13,... | collective-permute-start | bytes 589832 | tf_op jit(solution)/shard_map/ppermute | solution.py:343
  48.5 8.4 %collective-permute-start.13 = (bf16[128,768]{1,0:T(8,128)(2,1)S(1)}, bf16[128,768]{1,0:T(8,128)(2,1)S(1)}, u32[]{:S(2)}, u32[]{:S(2)}) collective-permute-start(bf16[128,768]{1,0:T(8,128)(2,1)S(1)} %get-tuple-element.49), channel_id=1, source_target_pairs={{6,0},{7,1},{4,2},{5,3},{2,4},{3,5},{0,6},{1,7},{14,8},{15,9},{12,... | collective-permute-start | bytes 589832 | tf_op jit(solution)/shard_map/ppermute | solution.py:343
  77.0 9.5 %collective-permute-start.16 = (bf16[16,16,768]{2,1,0:T(8,128)(2,1)S(1)}, bf16[16,16,768]{2,1,0:T(8,128)(2,1)S(1)}, u32[]{:S(2)}, u32[]{:S(2)}) collective-permute-start(bf16[16,16,768]{2,1,0:T(8,128)(2,1)S(1)} %all_to_all.5), channel_id=1, source_target_pairs={{0,1},{1,2},{2,3},{3,0},{4,5},{5,6},{6,7},{7,4},{8,9},{9,10},{10,1... | collective-permute-start | bytes 1179656 | tf_op jit(solution)/shard_map/ppermute | solution.py:367
  77.0 15.2 %collective-permute-start.15 = (bf16[16,16,768]{2,1,0:T(8,128)(2,1)S(1)}, bf16[16,16,768]{2,1,0:T(8,128)(2,1)S(1)}, u32[]{:S(2)}, u32[]{:S(2)}) collective-permute-start(bf16[16,16,768]{2,1,0:T(8,128)(2,1)S(1)} %all_to_all.5), channel_id=1, source_target_pairs={{0,96},{8,104},{16,112},{24,120},{32,0},{40,8},{48,16},{56,24},{64... | collective-permute-start | bytes 1179656 | tf_op jit(solution)/shard_map/ppermute | solution.py:366
  77.0 15.2 %collective-permute-start.14 = (bf16[16,16,768]{2,1,0:T(8,128)(2,1)S(1)}, bf16[16,16,768]{2,1,0:T(8,128)(2,1)S(1)}, u32[]{:S(2)}, u32[]{:S(2)}) collective-permute-start(bf16[16,16,768]{2,1,0:T(8,128)(2,1)S(1)} %all_to_all.5), channel_id=1, source_target_pairs={{0,3},{1,0},{2,1},{3,2},{4,7},{5,4},{6,5},{7,6},{8,11},{9,8},{10,9... | collective-permute-start | bytes 1179656 | tf_op jit(solution)/shard_map/ppermute | solution.py:365
  79.6 13.1 %collective-permute-start.17 = (bf16[16,16,768]{2,1,0:T(8,128)(2,1)S(1)}, bf16[16,16,768]{2,1,0:T(8,128)(2,1)S(1)}, u32[]{:S(2)}, u32[]{:S(2)}) collective-permute-start(bf16[16,16,768]{2,1,0:T(8,128)(2,1)S(1)} %all_to_all.5), channel_id=1, source_target_pairs={{0,8},{8,0},{16,24},{24,16},{32,40},{40,32},{48,56},{56,48},{64,72... | collective-permute-start | bytes 1179656 | tf_op jit(solution)/shard_map/ppermute | solution.py:369
  86.4 8.3 %collective-permute-start.20 = (bf16[16,16,768]{2,1,0:T(8,128)(2,1)S(1)}, bf16[16,16,768]{2,1,0:T(8,128)(2,1)S(1)}, u32[]{:S(2)}, u32[]{:S(2)}) collective-permute-start(bf16[16,16,768]{2,1,0:T(8,128)(2,1)S(1)} %collective-permute-done.16), channel_id=1, source_target_pairs={{0,8},{8,0},{16,24},{24,16},{32,40},{40,32},{48,56},{56,48},{64,72... | collective-permute-start | bytes 1179656 | tf_op jit(solution)/shard_map/ppermute | solution.py:369
  92.1 2.5 %collective-permute-start.19 = (bf16[16,16,768]{2,1,0:T(8,128)(2,1)S(1)}, bf16[16,16,768]{2,1,0:T(8,128)(2,1)S(1)}, u32[]{:S(2)}, u32[]{:S(2)}) collective-permute-start(bf16[16,16,768]{2,1,0:T(8,128)(2,1)S(1)} %collective-permute-done.15), channel_id=1, source_target_pairs={{0,8},{8,0},{16,24},{24,16},{32,40},{40,32},{48,56},{56,48},{64,72... | collective-permute-start | bytes 1179656 | tf_op jit(solution)/shard_map/ppermute | solution.py:369
  92.2 2.5 %collective-permute-start.18 = (bf16[16,16,768]{2,1,0:T(8,128)(2,1)S(1)}, bf16[16,16,768]{2,1,0:T(8,128)(2,1)S(1)}, u32[]{:S(2)}, u32[]{:S(2)}) collective-permute-start(bf16[16,16,768]{2,1,0:T(8,128)(2,1)S(1)} %collective-permute-done.14), channel_id=1, source_target_pairs={{0,8},{8,0},{16,24},{24,16},{32,40},{40,32},{48,56},{56,48},{64,72... | collective-permute-start | bytes 1179656 | tf_op jit(solution)/shard_map/ppermute | solution.py:369

commit v9 on v8

--- a/solution.py
+++ b/solution.py
@@ -14,6 +14,8 @@
 bf16 = jnp.bfloat16
 mebibyte = 1024 * 1024
 plane = 4
+block = 512
+head = 512
 line = 4
 move_groups = (
     ((0, 0), (1, 0), (3, 0), (0, 1)),
@@ -71,9 +73,9 @@
 
 
 def route_kernel(
-    tokens_hbm, routes_hbm, gain_hbm, router_hbm, *refs
+    tokens_hbm, routes_hbm, gain_hbm, router_hbm, gate_hbm, up_hbm, *refs, head
 ):
-    *out_refs, slots_ref, weights_ref, tokens_ref, routes_ref, gain_ref, router_ref, sems = refs
+    *out_refs, slots_ref, weights_ref, gate_ref, up_ref, tokens_ref, routes_ref, gain_ref, router_ref, sems = refs
     copies = [
         pltpu.make_async_copy(tokens_hbm, tokens_ref, sems.at[0]),
         pltpu.make_async_copy(gain_hbm, gain_ref, sems.at[1]),
@@ -81,6 +83,12 @@
         pltpu.make_async_copy(router_hbm, router_ref, sems.at[3]),
     ]
     for copy in copies:
+        copy.start()
+    heads = [
+        pltpu.make_async_copy(gate_hbm.at[:, :head], gate_ref.at[:, :head], sems.at[4]),
+        pltpu.make_async_copy(up_hbm.at[:, :head], up_ref.at[:, :head], sems.at[5]),
+    ]
+    for copy in heads:
         copy.start()
     for copy in copies:
         copy.wait()
@@ -116,6 +124,8 @@
     both = jnp.sum(hits_down * logits, axis=-1, keepdims=True)
     slots_ref[...] = jnp.where(hits_down > 0.5, ranks_down, -1.0)
     weights_ref[...] = hits_down / (1.0 + jnp.exp(both - 2.0 * logits))
+    for copy in heads:
+        copy.wait()
 
 
 def stack(x_refs, x_ref):
@@ -137,10 +147,10 @@
     hidden_ref[:, at] = (gate_act / (1.0 + jnp.exp(-gate_act)) * up_act).astype(bf16)
 
 
-def first_expert_kernel(*refs, blocks, block, ahead):
-    x_refs, out_refs = refs[:blocks], refs[blocks + 3 : 2 * blocks + 3]
+def first_expert_kernel(*refs, blocks, block, present, ahead):
+    x_refs, out_refs = refs[:blocks], refs[blocks + 5 : 2 * blocks + 5]
     gate_hbm, up_hbm, down_hbm = refs[blocks : blocks + 3]
-    gate_ref, up_ref, down_ref, x_ref, hidden_ref, sems = refs[2 * blocks + 3 :]
+    gate_ref, up_ref, down_ref, x_ref, hidden_ref, sems = refs[2 * blocks + 5 :]
     steps = hidden_ref.shape[1] // block
 
     def part(step):
@@ -154,7 +164,7 @@
         )
 
     down_fetch = pltpu.make_async_copy(down_hbm, down_ref, sems.at[2, 0])
-    for step in range(ahead):
+    for step in range(present, ahead):
         for copy in fetches(step):
             copy.start()
     stack(x_refs, x_ref)
@@ -169,8 +179,11 @@
         def _():
             down_fetch.start()
 
-        for copy in fetches(step):
-            copy.wait()
+        @pl.when(step >= present)
+        def _():
+            for copy in fetches(step):
+                copy.wait()
+
         hidden_block(x_ref, gate_ref, up_ref, hidden_ref, part(step))
         return carry
 
@@ -194,20 +207,24 @@
     unstack(dot(hidden_ref[...], down_ref[...]).astype(bf16), out_refs)
 
 
-def expert_rows(xs, weights, first, block=512, ahead=2):
+def expert_rows(xs, weights, heads, ahead=2):
     rows, width = xs[0].shape
     hidden = weights[0].shape[1]
     blocks = len(xs)
     places = range(blocks, blocks + 3)
     results = [jax.ShapeDtypeStruct(x.shape, bf16) for x in xs]
     scratch = [pltpu.VMEM((blocks * rows, width), bf16), pltpu.VMEM((blocks * rows, hidden), bf16)]
-    if first:
+    if heads:
         out = call(
-            functools.partial(first_expert_kernel, blocks=blocks, block=block, ahead=ahead),
+            functools.partial(
+                first_expert_kernel, blocks=blocks, block=block, present=head // block, ahead=ahead
+            ),
             results + [jax.ShapeDtypeStruct(w.shape, bf16) for w in weights],
-            *xs, *weights,
+            *xs, *weights, *heads,
             budget=20,
             outside=places,
+            inside=range(blocks + 3, blocks + 5),
+            input_output_aliases={blocks + 3: blocks, blocks + 4: blocks + 1},
             scratch_shapes=scratch + [pltpu.SemaphoreType.DMA((3, hidden // block))],
         )
         return out[:blocks], out[blocks:]
@@ -288,20 +305,22 @@
     doc_grad_ref[...] = logit_scale * (fold(dot(likely, all_queries))[count:] + diagonal * queries)
 
 
-def route(tokens, routes, norm_gain, router_weight):
+def route(tokens, routes, norm_gain, router_weight, gate, up):
     rows, width = tokens.shape
     experts = router_weight.shape[1]
-    operands = (tokens, routes.T, norm_gain, router_weight.T)
+    operands = (tokens, routes.T, norm_gain, router_weight.T, gate, up)
     return call(
-        route_kernel,
+        functools.partial(route_kernel, head=head),
         [
             *[jax.ShapeDtypeStruct((rows // 2, width), bf16) for _ in range(experts)],
             jax.ShapeDtypeStruct((rows, experts), f32),
             jax.ShapeDtypeStruct((rows, experts), f32),
+            jax.ShapeDtypeStruct(gate.shape, bf16),
+            jax.ShapeDtypeStruct(up.shape, bf16),
         ],
         *operands,
-        outside=(0, 1, 2, 3),
-        scratch_shapes=[pltpu.VMEM(x.shape, x.dtype) for x in operands]
+        outside=range(6),
+        scratch_shapes=[pltpu.VMEM(x.shape, x.dtype) for x in operands[:4]]
         + [pltpu.SemaphoreType.DMA((len(operands),))],
     )
 
@@ -333,7 +352,10 @@
 def body(tokens, routes, lengths, norm_gain, router_weight, gate_weight, up_weight, down_weight):
     width = tokens.shape[1]
     experts = router_weight.shape[1]
-    *outgoing, slots, weights = route(tokens, routes, norm_gain, router_weight)
+    matrices = [gate_weight[0], up_weight[0], down_weight[0]]
+    *outgoing, slots, weights, gate, up = route(
+        tokens, routes, norm_gain, router_weight, *matrices[:2]
+    )
 
     def pairs(move, back):
         places = [(e, target(e, move)) for e in range(experts)]
@@ -343,10 +365,10 @@
         return x if move == (0, 0) else lax.ppermute(x, "expert", pairs(move, back))
 
     incoming = {move: send(x, move) for move, x in zip(moves, outgoing)}
-    matrices = [gate_weight[0], up_weight[0], down_weight[0]]
-    backs = []
-    for at, group in enumerate(move_groups):
-        results, matrices = expert_rows([incoming[move] for move in group], matrices, at == 0)
+    backs, heads = [], [gate, up]
+    for group in move_groups:
+        results, matrices = expert_rows([incoming[move] for move in group], matrices, heads)
+        heads = []
         backs += [send(x, move, back=True) for move, x in zip(group, results)]
     hidden_out, embedded, rounded = combine(tokens, slots, weights, backs, lengths)
 

time: 98.8 us -> 97.7 us (0.989)
  starting transfers between devices: 42.9 us -> 40 us
  blocking collectives: 18.6 us -> 20.7 us
  Pallas kernels: 29.3 us -> 28.3 us
    ppermute x4, starting transfers between devices: 13 us -> 9.96 us  [body(): blocks += [lax.ppermute(x, 'dp', swap) for x in blocks]]
    all_to_all x1, blocking collectives: 18.6 us -> 20.7 us  [body(): lax.all_to_all(copies, ('dp', 'expert'), split_axis=0, concat_axis=0, til...]
    pallas_call x7, Pallas kernels: 29.3 us -> 28.3 us  [call(): pl.pallas_call(kernel, out_shape=outs, in_specs=[left if at in outside el...]
  transfers between devices with their start and end apart: 21 -> 21, of which waited for: 3 -> 5; matrix products, arithmetic and copies ran while one was open for 0% -> 0% of each run, Pallas kernels for 22% -> 21%
where the time goes in v9:
time: 97.7 us; the launch traced here: 97.5 us
  starting transfers between devices  40 us (41%)
  Pallas kernels  28.3 us (29%)
  blocking collectives  20.7 us (21%)
  waiting for transfers between devices  7.38 us (8%)
    pallas_call x7, Pallas kernels, call(): pl.pallas_call(kernel, out_shape=outs, in_specs=[left if at in outside el...  28.3 us
    ppermute x14, starting transfers between devices, send(): return x if move == (0, 0) else lax.ppermute(x, 'expert', pairs(move, back))  27.3 us
    all_to_all x1, blocking collectives, body(): lax.all_to_all(copies, ('dp', 'expert'), split_axis=0, concat_axis=0, til...  20.7 us
    ppermute x4, starting transfers between devices, body(): blocks += [lax.ppermute(x, 'dp', swap) for x in blocks]  9.96 us
    ppermute x14, waiting for transfers between devices, send(): return x if move == (0, 0) else lax.ppermute(x, 'expert', pairs(move, back))  4.98 us
    ppermute x1, starting transfers between devices, body(): lax.ppermute(own, 'expert', pairs((3, 0), False))  2.67 us
  transfers between devices with their start and end apart: 21, of which 5 were waited for; matrix products, arithmetic and copies ran while one was open for 0% of the time, Pallas kernels for 21%

profile of v9, /device:TPU:1, one launch (start us, length us, event | category | flops | bytes accessed | tf_op | source)
XLA Modules:
  0.0 97.5 jit_solution(8596418002263162912)
XLA Ops:
  0.6 2.2 %shard_map.103 = (bf16[128,768]{1,0:T(8,128)(2,1)S(1)}, bf16[128,768]{1,0:T(8,128)(2,1)S(1)}, bf16[128,768]{1,0:T(8,128)(2,1)S(1)}, bf16[128,768]{1,0:T(8,128)(2...) custom-call(bf16[256,768]{1,0:T(8,128)(2,1)} %tokens_ref.1, ...), custom_call_target="tpu_custom_call" | custom-call | tf_op jit(solution)/shard_map/pallas_call | solution.py:65
  2.8 2.1 %collective-permute-start = (bf16[128,768]{1,0:T(8,128)(2,1)S(1)}, bf16[128,768]{1,0:T(8,128)(2,1)S(1)}, u32[]{:S(2)}, u32[]{:S(2)}) collective-permute-start(bf16[128,768]{1,0:T(8,128)(2,1)S(1)} %get-tuple-element.34), channel_id=1, source_target_pairs={{0,1},{1,2},{2,3},{3,0},{4,5},{5,6},{6,7},{7,4},{8,9},{9,10},{10,1... | collective-permute-start | bytes 589832 | tf_op jit(solution)/shard_map/ppermute | solution.py:365
  5.0 1.3 %collective-permute-start.1 = (bf16[128,768]{1,0:T(8,128)(2,1)S(1)}, bf16[128,768]{1,0:T(8,128)(2,1)S(1)}, u32[]{:S(2)}, u32[]{:S(2)}) collective-permute-start(bf16[128,768]{1,0:T(8,128)(2,1)S(1)} %get-tuple-element.35), channel_id=1, source_target_pairs={{0,3},{1,0},{2,1},{3,2},{4,7},{5,4},{6,5},{7,6},{8,11},{9,8},{10,9... | collective-permute-start | bytes 589832 | tf_op jit(solution)/shard_map/ppermute | solution.py:365
  6.3 3.7 %collective-permute-start.2 = (bf16[128,768]{1,0:T(8,128)(2,1)S(1)}, bf16[128,768]{1,0:T(8,128)(2,1)S(1)}, u32[]{:S(2)}, u32[]{:S(2)}) collective-permute-start(bf16[128,768]{1,0:T(8,128)(2,1)S(1)} %get-tuple-element.36), channel_id=1, source_target_pairs={{0,4},{1,5},{2,6},{3,7},{4,0},{5,1},{6,2},{7,3},{8,12},{9,13},{10,... | collective-permute-start | bytes 589832 | tf_op jit(solution)/shard_map/ppermute | solution.py:365
  10.0 1.5 %collective-permute-start.6 = (bf16[128,768]{1,0:T(8,128)(2,1)S(1)}, bf16[128,768]{1,0:T(8,128)(2,1)S(1)}, u32[]{:S(2)}, u32[]{:S(2)}) collective-permute-start(bf16[128,768]{1,0:T(8,128)(2,1)S(1)} %get-tuple-element.43), channel_id=1, source_target_pairs={{0,2},{1,3},{2,0},{3,1},{4,6},{5,7},{6,4},{7,5},{8,10},{9,11},{10,... | collective-permute-start | bytes 589832 | tf_op jit(solution)/shard_map/ppermute | solution.py:365
  11.6 0.0 collective-permute-start.7
  11.6 5.1 %collective-permute-start.10 = (bf16[128,768]{1,0:T(8,128)(2,1)S(1)}, bf16[128,768]{1,0:T(8,128)(2,1)S(1)}, u32[]{:S(2)}, u32[]{:S(2)}) collective-permute-start(bf16[128,768]{1,0:T(8,128)(2,1)S(1)} %get-tuple-element.50), channel_id=1, source_target_pairs={{0,7},{1,4},{2,5},{3,6},{4,3},{5,0},{6,1},{7,2},{8,15},{9,12},{10,... | collective-permute-start | bytes 589832 | tf_op jit(solution)/shard_map/ppermute | solution.py:365
  16.6 9.7 %shard_map.104 = (bf16[128,768]{1,0:T(8,128)(2,1)S(1)}, bf16[128,768]{1,0:T(8,128)(2,1)S(1)}, bf16[128,768]{1,0:T(8,128)(2,1)S(1)}, bf16[128,768]{1,0:T(8,128)(2...) custom-call(bf16[128,768]{1,0:T(8,128)(2,1)S(1)} %get-tuple-element., ...), custom_call_target="tpu_custom_call", output_to_operand_aliasing={{4}: (7, {}), {5}: (8, {})} | custom-call | tf_op jit(solution)/shard_map/pallas_call | solution.py:65
  26.4 1.0 %collective-permute-done.7.refs_1_ = bf16[128,768]{1,0:T(8,128)(2,1)S(1)} collective-permute-done((bf16[128,768]{1,0:T(8,128)(2,1)S(1)}, bf16[128,768]{1,0:T(8,128)(2,1)S(1)}, u32[]{:S(2)}, u32[]{:S(2)}) %collective-permute-start.7) | collective-permute-done | bytes 196640 | tf_op jit(solution)/shard_map/ppermute | solution.py:365
  27.4 5.0 %shard_map.105 = (bf16[128,768]{1,0:T(8,128)(2,1)S(1)}, bf16[128,768]{1,0:T(8,128)(2,1)S(1)}) custom-call(bf16[128,768]{1,0:T(8,128)(2,1)S(1)} %collective-permute-done.6.refs_0_, bf16[128,768]{1,0:T(8,128)(2,1)S(1)} %collective-permute-done.7.refs_1_, bf16[768,3072]{1,0:T(8,128)(2,1)S(1)} %get-tuple-element.45.refs_2_, ...), custom_call_target="tpu_custom_call" | custom-call | tf_op jit(solution)/shard_map/pallas_call | solution.py:65
  32.3 1.7 %collective-permute-start.8 = (bf16[128,768]{1,0:T(8,128)(2,1)S(1)}, bf16[128,768]{1,0:T(8,128)(2,1)S(1)}, u32[]{:S(2)}, u32[]{:S(2)}) collective-permute-start(bf16[128,768]{1,0:T(8,128)(2,1)S(1)} %get-tuple-element.48), channel_id=1, source_target_pairs={{2,0},{3,1},{0,2},{1,3},{6,4},{7,5},{4,6},{5,7},{10,8},{11,9},{8,1... | collective-permute-start | bytes 589832 | tf_op jit(solution)/shard_map/ppermute | solution.py:365
  34.1 2.4 %collective-permute-start.9 = (bf16[128,768]{1,0:T(8,128)(2,1)S(1)}, bf16[128,768]{1,0:T(8,128)(2,1)S(1)}, u32[]{:S(2)}, u32[]{:S(2)}) collective-permute-start(bf16[128,768]{1,0:T(8,128)(2,1)S(1)} %get-tuple-element.49), channel_id=1, source_target_pairs={{5,0},{6,1},{7,2},{4,3},{1,4},{2,5},{3,6},{0,7},{13,8},{14,9},{15,... | collective-permute-start | bytes 589832 | tf_op jit(solution)/shard_map/ppermute | solution.py:365
  36.4 3.1 %collective-permute-start.3 = (bf16[128,768]{1,0:T(8,128)(2,1)S(1)}, bf16[128,768]{1,0:T(8,128)(2,1)S(1)}, u32[]{:S(2)}, u32[]{:S(2)}) collective-permute-start(bf16[128,768]{1,0:T(8,128)(2,1)S(1)} %get-tuple-element.40), channel_id=1, source_target_pairs={{1,0},{2,1},{3,2},{0,3},{5,4},{6,5},{7,6},{4,7},{9,8},{10,9},{11,1... | collective-permute-start | bytes 589832 | tf_op jit(solution)/shard_map/ppermute | solution.py:365
  39.6 0.0 copy-start
  39.6 0.1 collective-permute-start.5
  39.7 4.9 %shard_map.107 = (bf16[128,768]{1,0:T(8,128)(2,1)S(1)}, bf16[128,768]{1,0:T(8,128)(2,1)S(1)}) custom-call(bf16[128,768]{1,0:T(8,128)(2,1)S(1)} %collective-permute-done.10.refs_0_, bf16[128,768]{1,0:T(8,128)(2,1)S(1)} %collective-permute-done.11.refs_1_, bf16[768,3072]{1,0:T(8,128)(2,1)S(1)} %get-tuple-element.45.refs_2_, ...), custom_call_target="tpu_custom_call" | custom-call | tf_op jit(solution)/shard_map/pallas_call | solution.py:65
  44.6 0.0 copy-start.1
  44.6 2.8 %collective-permute-start.12 = (bf16[128,768]{1,0:T(8,128)(2,1)S(1)}, bf16[128,768]{1,0:T(8,128)(2,1)S(1)}, u32[]{:S(2)}, u32[]{:S(2)}) collective-permute-start(bf16[128,768]{1,0:T(8,128)(2,1)S(1)} %get-tuple-element.52), channel_id=1, source_target_pairs={{7,0},{4,1},{5,2},{6,3},{3,4},{0,5},{1,6},{2,7},{15,8},{12,9},{13,... | collective-permute-start | bytes 589832 | tf_op jit(solution)/shard_map/ppermute | solution.py:365
  47.4 3.5 %collective-permute-start.13 = (bf16[128,768]{1,0:T(8,128)(2,1)S(1)}, bf16[128,768]{1,0:T(8,128)(2,1)S(1)}, u32[]{:S(2)}, u32[]{:S(2)}) collective-permute-start(bf16[128,768]{1,0:T(8,128)(2,1)S(1)} %get-tuple-element.53), channel_id=1, source_target_pairs={{6,0},{7,1},{4,2},{5,3},{2,4},{3,5},{0,6},{1,7},{14,8},{15,9},{12,... | collective-permute-start | bytes 589832 | tf_op jit(solution)/shard_map/ppermute | solution.py:365
  50.9 1.2 %shard_map.106.early_ref = f32[256,768]{1,0:T(8,128)S(1)} custom-call(bf16[256,768]{1,0:T(8,128)(2,1)S(1)} %copy-done, f32[256,8]{1,0:T(8,128)S(1)} %get-tuple-element.31.slots_ref, f32[256,8]{1,0:T(8,128)S(1)} %get-tuple-element.32.weights_ref, bf16[128,768]{1,0:T(8,128)(2,1)S(1)} %get-tuple-element.39.refs_0_, ...), custom_call_target="tpu_custom_call" | custom-call | tf_op jit(solution)/shard_map/pallas_call | solution.py:65
  52.2 0.9 collective-permute-done.12.refs_0_
  53.0 3.1 %collective-permute-done.13.refs_1_ = bf16[128,768]{1,0:T(8,128)(2,1)S(1)} collective-permute-done((bf16[128,768]{1,0:T(8,128)(2,1)S(1)}, bf16[128,768]{1,0:T(8,128)(2,1)S(1)}, u32[]{:S(2)}, u32[]{:S(2)}) %collective-permute-start.13) | collective-permute-done | bytes 196640 | tf_op jit(solution)/shard_map/ppermute | solution.py:365
  56.1 1.4 %shard_map.108 = (bf16[256,768]{1,0:T(8,128)(2,1)}, f32[16,768]{1,0:T(8,128)S(1)}, bf16[16,768]{1,0:T(8,128)(2,1)S(1)}) custom-call(f32[256,768]{1,0:T(8,128)S(1)} %shard_map.106.early_ref, f32[256,8]{1,0:T(8,128)S(1)} %get-tuple-element.31.slots_ref, f32[256,8]{1,0:T(8,128)S(1)} %get-tuple-element.32.weights_ref, s32[1,16]{1,0:T(1,128)S(1)} %copy-done.1, ...), custom_call_target="tpu_custom_call" | custom-call | tf_op jit(solution)/shard_map/pallas_call | solution.py:65
  57.6 20.7 %all_to_all.5 = bf16[16,16,768]{2,1,0:T(8,128)(2,1)S(1)} all-to-all(bf16[16,16,768]{2,1,0:T(8,128)(2,1)S(1)} %broadcast_in_dim.2), channel_id=1, replica_groups={{0,4,16,20,34,38,50,54,64,68,80,84,98,102,114,118},{8,12,24,28,42,46,58..., dimensions={0} | all-to-all | bytes 786432 | tf_op jit(solution)/shard_map/all_to_all | solution.py:382
  78.3 2.7 %collective-permute-start.14 = (bf16[16,16,768]{2,1,0:T(8,128)(2,1)S(1)}, bf16[16,16,768]{2,1,0:T(8,128)(2,1)S(1)}, u32[]{:S(2)}, u32[]{:S(2)}) collective-permute-start(bf16[16,16,768]{2,1,0:T(8,128)(2,1)S(1)} %all_to_all.5), channel_id=1, source_target_pairs={{0,3},{1,0},{2,1},{3,2},{4,7},{5,4},{6,5},{7,6},{8,11},{9,8},{10,9... | collective-permute-start | bytes 1179656 | tf_op jit(solution)/shard_map/ppermute | solution.py:387
  81.0 4.9 %collective-permute-start.17 = (bf16[16,16,768]{2,1,0:T(8,128)(2,1)S(1)}, bf16[16,16,768]{2,1,0:T(8,128)(2,1)S(1)}, u32[]{:S(2)}, u32[]{:S(2)}) collective-permute-start(bf16[16,16,768]{2,1,0:T(8,128)(2,1)S(1)} %all_to_all.5), channel_id=1, source_target_pairs={{0,8},{8,0},{16,24},{24,16},{32,40},{40,32},{48,56},{56,48},{64,72... | collective-permute-start | bytes 1179656 | tf_op jit(solution)/shard_map/ppermute | solution.py:391
  86.0 0.6 collective-permute-done.16
  86.5 4.5 %collective-permute-start.20 = (bf16[16,16,768]{2,1,0:T(8,128)(2,1)S(1)}, bf16[16,16,768]{2,1,0:T(8,128)(2,1)S(1)}, u32[]{:S(2)}, u32[]{:S(2)}) collective-permute-start(bf16[16,16,768]{2,1,0:T(8,128)(2,1)S(1)} %collective-permute-done.16), channel_id=1, source_target_pairs={{0,8},{8,0},{16,24},{24,16},{32,40},{40,32},{48,56},{56,48},{64,72... | collective-permute-start | bytes 1179656 | tf_op jit(solution)/shard_map/ppermute | solution.py:391
  91.0 0.0 collective-permute-start.19
  91.1 0.5 collective-permute-start.18
  91.7 1.8 %collective-permute-done.18 = bf16[16,16,768]{2,1,0:T(8,128)(2,1)S(1)} collective-permute-done((bf16[16,16,768]{2,1,0:T(8,128)(2,1)S(1)}, bf16[16,16,768]{2,1,0:T(8,128)(2,1)S(1)}, u32[]{:S(2)}, u32[]{:S(2)}) %collective-permute-start.18) | collective-permute-done | bytes 393248 | tf_op jit(solution)/shard_map/ppermute | solution.py:391
  93.6 3.8 %shard_map.109 = (f32[8,768]{1,0:T(8,128)}, f32[8,768]{1,0:T(8,128)}) custom-call(bf16[1024,768]{1,0:T(8,128)(2,1)S(1)} %bitcast.8, bf16[1024,768]{1,0:T(8,128)(2,1)S(1)} %bitcast.7, f32[16,768]{1,0:T(8,128)S(1)} %get-tuple-element.56.embedded_ref), custom_call_target="tpu_custom_call" | custom-call | tf_op jit(solution)/shard_map/pallas_call | solution.py:65
  (31 shorter events, 0.3 us)
Async XLA Ops:
  2.8 8.7 %collective-permute-start = (bf16[128,768]{1,0:T(8,128)(2,1)S(1)}, bf16[128,768]{1,0:T(8,128)(2,1)S(1)}, u32[]{:S(2)}, u32[]{:S(2)}) collective-permute-start(bf16[128,768]{1,0:T(8,128)(2,1)S(1)} %get-tuple-element.34), channel_id=1, source_target_pairs={{0,1},{1,2},{2,3},{3,0},{4,5},{5,6},{6,7},{7,4},{8,9},{9,10},{10,1... | collective-permute-start | bytes 589832 | tf_op jit(solution)/shard_map/ppermute | solution.py:365
  5.0 11.7 %collective-permute-start.1 = (bf16[128,768]{1,0:T(8,128)(2,1)S(1)}, bf16[128,768]{1,0:T(8,128)(2,1)S(1)}, u32[]{:S(2)}, u32[]{:S(2)}) collective-permute-start(bf16[128,768]{1,0:T(8,128)(2,1)S(1)} %get-tuple-element.35), channel_id=1, source_target_pairs={{0,3},{1,0},{2,1},{3,2},{4,7},{5,4},{6,5},{7,6},{8,11},{9,8},{10,9... | collective-permute-start | bytes 589832 | tf_op jit(solution)/shard_map/ppermute | solution.py:365
  6.3 10.3 %collective-permute-start.2 = (bf16[128,768]{1,0:T(8,128)(2,1)S(1)}, bf16[128,768]{1,0:T(8,128)(2,1)S(1)}, u32[]{:S(2)}, u32[]{:S(2)}) collective-permute-start(bf16[128,768]{1,0:T(8,128)(2,1)S(1)} %get-tuple-element.36), channel_id=1, source_target_pairs={{0,4},{1,5},{2,6},{3,7},{4,0},{5,1},{6,2},{7,3},{8,12},{9,13},{10,... | collective-permute-start | bytes 589832 | tf_op jit(solution)/shard_map/ppermute | solution.py:365
  10.0 16.3 %collective-permute-start.6 = (bf16[128,768]{1,0:T(8,128)(2,1)S(1)}, bf16[128,768]{1,0:T(8,128)(2,1)S(1)}, u32[]{:S(2)}, u32[]{:S(2)}) collective-permute-start(bf16[128,768]{1,0:T(8,128)(2,1)S(1)} %get-tuple-element.43), channel_id=1, source_target_pairs={{0,2},{1,3},{2,0},{3,1},{4,6},{5,7},{6,4},{7,5},{8,10},{9,11},{10,... | collective-permute-start | bytes 589832 | tf_op jit(solution)/shard_map/ppermute | solution.py:365
  11.6 15.8 %collective-permute-start.7 = (bf16[128,768]{1,0:T(8,128)(2,1)S(1)}, bf16[128,768]{1,0:T(8,128)(2,1)S(1)}, u32[]{:S(2)}, u32[]{:S(2)}) collective-permute-start(bf16[128,768]{1,0:T(8,128)(2,1)S(1)} %get-tuple-element.44), channel_id=1, source_target_pairs={{0,5},{1,6},{2,7},{3,4},{4,1},{5,2},{6,3},{7,0},{8,13},{9,14},{10,... | collective-permute-start | bytes 589832 | tf_op jit(solution)/shard_map/ppermute | solution.py:365
  11.6 28.0 %collective-permute-start.10 = (bf16[128,768]{1,0:T(8,128)(2,1)S(1)}, bf16[128,768]{1,0:T(8,128)(2,1)S(1)}, u32[]{:S(2)}, u32[]{:S(2)}) collective-permute-start(bf16[128,768]{1,0:T(8,128)(2,1)S(1)} %get-tuple-element.50), channel_id=1, source_target_pairs={{0,7},{1,4},{2,5},{3,6},{4,3},{5,0},{6,1},{7,2},{8,15},{9,12},{10,... | collective-permute-start | bytes 589832 | tf_op jit(solution)/shard_map/ppermute | solution.py:365
  16.6 22.9 %collective-permute-start.11 = (bf16[128,768]{1,0:T(8,128)(2,1)S(1)}, bf16[128,768]{1,0:T(8,128)(2,1)S(1)}, u32[]{:S(2)}, u32[]{:S(2)}) collective-permute-start(bf16[128,768]{1,0:T(8,128)(2,1)S(1)} %get-tuple-element.51), channel_id=1, source_target_pairs={{0,6},{1,7},{2,4},{3,5},{4,2},{5,3},{6,0},{7,1},{8,14},{9,15},{10,... | collective-permute-start | bytes 589832 | tf_op jit(solution)/shard_map/ppermute | solution.py:365
  32.3 12.3 %collective-permute-start.8 = (bf16[128,768]{1,0:T(8,128)(2,1)S(1)}, bf16[128,768]{1,0:T(8,128)(2,1)S(1)}, u32[]{:S(2)}, u32[]{:S(2)}) collective-permute-start(bf16[128,768]{1,0:T(8,128)(2,1)S(1)} %get-tuple-element.48), channel_id=1, source_target_pairs={{2,0},{3,1},{0,2},{1,3},{6,4},{7,5},{4,6},{5,7},{10,8},{11,9},{8,1... | collective-permute-start | bytes 589832 | tf_op jit(solution)/shard_map/ppermute | solution.py:365
  34.1 13.3 %collective-permute-start.9 = (bf16[128,768]{1,0:T(8,128)(2,1)S(1)}, bf16[128,768]{1,0:T(8,128)(2,1)S(1)}, u32[]{:S(2)}, u32[]{:S(2)}) collective-permute-start(bf16[128,768]{1,0:T(8,128)(2,1)S(1)} %get-tuple-element.49), channel_id=1, source_target_pairs={{5,0},{6,1},{7,2},{4,3},{1,4},{2,5},{3,6},{0,7},{13,8},{14,9},{15,... | collective-permute-start | bytes 589832 | tf_op jit(solution)/shard_map/ppermute | solution.py:365
  36.4 14.5 %collective-permute-start.3 = (bf16[128,768]{1,0:T(8,128)(2,1)S(1)}, bf16[128,768]{1,0:T(8,128)(2,1)S(1)}, u32[]{:S(2)}, u32[]{:S(2)}) collective-permute-start(bf16[128,768]{1,0:T(8,128)(2,1)S(1)} %get-tuple-element.40), channel_id=1, source_target_pairs={{1,0},{2,1},{3,2},{0,3},{5,4},{6,5},{7,6},{4,7},{9,8},{10,9},{11,1... | collective-permute-start | bytes 589832 | tf_op jit(solution)/shard_map/ppermute | solution.py:365
  39.5 11.4 %collective-permute-start.4 = (bf16[128,768]{1,0:T(8,128)(2,1)S(1)}, bf16[128,768]{1,0:T(8,128)(2,1)S(1)}, u32[]{:S(2)}, u32[]{:S(2)}) collective-permute-start(bf16[128,768]{1,0:T(8,128)(2,1)S(1)} %get-tuple-element.41), channel_id=1, source_target_pairs={{3,0},{0,1},{1,2},{2,3},{7,4},{4,5},{5,6},{6,7},{11,8},{8,9},{9,10... | collective-permute-start | bytes 589832 | tf_op jit(solution)/shard_map/ppermute | solution.py:365
  39.6 11.4 %copy-start = (bf16[256,768]{1,0:T(8,128)(2,1)S(1)}, bf16[256,768]{1,0:T(8,128)(2,1)}, u32[]{:S(2)}) copy-start(bf16[256,768]{1,0:T(8,128)(2,1)} %tokens_ref.1) | copy-start | bytes 1179652
  39.6 11.4 %collective-permute-start.5 = (bf16[128,768]{1,0:T(8,128)(2,1)S(1)}, bf16[128,768]{1,0:T(8,128)(2,1)S(1)}, u32[]{:S(2)}, u32[]{:S(2)}) collective-permute-start(bf16[128,768]{1,0:T(8,128)(2,1)S(1)} %get-tuple-element.42), channel_id=1, source_target_pairs={{4,0},{5,1},{6,2},{7,3},{0,4},{1,5},{2,6},{3,7},{12,8},{13,9},{14,... | collective-permute-start | bytes 589832 | tf_op jit(solution)/shard_map/ppermute | solution.py:365
  44.6 11.5 %copy-start.1 = (s32[1,16]{1,0:T(1,128)S(1)}, s32[1,16]{1,0:T(1,128)}, u32[]{:S(2)}) copy-start(s32[1,16]{1,0:T(1,128)} %lengths_ref.1) | copy-start | bytes 196
  44.6 8.4 %collective-permute-start.12 = (bf16[128,768]{1,0:T(8,128)(2,1)S(1)}, bf16[128,768]{1,0:T(8,128)(2,1)S(1)}, u32[]{:S(2)}, u32[]{:S(2)}) collective-permute-start(bf16[128,768]{1,0:T(8,128)(2,1)S(1)} %get-tuple-element.52), channel_id=1, source_target_pairs={{7,0},{4,1},{5,2},{6,3},{3,4},{0,5},{1,6},{2,7},{15,8},{12,9},{13,... | collective-permute-start | bytes 589832 | tf_op jit(solution)/shard_map/ppermute | solution.py:365
  47.4 8.7 %collective-permute-start.13 = (bf16[128,768]{1,0:T(8,128)(2,1)S(1)}, bf16[128,768]{1,0:T(8,128)(2,1)S(1)}, u32[]{:S(2)}, u32[]{:S(2)}) collective-permute-start(bf16[128,768]{1,0:T(8,128)(2,1)S(1)} %get-tuple-element.53), channel_id=1, source_target_pairs={{6,0},{7,1},{4,2},{5,3},{2,4},{3,5},{0,6},{1,7},{14,8},{15,9},{12,... | collective-permute-start | bytes 589832 | tf_op jit(solution)/shard_map/ppermute | solution.py:365
  78.3 8.2 %collective-permute-start.16 = (bf16[16,16,768]{2,1,0:T(8,128)(2,1)S(1)}, bf16[16,16,768]{2,1,0:T(8,128)(2,1)S(1)}, u32[]{:S(2)}, u32[]{:S(2)}) collective-permute-start(bf16[16,16,768]{2,1,0:T(8,128)(2,1)S(1)} %all_to_all.5), channel_id=1, source_target_pairs={{0,1},{1,2},{2,3},{3,0},{4,5},{5,6},{6,7},{7,4},{8,9},{9,10},{10,1... | collective-permute-start | bytes 1179656 | tf_op jit(solution)/shard_map/ppermute | solution.py:389
  78.3 12.7 %collective-permute-start.15 = (bf16[16,16,768]{2,1,0:T(8,128)(2,1)S(1)}, bf16[16,16,768]{2,1,0:T(8,128)(2,1)S(1)}, u32[]{:S(2)}, u32[]{:S(2)}) collective-permute-start(bf16[16,16,768]{2,1,0:T(8,128)(2,1)S(1)} %all_to_all.5), channel_id=1, source_target_pairs={{0,96},{8,104},{16,112},{24,120},{32,0},{40,8},{48,16},{56,24},{64... | collective-permute-start | bytes 1179656 | tf_op jit(solution)/shard_map/ppermute | solution.py:388
  78.3 12.7 %collective-permute-start.14 = (bf16[16,16,768]{2,1,0:T(8,128)(2,1)S(1)}, bf16[16,16,768]{2,1,0:T(8,128)(2,1)S(1)}, u32[]{:S(2)}, u32[]{:S(2)}) collective-permute-start(bf16[16,16,768]{2,1,0:T(8,128)(2,1)S(1)} %all_to_all.5), channel_id=1, source_target_pairs={{0,3},{1,0},{2,1},{3,2},{4,7},{5,4},{6,5},{7,6},{8,11},{9,8},{10,9... | collective-permute-start | bytes 1179656 | tf_op jit(solution)/shard_map/ppermute | solution.py:387
  81.0 10.7 %collective-permute-start.17 = (bf16[16,16,768]{2,1,0:T(8,128)(2,1)S(1)}, bf16[16,16,768]{2,1,0:T(8,128)(2,1)S(1)}, u32[]{:S(2)}, u32[]{:S(2)}) collective-permute-start(bf16[16,16,768]{2,1,0:T(8,128)(2,1)S(1)} %all_to_all.5), channel_id=1, source_target_pairs={{0,8},{8,0},{16,24},{24,16},{32,40},{40,32},{48,56},{56,48},{64,72... | collective-permute-start | bytes 1179656 | tf_op jit(solution)/shard_map/ppermute | solution.py:391
  86.5 7.1 %collective-permute-start.20 = (bf16[16,16,768]{2,1,0:T(8,128)(2,1)S(1)}, bf16[16,16,768]{2,1,0:T(8,128)(2,1)S(1)}, u32[]{:S(2)}, u32[]{:S(2)}) collective-permute-start(bf16[16,16,768]{2,1,0:T(8,128)(2,1)S(1)} %collective-permute-done.16), channel_id=1, source_target_pairs={{0,8},{8,0},{16,24},{24,16},{32,40},{40,32},{48,56},{56,48},{64,72... | collective-permute-start | bytes 1179656 | tf_op jit(solution)/shard_map/ppermute | solution.py:391
  91.0 2.5 %collective-permute-start.19 = (bf16[16,16,768]{2,1,0:T(8,128)(2,1)S(1)}, bf16[16,16,768]{2,1,0:T(8,128)(2,1)S(1)}, u32[]{:S(2)}, u32[]{:S(2)}) collective-permute-start(bf16[16,16,768]{2,1,0:T(8,128)(2,1)S(1)} %collective-permute-done.15), channel_id=1, source_target_pairs={{0,8},{8,0},{16,24},{24,16},{32,40},{40,32},{48,56},{56,48},{64,72... | collective-permute-start | bytes 1179656 | tf_op jit(solution)/shard_map/ppermute | solution.py:391
  91.1 2.5 %collective-permute-start.18 = (bf16[16,16,768]{2,1,0:T(8,128)(2,1)S(1)}, bf16[16,16,768]{2,1,0:T(8,128)(2,1)S(1)}, u32[]{:S(2)}, u32[]{:S(2)}) collective-permute-start(bf16[16,16,768]{2,1,0:T(8,128)(2,1)S(1)} %collective-permute-done.14), channel_id=1, source_target_pairs={{0,8},{8,0},{16,24},{24,16},{32,40},{40,32},{48,56},{56,48},{64,72... | collective-permute-start | bytes 1179656 | tf_op jit(solution)/shard_map/ppermute | solution.py:391

commit v10 on v9

--- a/solution.py
+++ b/solution.py
@@ -147,10 +147,12 @@
     hidden_ref[:, at] = (gate_act / (1.0 + jnp.exp(-gate_act)) * up_act).astype(bf16)
 
 
-def first_expert_kernel(*refs, blocks, block, present, ahead):
-    x_refs, out_refs = refs[:blocks], refs[blocks + 5 : 2 * blocks + 5]
+def first_expert_kernel(*refs, blocks, held, block, present, ahead):
+    outs = blocks + 5 + held
+    x_refs, out_refs = refs[:blocks], refs[outs : outs + blocks]
     gate_hbm, up_hbm, down_hbm = refs[blocks : blocks + 3]
-    gate_ref, up_ref, down_ref, x_ref, hidden_ref, sems = refs[2 * blocks + 5 :]
+    gate_ref, up_ref, down_ref = refs[outs + blocks : outs + blocks + 3]
+    x_ref, hidden_ref, sems = refs[outs + blocks + 3 + held :]
     steps = hidden_ref.shape[1] // block
 
     def part(step):
@@ -207,7 +209,7 @@
     unstack(dot(hidden_ref[...], down_ref[...]).astype(bf16), out_refs)
 
 
-def expert_rows(xs, weights, heads, ahead=2):
+def expert_rows(xs, weights, heads, held, ahead=2):
     rows, width = xs[0].shape
     hidden = weights[0].shape[1]
     blocks = len(xs)
@@ -217,17 +219,26 @@
     if heads:
         out = call(
             functools.partial(
-                first_expert_kernel, blocks=blocks, block=block, present=head // block, ahead=ahead
+                first_expert_kernel,
+                blocks=blocks,
+                held=len(held),
+                block=block,
+                present=head // block,
+                ahead=ahead,
             ),
-            results + [jax.ShapeDtypeStruct(w.shape, bf16) for w in weights],
-            *xs, *weights, *heads,
+            results + [jax.ShapeDtypeStruct(w.shape, bf16) for w in [*weights, *held]],
+            *xs, *weights, *heads, *held,
             budget=20,
             outside=places,
             inside=range(blocks + 3, blocks + 5),
-            input_output_aliases={blocks + 3: blocks, blocks + 4: blocks + 1},
+            input_output_aliases={
+                blocks + 3: blocks,
+                blocks + 4: blocks + 1,
+                **{blocks + 5 + at: blocks + 3 + at for at in range(len(held))},
+            },
             scratch_shapes=scratch + [pltpu.SemaphoreType.DMA((3, hidden // block))],
         )
-        return out[:blocks], out[blocks:]
+        return out[:blocks], out[blocks : blocks + 3], out[blocks + 3 :]
     out = call(
         functools.partial(later_expert_kernel, blocks=blocks, block=block),
         results,
@@ -236,7 +247,7 @@
         inside=places,
         scratch_shapes=scratch,
     )
-    return out, weights
+    return out, weights, held
 
 
 def weighted_rows(slots_ref, weights_ref, back_refs, start):
@@ -364,10 +375,16 @@
     def send(x, move, back=False):
         return x if move == (0, 0) else lax.ppermute(x, "expert", pairs(move, back))
 
-    incoming = {move: send(x, move) for move, x in zip(moves, outgoing)}
+    late = move_groups[-1]
+    held = outgoing[-len(late) :]
+    incoming = {move: send(x, move) for move, x in zip(moves, outgoing) if move not in late}
     backs, heads = [], [gate, up]
     for group in move_groups:
-        results, matrices = expert_rows([incoming[move] for move in group], matrices, heads)
+        results, matrices, held = expert_rows(
+            [incoming[move] for move in group], matrices, heads, held
+        )
+        if heads:
+            incoming |= {move: send(x, move) for move, x in zip(late, held)}
         heads = []
         backs += [send(x, move, back=True) for move, x in zip(group, results)]
     hidden_out, embedded, rounded = combine(tokens, slots, weights, backs, lengths)

time: 97.7 us -> 101 us (1.034)
  starting transfers between devices: 40 us -> 45.8 us
  blocking collectives: 20.7 us -> 15.7 us
  waiting for transfers between devices: 7.38 us -> 9.45 us
    ppermute x4, starting transfers between devices: 9.96 us -> 16.7 us  [body(): blocks += [lax.ppermute(x, 'dp', swap) for x in blocks]]
    all_to_all x1, blocking collectives: 20.7 us -> 15.7 us  [body(): lax.all_to_all(copies, ('dp', 'expert'), split_axis=0, concat_axis=0, til...]
    ppermute x14, waiting for transfers between devices: 4.98 us -> 7.63 us  [send(): return x if move == (0, 0) else lax.ppermute(x, 'expert', pairs(move, back))]
    ppermute x14, starting transfers between devices: 27.3 us -> 25.6 us  [send(): return x if move == (0, 0) else lax.ppermute(x, 'expert', pairs(move, back))]
    ppermute x1, starting transfers between devices: 0.01 us -> 1.36 us  [body(): lax.ppermute(own, 'expert', pairs((1, 0), False))]
  transfers between devices with their start and end apart: 21 -> 21, of which waited for: 5 -> 4; matrix products, arithmetic and copies ran while one was open for 0% -> 0% of each run, Pallas kernels for 21% -> 21%
where the time goes in v10:
time: 101 us; the launch traced here: 100 us
  starting transfers between devices  45.8 us (45%)
  Pallas kernels  28.3 us (28%)
  blocking collectives  15.7 us (16%)
  waiting for transfers between devices  9.45 us (9%)
    pallas_call x7, Pallas kernels, call(): pl.pallas_call(kernel, out_shape=outs, in_specs=[left if at in outside el...  28.3 us
    ppermute x14, starting transfers between devices, send(): return x if move == (0, 0) else lax.ppermute(x, 'expert', pairs(move, back))  25.6 us
    ppermute x4, starting transfers between devices, body(): blocks += [lax.ppermute(x, 'dp', swap) for x in blocks]  16.7 us
    all_to_all x1, blocking collectives, body(): lax.all_to_all(copies, ('dp', 'expert'), split_axis=0, concat_axis=0, til...  15.7 us
    ppermute x14, waiting for transfers between devices, send(): return x if move == (0, 0) else lax.ppermute(x, 'expert', pairs(move, back))  7.63 us
    ppermute x1, starting transfers between devices, body(): lax.ppermute(own, 'expert', pairs((3, 0), False))  2.07 us
  transfers between devices with their start and end apart: 21, of which 4 were waited for; matrix products, arithmetic and copies ran while one was open for 0% of the time, Pallas kernels for 21%

profile of v10, /device:TPU:1, one launch (start us, length us, event | category | flops | bytes accessed | tf_op | source)
XLA Modules:
  0.0 100.3 jit_solution(17795319838922446500)
XLA Ops:
  0.6 2.2 %shard_map.103 = (bf16[128,768]{1,0:T(8,128)(2,1)S(1)}, bf16[128,768]{1,0:T(8,128)(2,1)S(1)}, bf16[128,768]{1,0:T(8,128)(2,1)S(1)}, bf16[128,768]{1,0:T(8,128)(2...) custom-call(bf16[256,768]{1,0:T(8,128)(2,1)} %tokens_ref.1, ...), custom_call_target="tpu_custom_call" | custom-call | tf_op jit(solution)/shard_map/pallas_call | solution.py:65
  2.8 2.1 %collective-permute-start = (bf16[128,768]{1,0:T(8,128)(2,1)S(1)}, bf16[128,768]{1,0:T(8,128)(2,1)S(1)}, u32[]{:S(2)}, u32[]{:S(2)}) collective-permute-start(bf16[128,768]{1,0:T(8,128)(2,1)S(1)} %get-tuple-element.36), channel_id=1, source_target_pairs={{0,1},{1,2},{2,3},{3,0},{4,5},{5,6},{6,7},{7,4},{8,9},{9,10},{10,1... | collective-permute-start | bytes 589832 | tf_op jit(solution)/shard_map/ppermute | solution.py:376
  5.0 1.3 %collective-permute-start.1 = (bf16[128,768]{1,0:T(8,128)(2,1)S(1)}, bf16[128,768]{1,0:T(8,128)(2,1)S(1)}, u32[]{:S(2)}, u32[]{:S(2)}) collective-permute-start(bf16[128,768]{1,0:T(8,128)(2,1)S(1)} %get-tuple-element.37), channel_id=1, source_target_pairs={{0,3},{1,0},{2,1},{3,2},{4,7},{5,4},{6,5},{7,6},{8,11},{9,8},{10,9... | collective-permute-start | bytes 589832 | tf_op jit(solution)/shard_map/ppermute | solution.py:376
  6.3 3.7 %collective-permute-start.2 = (bf16[128,768]{1,0:T(8,128)(2,1)S(1)}, bf16[128,768]{1,0:T(8,128)(2,1)S(1)}, u32[]{:S(2)}, u32[]{:S(2)}) collective-permute-start(bf16[128,768]{1,0:T(8,128)(2,1)S(1)} %get-tuple-element.38), channel_id=1, source_target_pairs={{0,4},{1,5},{2,6},{3,7},{4,0},{5,1},{6,2},{7,3},{8,12},{9,13},{10,... | collective-permute-start | bytes 589832 | tf_op jit(solution)/shard_map/ppermute | solution.py:376
  10.0 1.5 %collective-permute-start.6 = (bf16[128,768]{1,0:T(8,128)(2,1)S(1)}, bf16[128,768]{1,0:T(8,128)(2,1)S(1)}, u32[]{:S(2)}, u32[]{:S(2)}) collective-permute-start(bf16[128,768]{1,0:T(8,128)(2,1)S(1)} %get-tuple-element.47), channel_id=1, source_target_pairs={{0,2},{1,3},{2,0},{3,1},{4,6},{5,7},{6,4},{7,5},{8,10},{9,11},{10,... | collective-permute-start | bytes 589832 | tf_op jit(solution)/shard_map/ppermute | solution.py:376
  11.6 0.0 collective-permute-start.7
  11.6 2.4 %collective-permute-done.2.refs_3_ = bf16[128,768]{1,0:T(8,128)(2,1)S(1)} collective-permute-done((bf16[128,768]{1,0:T(8,128)(2,1)S(1)}, bf16[128,768]{1,0:T(8,128)(2,1)S(1)}, u32[]{:S(2)}, u32[]{:S(2)}) %collective-permute-start.2) | collective-permute-done | bytes 196640 | tf_op jit(solution)/shard_map/ppermute | solution.py:376
  14.0 9.7 %shard_map.104 = (bf16[128,768]{1,0:T(8,128)(2,1)S(1)}, bf16[128,768]{1,0:T(8,128)(2,1)S(1)}, bf16[128,768]{1,0:T(8,128)(2,1)S(1)}, bf16[128,768]{1,0:T(8,128)(2...) custom-call(bf16[128,768]{1,0:T(8,128)(2,1)S(1)} %get-tuple-element., ...), custom_call_target="tpu_custom_call", output_to_operand_aliasing={{4}: (7, {}), {5}: (8, {}), {7}: (9, {}), {8}: (10, {})} | custom-call | tf_op jit(solution)/shard_map/pallas_call | solution.py:65
  23.7 3.7 %collective-permute-start.10 = (bf16[128,768]{1,0:T(8,128)(2,1)S(1)}, bf16[128,768]{1,0:T(8,128)(2,1)S(1)}, u32[]{:S(2)}, u32[]{:S(2)}) collective-permute-start(bf16[128,768]{1,0:T(8,128)(2,1)S(1)} %get-tuple-element.54), channel_id=1, source_target_pairs={{0,7},{1,4},{2,5},{3,6},{4,3},{5,0},{6,1},{7,2},{8,15},{9,12},{10,... | collective-permute-start | bytes 589832 | tf_op jit(solution)/shard_map/ppermute | solution.py:376
  27.4 0.8 collective-permute-start.11
  28.3 5.0 %shard_map.105 = (bf16[128,768]{1,0:T(8,128)(2,1)S(1)}, bf16[128,768]{1,0:T(8,128)(2,1)S(1)}) custom-call(bf16[128,768]{1,0:T(8,128)(2,1)S(1)} %collective-permute-done.6.refs_0_, bf16[128,768]{1,0:T(8,128)(2,1)S(1)} %collective-permute-done.7.refs_1_, bf16[768,3072]{1,0:T(8,128)(2,1)S(1)} %get-tuple-element.49.refs_2_, ...), custom_call_target="tpu_custom_call" | custom-call | tf_op jit(solution)/shard_map/pallas_call | solution.py:65
  33.2 2.2 %collective-permute-start.8 = (bf16[128,768]{1,0:T(8,128)(2,1)S(1)}, bf16[128,768]{1,0:T(8,128)(2,1)S(1)}, u32[]{:S(2)}, u32[]{:S(2)}) collective-permute-start(bf16[128,768]{1,0:T(8,128)(2,1)S(1)} %get-tuple-element.52), channel_id=1, source_target_pairs={{2,0},{3,1},{0,2},{1,3},{6,4},{7,5},{4,6},{5,7},{10,8},{11,9},{8,1... | collective-permute-start | bytes 589832 | tf_op jit(solution)/shard_map/ppermute | solution.py:376
  35.5 3.4 %collective-permute-start.9 = (bf16[128,768]{1,0:T(8,128)(2,1)S(1)}, bf16[128,768]{1,0:T(8,128)(2,1)S(1)}, u32[]{:S(2)}, u32[]{:S(2)}) collective-permute-start(bf16[128,768]{1,0:T(8,128)(2,1)S(1)} %get-tuple-element.53), channel_id=1, source_target_pairs={{5,0},{6,1},{7,2},{4,3},{1,4},{2,5},{3,6},{0,7},{13,8},{14,9},{15,... | collective-permute-start | bytes 589832 | tf_op jit(solution)/shard_map/ppermute | solution.py:376
  38.9 0.0 collective-permute-start.3
  38.9 1.5 %collective-permute-start.4 = (bf16[128,768]{1,0:T(8,128)(2,1)S(1)}, bf16[128,768]{1,0:T(8,128)(2,1)S(1)}, u32[]{:S(2)}, u32[]{:S(2)}) collective-permute-start(bf16[128,768]{1,0:T(8,128)(2,1)S(1)} %get-tuple-element.45), channel_id=1, source_target_pairs={{3,0},{0,1},{1,2},{2,3},{7,4},{4,5},{5,6},{6,7},{11,8},{8,9},{9,10... | collective-permute-start | bytes 589832 | tf_op jit(solution)/shard_map/ppermute | solution.py:376
  40.4 5.0 %shard_map.107 = (bf16[128,768]{1,0:T(8,128)(2,1)S(1)}, bf16[128,768]{1,0:T(8,128)(2,1)S(1)}) custom-call(bf16[128,768]{1,0:T(8,128)(2,1)S(1)} %collective-permute-done.10.refs_0_, bf16[128,768]{1,0:T(8,128)(2,1)S(1)} %collective-permute-done.11.refs_1_, bf16[768,3072]{1,0:T(8,128)(2,1)S(1)} %get-tuple-element.49.refs_2_, ...), custom_call_target="tpu_custom_call" | custom-call | tf_op jit(solution)/shard_map/pallas_call | solution.py:65
  45.4 0.0 copy-start.1
  45.4 3.1 %collective-permute-start.12 = (bf16[128,768]{1,0:T(8,128)(2,1)S(1)}, bf16[128,768]{1,0:T(8,128)(2,1)S(1)}, u32[]{:S(2)}, u32[]{:S(2)}) collective-permute-start(bf16[128,768]{1,0:T(8,128)(2,1)S(1)} %get-tuple-element.56), channel_id=1, source_target_pairs={{7,0},{4,1},{5,2},{6,3},{3,4},{0,5},{1,6},{2,7},{15,8},{12,9},{13,... | collective-permute-start | bytes 589832 | tf_op jit(solution)/shard_map/ppermute | solution.py:376
  48.5 2.0 %collective-permute-start.13 = (bf16[128,768]{1,0:T(8,128)(2,1)S(1)}, bf16[128,768]{1,0:T(8,128)(2,1)S(1)}, u32[]{:S(2)}, u32[]{:S(2)}) collective-permute-start(bf16[128,768]{1,0:T(8,128)(2,1)S(1)} %get-tuple-element.57), channel_id=1, source_target_pairs={{6,0},{7,1},{4,2},{5,3},{2,4},{3,5},{0,6},{1,7},{14,8},{15,9},{12,... | collective-permute-start | bytes 589832 | tf_op jit(solution)/shard_map/ppermute | solution.py:376
  50.6 1.2 %shard_map.106.early_ref = f32[256,768]{1,0:T(8,128)S(1)} custom-call(bf16[256,768]{1,0:T(8,128)(2,1)S(1)} %copy-done, f32[256,8]{1,0:T(8,128)S(1)} %get-tuple-element.33.slots_ref, f32[256,8]{1,0:T(8,128)S(1)} %get-tuple-element.34.weights_ref, bf16[128,768]{1,0:T(8,128)(2,1)S(1)} %get-tuple-element.43.refs_0_, ...), custom_call_target="tpu_custom_call" | custom-call | tf_op jit(solution)/shard_map/pallas_call | solution.py:65
  51.8 1.9 %collective-permute-done.12.refs_0_ = bf16[128,768]{1,0:T(8,128)(2,1)S(1)} collective-permute-done((bf16[128,768]{1,0:T(8,128)(2,1)S(1)}, bf16[128,768]{1,0:T(8,128)(2,1)S(1)}, u32[]{:S(2)}, u32[]{:S(2)}) %collective-permute-start.12) | collective-permute-done | bytes 196640 | tf_op jit(solution)/shard_map/ppermute | solution.py:376
  53.7 3.3 %collective-permute-done.13.refs_1_ = bf16[128,768]{1,0:T(8,128)(2,1)S(1)} collective-permute-done((bf16[128,768]{1,0:T(8,128)(2,1)S(1)}, bf16[128,768]{1,0:T(8,128)(2,1)S(1)}, u32[]{:S(2)}, u32[]{:S(2)}) %collective-permute-start.13) | collective-permute-done | bytes 196640 | tf_op jit(solution)/shard_map/ppermute | solution.py:376
  57.0 1.4 %shard_map.108 = (bf16[256,768]{1,0:T(8,128)(2,1)}, f32[16,768]{1,0:T(8,128)S(1)}, bf16[16,768]{1,0:T(8,128)(2,1)S(1)}) custom-call(f32[256,768]{1,0:T(8,128)S(1)} %shard_map.106.early_ref, f32[256,8]{1,0:T(8,128)S(1)} %get-tuple-element.33.slots_ref, f32[256,8]{1,0:T(8,128)S(1)} %get-tuple-element.34.weights_ref, s32[1,16]{1,0:T(1,128)S(1)} %copy-done.1, ...), custom_call_target="tpu_custom_call" | custom-call | tf_op jit(solution)/shard_map/pallas_call | solution.py:65
  58.5 15.7 %all_to_all.5 = bf16[16,16,768]{2,1,0:T(8,128)(2,1)S(1)} all-to-all(bf16[16,16,768]{2,1,0:T(8,128)(2,1)S(1)} %broadcast_in_dim.2), channel_id=1, replica_groups={{0,4,16,20,34,38,50,54,64,68,80,84,98,102,114,118},{8,12,24,28,42,46,58..., dimensions={0} | all-to-all | bytes 786432 | tf_op jit(solution)/shard_map/all_to_all | solution.py:399
  74.2 1.4 %collective-permute-start.16 = (bf16[16,16,768]{2,1,0:T(8,128)(2,1)S(1)}, bf16[16,16,768]{2,1,0:T(8,128)(2,1)S(1)}, u32[]{:S(2)}, u32[]{:S(2)}) collective-permute-start(bf16[16,16,768]{2,1,0:T(8,128)(2,1)S(1)} %all_to_all.5), channel_id=1, source_target_pairs={{0,1},{1,2},{2,3},{3,0},{4,5},{5,6},{6,7},{7,4},{8,9},{9,10},{10,1... | collective-permute-start | bytes 1179656 | tf_op jit(solution)/shard_map/ppermute | solution.py:406
  75.6 2.1 %collective-permute-start.14 = (bf16[16,16,768]{2,1,0:T(8,128)(2,1)S(1)}, bf16[16,16,768]{2,1,0:T(8,128)(2,1)S(1)}, u32[]{:S(2)}, u32[]{:S(2)}) collective-permute-start(bf16[16,16,768]{2,1,0:T(8,128)(2,1)S(1)} %all_to_all.5), channel_id=1, source_target_pairs={{0,3},{1,0},{2,1},{3,2},{4,7},{5,4},{6,5},{7,6},{8,11},{9,8},{10,9... | collective-permute-start | bytes 1179656 | tf_op jit(solution)/shard_map/ppermute | solution.py:404
  77.6 10.5 %collective-permute-start.17 = (bf16[16,16,768]{2,1,0:T(8,128)(2,1)S(1)}, bf16[16,16,768]{2,1,0:T(8,128)(2,1)S(1)}, u32[]{:S(2)}, u32[]{:S(2)}) collective-permute-start(bf16[16,16,768]{2,1,0:T(8,128)(2,1)S(1)} %all_to_all.5), channel_id=1, source_target_pairs={{0,8},{8,0},{16,24},{24,16},{32,40},{40,32},{48,56},{56,48},{64,72... | collective-permute-start | bytes 1179656 | tf_op jit(solution)/shard_map/ppermute | solution.py:408
  88.2 5.7 %collective-permute-start.20 = (bf16[16,16,768]{2,1,0:T(8,128)(2,1)S(1)}, bf16[16,16,768]{2,1,0:T(8,128)(2,1)S(1)}, u32[]{:S(2)}, u32[]{:S(2)}) collective-permute-start(bf16[16,16,768]{2,1,0:T(8,128)(2,1)S(1)} %collective-permute-done.16), channel_id=1, source_target_pairs={{0,8},{8,0},{16,24},{24,16},{32,40},{40,32},{48,56},{56,48},{64,72... | collective-permute-start | bytes 1179656 | tf_op jit(solution)/shard_map/ppermute | solution.py:408
  93.9 0.0 collective-permute-start.19
  93.9 0.5 collective-permute-start.18
  94.6 1.8 %collective-permute-done.18 = bf16[16,16,768]{2,1,0:T(8,128)(2,1)S(1)} collective-permute-done((bf16[16,16,768]{2,1,0:T(8,128)(2,1)S(1)}, bf16[16,16,768]{2,1,0:T(8,128)(2,1)S(1)}, u32[]{:S(2)}, u32[]{:S(2)}) %collective-permute-start.18) | collective-permute-done | bytes 393248 | tf_op jit(solution)/shard_map/ppermute | solution.py:408
  96.5 3.8 %shard_map.109 = (f32[8,768]{1,0:T(8,128)}, f32[8,768]{1,0:T(8,128)}) custom-call(bf16[1024,768]{1,0:T(8,128)(2,1)S(1)} %bitcast.8, bf16[1024,768]{1,0:T(8,128)(2,1)S(1)} %bitcast.7, f32[16,768]{1,0:T(8,128)S(1)} %get-tuple-element.60.embedded_ref), custom_call_target="tpu_custom_call" | custom-call | tf_op jit(solution)/shard_map/pallas_call | solution.py:65
  (31 shorter events, 0.3 us)
Async XLA Ops:
  2.8 8.7 %collective-permute-start = (bf16[128,768]{1,0:T(8,128)(2,1)S(1)}, bf16[128,768]{1,0:T(8,128)(2,1)S(1)}, u32[]{:S(2)}, u32[]{:S(2)}) collective-permute-start(bf16[128,768]{1,0:T(8,128)(2,1)S(1)} %get-tuple-element.36), channel_id=1, source_target_pairs={{0,1},{1,2},{2,3},{3,0},{4,5},{5,6},{6,7},{7,4},{8,9},{9,10},{10,1... | collective-permute-start | bytes 589832 | tf_op jit(solution)/shard_map/ppermute | solution.py:376
  5.0 6.6 %collective-permute-start.1 = (bf16[128,768]{1,0:T(8,128)(2,1)S(1)}, bf16[128,768]{1,0:T(8,128)(2,1)S(1)}, u32[]{:S(2)}, u32[]{:S(2)}) collective-permute-start(bf16[128,768]{1,0:T(8,128)(2,1)S(1)} %get-tuple-element.37), channel_id=1, source_target_pairs={{0,3},{1,0},{2,1},{3,2},{4,7},{5,4},{6,5},{7,6},{8,11},{9,8},{10,9... | collective-permute-start | bytes 589832 | tf_op jit(solution)/shard_map/ppermute | solution.py:376
  6.3 7.7 %collective-permute-start.2 = (bf16[128,768]{1,0:T(8,128)(2,1)S(1)}, bf16[128,768]{1,0:T(8,128)(2,1)S(1)}, u32[]{:S(2)}, u32[]{:S(2)}) collective-permute-start(bf16[128,768]{1,0:T(8,128)(2,1)S(1)} %get-tuple-element.38), channel_id=1, source_target_pairs={{0,4},{1,5},{2,6},{3,7},{4,0},{5,1},{6,2},{7,3},{8,12},{9,13},{10,... | collective-permute-start | bytes 589832 | tf_op jit(solution)/shard_map/ppermute | solution.py:376
  10.0 18.3 %collective-permute-start.6 = (bf16[128,768]{1,0:T(8,128)(2,1)S(1)}, bf16[128,768]{1,0:T(8,128)(2,1)S(1)}, u32[]{:S(2)}, u32[]{:S(2)}) collective-permute-start(bf16[128,768]{1,0:T(8,128)(2,1)S(1)} %get-tuple-element.47), channel_id=1, source_target_pairs={{0,2},{1,3},{2,0},{3,1},{4,6},{5,7},{6,4},{7,5},{8,10},{9,11},{10,... | collective-permute-start | bytes 589832 | tf_op jit(solution)/shard_map/ppermute | solution.py:376
  11.6 16.7 %collective-permute-start.7 = (bf16[128,768]{1,0:T(8,128)(2,1)S(1)}, bf16[128,768]{1,0:T(8,128)(2,1)S(1)}, u32[]{:S(2)}, u32[]{:S(2)}) collective-permute-start(bf16[128,768]{1,0:T(8,128)(2,1)S(1)} %get-tuple-element.48), channel_id=1, source_target_pairs={{0,5},{1,6},{2,7},{3,4},{4,1},{5,2},{6,3},{7,0},{8,13},{9,14},{10,... | collective-permute-start | bytes 589832 | tf_op jit(solution)/shard_map/ppermute | solution.py:376
  23.7 15.2 %collective-permute-start.10 = (bf16[128,768]{1,0:T(8,128)(2,1)S(1)}, bf16[128,768]{1,0:T(8,128)(2,1)S(1)}, u32[]{:S(2)}, u32[]{:S(2)}) collective-permute-start(bf16[128,768]{1,0:T(8,128)(2,1)S(1)} %get-tuple-element.54), channel_id=1, source_target_pairs={{0,7},{1,4},{2,5},{3,6},{4,3},{5,0},{6,1},{7,2},{8,15},{9,12},{10,... | collective-permute-start | bytes 589832 | tf_op jit(solution)/shard_map/ppermute | solution.py:376
  27.4 12.9 %collective-permute-start.11 = (bf16[128,768]{1,0:T(8,128)(2,1)S(1)}, bf16[128,768]{1,0:T(8,128)(2,1)S(1)}, u32[]{:S(2)}, u32[]{:S(2)}) collective-permute-start(bf16[128,768]{1,0:T(8,128)(2,1)S(1)} %get-tuple-element.55), channel_id=1, source_target_pairs={{0,6},{1,7},{2,4},{3,5},{4,2},{5,3},{6,0},{7,1},{8,14},{9,15},{10,... | collective-permute-start | bytes 589832 | tf_op jit(solution)/shard_map/ppermute | solution.py:376
  33.2 12.1 %collective-permute-start.8 = (bf16[128,768]{1,0:T(8,128)(2,1)S(1)}, bf16[128,768]{1,0:T(8,128)(2,1)S(1)}, u32[]{:S(2)}, u32[]{:S(2)}) collective-permute-start(bf16[128,768]{1,0:T(8,128)(2,1)S(1)} %get-tuple-element.52), channel_id=1, source_target_pairs={{2,0},{3,1},{0,2},{1,3},{6,4},{7,5},{4,6},{5,7},{10,8},{11,9},{8,1... | collective-permute-start | bytes 589832 | tf_op jit(solution)/shard_map/ppermute | solution.py:376
  35.5 13.0 %collective-permute-start.9 = (bf16[128,768]{1,0:T(8,128)(2,1)S(1)}, bf16[128,768]{1,0:T(8,128)(2,1)S(1)}, u32[]{:S(2)}, u32[]{:S(2)}) collective-permute-start(bf16[128,768]{1,0:T(8,128)(2,1)S(1)} %get-tuple-element.53), channel_id=1, source_target_pairs={{5,0},{6,1},{7,2},{4,3},{1,4},{2,5},{3,6},{0,7},{13,8},{14,9},{15,... | collective-permute-start | bytes 589832 | tf_op jit(solution)/shard_map/ppermute | solution.py:376
  38.9 11.7 %collective-permute-start.3 = (bf16[128,768]{1,0:T(8,128)(2,1)S(1)}, bf16[128,768]{1,0:T(8,128)(2,1)S(1)}, u32[]{:S(2)}, u32[]{:S(2)}) collective-permute-start(bf16[128,768]{1,0:T(8,128)(2,1)S(1)} %get-tuple-element.44), channel_id=1, source_target_pairs={{1,0},{2,1},{3,2},{0,3},{5,4},{6,5},{7,6},{4,7},{9,8},{10,9},{11,1... | collective-permute-start | bytes 589832 | tf_op jit(solution)/shard_map/ppermute | solution.py:376
  38.9 11.7 %collective-permute-start.4 = (bf16[128,768]{1,0:T(8,128)(2,1)S(1)}, bf16[128,768]{1,0:T(8,128)(2,1)S(1)}, u32[]{:S(2)}, u32[]{:S(2)}) collective-permute-start(bf16[128,768]{1,0:T(8,128)(2,1)S(1)} %get-tuple-element.45), channel_id=1, source_target_pairs={{3,0},{0,1},{1,2},{2,3},{7,4},{4,5},{5,6},{6,7},{11,8},{8,9},{9,10... | collective-permute-start | bytes 589832 | tf_op jit(solution)/shard_map/ppermute | solution.py:376
  40.4 10.2 %copy-start = (bf16[256,768]{1,0:T(8,128)(2,1)S(1)}, bf16[256,768]{1,0:T(8,128)(2,1)}, u32[]{:S(2)}) copy-start(bf16[256,768]{1,0:T(8,128)(2,1)} %tokens_ref.1) | copy-start | bytes 1179652
  40.4 10.2 %collective-permute-start.5 = (bf16[128,768]{1,0:T(8,128)(2,1)S(1)}, bf16[128,768]{1,0:T(8,128)(2,1)S(1)}, u32[]{:S(2)}, u32[]{:S(2)}) collective-permute-start(bf16[128,768]{1,0:T(8,128)(2,1)S(1)} %get-tuple-element.46), channel_id=1, source_target_pairs={{4,0},{5,1},{6,2},{7,3},{0,4},{1,5},{2,6},{3,7},{12,8},{13,9},{14,... | collective-permute-start | bytes 589832 | tf_op jit(solution)/shard_map/ppermute | solution.py:376
  45.4 11.7 %copy-start.1 = (s32[1,16]{1,0:T(1,128)S(1)}, s32[1,16]{1,0:T(1,128)}, u32[]{:S(2)}) copy-start(s32[1,16]{1,0:T(1,128)} %lengths_ref.1) | copy-start | bytes 196
  45.4 8.3 %collective-permute-start.12 = (bf16[128,768]{1,0:T(8,128)(2,1)S(1)}, bf16[128,768]{1,0:T(8,128)(2,1)S(1)}, u32[]{:S(2)}, u32[]{:S(2)}) collective-permute-start(bf16[128,768]{1,0:T(8,128)(2,1)S(1)} %get-tuple-element.56), channel_id=1, source_target_pairs={{7,0},{4,1},{5,2},{6,3},{3,4},{0,5},{1,6},{2,7},{15,8},{12,9},{13,... | collective-permute-start | bytes 589832 | tf_op jit(solution)/shard_map/ppermute | solution.py:376
  48.5 8.5 %collective-permute-start.13 = (bf16[128,768]{1,0:T(8,128)(2,1)S(1)}, bf16[128,768]{1,0:T(8,128)(2,1)S(1)}, u32[]{:S(2)}, u32[]{:S(2)}) collective-permute-start(bf16[128,768]{1,0:T(8,128)(2,1)S(1)} %get-tuple-element.57), channel_id=1, source_target_pairs={{6,0},{7,1},{4,2},{5,3},{2,4},{3,5},{0,6},{1,7},{14,8},{15,9},{12,... | collective-permute-start | bytes 589832 | tf_op jit(solution)/shard_map/ppermute | solution.py:376
  74.2 14.0 %collective-permute-start.16 = (bf16[16,16,768]{2,1,0:T(8,128)(2,1)S(1)}, bf16[16,16,768]{2,1,0:T(8,128)(2,1)S(1)}, u32[]{:S(2)}, u32[]{:S(2)}) collective-permute-start(bf16[16,16,768]{2,1,0:T(8,128)(2,1)S(1)} %all_to_all.5), channel_id=1, source_target_pairs={{0,1},{1,2},{2,3},{3,0},{4,5},{5,6},{6,7},{7,4},{8,9},{9,10},{10,1... | collective-permute-start | bytes 1179656 | tf_op jit(solution)/shard_map/ppermute | solution.py:406
  75.6 18.3 %collective-permute-start.15 = (bf16[16,16,768]{2,1,0:T(8,128)(2,1)S(1)}, bf16[16,16,768]{2,1,0:T(8,128)(2,1)S(1)}, u32[]{:S(2)}, u32[]{:S(2)}) collective-permute-start(bf16[16,16,768]{2,1,0:T(8,128)(2,1)S(1)} %all_to_all.5), channel_id=1, source_target_pairs={{0,96},{8,104},{16,112},{24,120},{32,0},{40,8},{48,16},{56,24},{64... | collective-permute-start | bytes 1179656 | tf_op jit(solution)/shard_map/ppermute | solution.py:405
  75.6 18.3 %collective-permute-start.14 = (bf16[16,16,768]{2,1,0:T(8,128)(2,1)S(1)}, bf16[16,16,768]{2,1,0:T(8,128)(2,1)S(1)}, u32[]{:S(2)}, u32[]{:S(2)}) collective-permute-start(bf16[16,16,768]{2,1,0:T(8,128)(2,1)S(1)} %all_to_all.5), channel_id=1, source_target_pairs={{0,3},{1,0},{2,1},{3,2},{4,7},{5,4},{6,5},{7,6},{8,11},{9,8},{10,9... | collective-permute-start | bytes 1179656 | tf_op jit(solution)/shard_map/ppermute | solution.py:404
  77.6 16.9 %collective-permute-start.17 = (bf16[16,16,768]{2,1,0:T(8,128)(2,1)S(1)}, bf16[16,16,768]{2,1,0:T(8,128)(2,1)S(1)}, u32[]{:S(2)}, u32[]{:S(2)}) collective-permute-start(bf16[16,16,768]{2,1,0:T(8,128)(2,1)S(1)} %all_to_all.5), channel_id=1, source_target_pairs={{0,8},{8,0},{16,24},{24,16},{32,40},{40,32},{48,56},{56,48},{64,72... | collective-permute-start | bytes 1179656 | tf_op jit(solution)/shard_map/ppermute | solution.py:408
  88.2 8.3 %collective-permute-start.20 = (bf16[16,16,768]{2,1,0:T(8,128)(2,1)S(1)}, bf16[16,16,768]{2,1,0:T(8,128)(2,1)S(1)}, u32[]{:S(2)}, u32[]{:S(2)}) collective-permute-start(bf16[16,16,768]{2,1,0:T(8,128)(2,1)S(1)} %collective-permute-done.16), channel_id=1, source_target_pairs={{0,8},{8,0},{16,24},{24,16},{32,40},{40,32},{48,56},{56,48},{64,72... | collective-permute-start | bytes 1179656 | tf_op jit(solution)/shard_map/ppermute | solution.py:408
  93.9 2.5 %collective-permute-start.19 = (bf16[16,16,768]{2,1,0:T(8,128)(2,1)S(1)}, bf16[16,16,768]{2,1,0:T(8,128)(2,1)S(1)}, u32[]{:S(2)}, u32[]{:S(2)}) collective-permute-start(bf16[16,16,768]{2,1,0:T(8,128)(2,1)S(1)} %collective-permute-done.15), channel_id=1, source_target_pairs={{0,8},{8,0},{16,24},{24,16},{32,40},{40,32},{48,56},{56,48},{64,72... | collective-permute-start | bytes 1179656 | tf_op jit(solution)/shard_map/ppermute | solution.py:408
  93.9 2.5 %collective-permute-start.18 = (bf16[16,16,768]{2,1,0:T(8,128)(2,1)S(1)}, bf16[16,16,768]{2,1,0:T(8,128)(2,1)S(1)}, u32[]{:S(2)}, u32[]{:S(2)}) collective-permute-start(bf16[16,16,768]{2,1,0:T(8,128)(2,1)S(1)} %collective-permute-done.14), channel_id=1, source_target_pairs={{0,8},{8,0},{16,24},{24,16},{32,40},{40,32},{48,56},{56,48},{64,72... | collective-permute-start | bytes 1179656 | tf_op jit(solution)/shard_map/ppermute | solution.py:408

commit v11 on v9

--- a/solution.py
+++ b/solution.py
@@ -257,11 +257,11 @@
 
 
 def combine_kernel(early_ref, slots_ref, weights_ref, lengths_ref, *refs):
-    *back_refs, hidden_ref, embedded_ref, rounded_ref = refs
+    *back_refs, mixed_ref, embedded_ref, rounded_ref = refs
     rows = early_ref.shape[0]
     start = slots_ref.shape[1] - len(back_refs)
     mixed = early_ref[...] + weighted_rows(slots_ref, weights_ref, back_refs, start)
-    hidden_ref[...] = mixed.astype(bf16)
+    mixed_ref[...] = mixed
     count = lengths_ref.shape[1]
     spans = jnp.broadcast_to(lengths_ref[...], (count, count)).astype(f32)
     down, across = iota((count, count), 0), iota((count, count), 1)
@@ -336,7 +336,7 @@
     return call(
         combine_kernel,
         [
-            jax.ShapeDtypeStruct(tokens.shape, bf16),
+            jax.ShapeDtypeStruct(tokens.shape, f32),
             jax.ShapeDtypeStruct((count, width), f32),
             jax.ShapeDtypeStruct((count, width), bf16),
         ],
@@ -370,7 +370,7 @@
         results, matrices = expert_rows([incoming[move] for move in group], matrices, heads)
         heads = []
         backs += [send(x, move, back=True) for move, x in zip(group, results)]
-    hidden_out, embedded, rounded = combine(tokens, slots, weights, backs, lengths)
+    mixed, embedded, rounded = combine(tokens, slots, weights, backs, lengths)
 
     groups = lax.axis_size("dp")
     swap = [(i, i ^ 1) for i in range(groups)]
@@ -393,7 +393,7 @@
     queries = jnp.concatenate([x[:, :half] for x in blocks]).reshape(-1, width)
     docs = jnp.concatenate([x[:, half:] for x in blocks]).reshape(-1, width)
     query_grad, doc_grad = info_nce(queries, docs, embedded)
-    return (hidden_out, query_grad, doc_grad)
+    return (mixed.astype(bf16), query_grad, doc_grad)
 
 
 def solution(mesh):

time: 97.7 us -> 97.3 us (level)
  transfers between devices with their start and end apart: 21 -> 21, of which waited for: 5 -> 4; matrix products, arithmetic and copies ran while one was open for 0% -> 1% of each run, Pallas kernels for 21% -> 21%
where the time goes in v11:
time: 97.3 us; the launch traced here: 97.2 us
  starting transfers between devices  39.8 us (41%)
  Pallas kernels  27.9 us (29%)
  blocking collectives  20.7 us (21%)
  waiting for transfers between devices  6.81 us (7%)
    pallas_call x7, Pallas kernels, call(): pl.pallas_call(kernel, out_shape=outs, in_specs=[left if at in outside el...  27.9 us
    ppermute x14, starting transfers between devices, send(): return x if move == (0, 0) else lax.ppermute(x, 'expert', pairs(move, back))  27.3 us
    all_to_all x1, blocking collectives, body(): lax.all_to_all(copies, ('dp', 'expert'), split_axis=0, concat_axis=0, til...  20.7 us
    ppermute x4, starting transfers between devices, body(): blocks += [lax.ppermute(x, 'dp', swap) for x in blocks]  9.74 us
    ppermute x14, waiting for transfers between devices, send(): return x if move == (0, 0) else lax.ppermute(x, 'expert', pairs(move, back))  4.98 us
    ppermute x1, starting transfers between devices, body(): lax.ppermute(own, 'expert', pairs((3, 0), False))  2.67 us
  transfers between devices with their start and end apart: 21, of which 4 were waited for; matrix products, arithmetic and copies ran while one was open for 1% of the time, Pallas kernels for 21%

profile of v11, /device:TPU:1, one launch (start us, length us, event | category | flops | bytes accessed | tf_op | source)
XLA Modules:
  0.0 97.2 jit_solution(3798601275313967594)
XLA Ops:
  0.6 2.2 %shard_map.103 = (bf16[128,768]{1,0:T(8,128)(2,1)S(1)}, bf16[128,768]{1,0:T(8,128)(2,1)S(1)}, bf16[128,768]{1,0:T(8,128)(2,1)S(1)}, bf16[128,768]{1,0:T(8,128)(2...) custom-call(bf16[256,768]{1,0:T(8,128)(2,1)} %tokens_ref.1, ...), custom_call_target="tpu_custom_call" | custom-call | tf_op jit(solution)/shard_map/pallas_call | solution.py:65
  2.8 2.1 %collective-permute-start = (bf16[128,768]{1,0:T(8,128)(2,1)S(1)}, bf16[128,768]{1,0:T(8,128)(2,1)S(1)}, u32[]{:S(2)}, u32[]{:S(2)}) collective-permute-start(bf16[128,768]{1,0:T(8,128)(2,1)S(1)} %get-tuple-element.34), channel_id=1, source_target_pairs={{0,1},{1,2},{2,3},{3,0},{4,5},{5,6},{6,7},{7,4},{8,9},{9,10},{10,1... | collective-permute-start | bytes 589832 | tf_op jit(solution)/shard_map/ppermute | solution.py:365
  5.0 1.3 %collective-permute-start.1 = (bf16[128,768]{1,0:T(8,128)(2,1)S(1)}, bf16[128,768]{1,0:T(8,128)(2,1)S(1)}, u32[]{:S(2)}, u32[]{:S(2)}) collective-permute-start(bf16[128,768]{1,0:T(8,128)(2,1)S(1)} %get-tuple-element.35), channel_id=1, source_target_pairs={{0,3},{1,0},{2,1},{3,2},{4,7},{5,4},{6,5},{7,6},{8,11},{9,8},{10,9... | collective-permute-start | bytes 589832 | tf_op jit(solution)/shard_map/ppermute | solution.py:365
  6.3 3.7 %collective-permute-start.2 = (bf16[128,768]{1,0:T(8,128)(2,1)S(1)}, bf16[128,768]{1,0:T(8,128)(2,1)S(1)}, u32[]{:S(2)}, u32[]{:S(2)}) collective-permute-start(bf16[128,768]{1,0:T(8,128)(2,1)S(1)} %get-tuple-element.36), channel_id=1, source_target_pairs={{0,4},{1,5},{2,6},{3,7},{4,0},{5,1},{6,2},{7,3},{8,12},{9,13},{10,... | collective-permute-start | bytes 589832 | tf_op jit(solution)/shard_map/ppermute | solution.py:365
  10.0 1.5 %collective-permute-start.6 = (bf16[128,768]{1,0:T(8,128)(2,1)S(1)}, bf16[128,768]{1,0:T(8,128)(2,1)S(1)}, u32[]{:S(2)}, u32[]{:S(2)}) collective-permute-start(bf16[128,768]{1,0:T(8,128)(2,1)S(1)} %get-tuple-element.43), channel_id=1, source_target_pairs={{0,2},{1,3},{2,0},{3,1},{4,6},{5,7},{6,4},{7,5},{8,10},{9,11},{10,... | collective-permute-start | bytes 589832 | tf_op jit(solution)/shard_map/ppermute | solution.py:365
  11.6 0.0 collective-permute-start.7
  11.6 5.1 %collective-permute-start.10 = (bf16[128,768]{1,0:T(8,128)(2,1)S(1)}, bf16[128,768]{1,0:T(8,128)(2,1)S(1)}, u32[]{:S(2)}, u32[]{:S(2)}) collective-permute-start(bf16[128,768]{1,0:T(8,128)(2,1)S(1)} %get-tuple-element.50), channel_id=1, source_target_pairs={{0,7},{1,4},{2,5},{3,6},{4,3},{5,0},{6,1},{7,2},{8,15},{9,12},{10,... | collective-permute-start | bytes 589832 | tf_op jit(solution)/shard_map/ppermute | solution.py:365
  16.6 9.7 %shard_map.104 = (bf16[128,768]{1,0:T(8,128)(2,1)S(1)}, bf16[128,768]{1,0:T(8,128)(2,1)S(1)}, bf16[128,768]{1,0:T(8,128)(2,1)S(1)}, bf16[128,768]{1,0:T(8,128)(2...) custom-call(bf16[128,768]{1,0:T(8,128)(2,1)S(1)} %get-tuple-element., ...), custom_call_target="tpu_custom_call", output_to_operand_aliasing={{4}: (7, {}), {5}: (8, {})} | custom-call | tf_op jit(solution)/shard_map/pallas_call | solution.py:65
  26.4 1.0 %collective-permute-done.7.refs_1_ = bf16[128,768]{1,0:T(8,128)(2,1)S(1)} collective-permute-done((bf16[128,768]{1,0:T(8,128)(2,1)S(1)}, bf16[128,768]{1,0:T(8,128)(2,1)S(1)}, u32[]{:S(2)}, u32[]{:S(2)}) %collective-permute-start.7) | collective-permute-done | bytes 196640 | tf_op jit(solution)/shard_map/ppermute | solution.py:365
  27.4 5.0 %shard_map.105 = (bf16[128,768]{1,0:T(8,128)(2,1)S(1)}, bf16[128,768]{1,0:T(8,128)(2,1)S(1)}) custom-call(bf16[128,768]{1,0:T(8,128)(2,1)S(1)} %collective-permute-done.6.refs_0_, bf16[128,768]{1,0:T(8,128)(2,1)S(1)} %collective-permute-done.7.refs_1_, bf16[768,3072]{1,0:T(8,128)(2,1)S(1)} %get-tuple-element.45.refs_2_, ...), custom_call_target="tpu_custom_call" | custom-call | tf_op jit(solution)/shard_map/pallas_call | solution.py:65
  32.3 1.7 %collective-permute-start.8 = (bf16[128,768]{1,0:T(8,128)(2,1)S(1)}, bf16[128,768]{1,0:T(8,128)(2,1)S(1)}, u32[]{:S(2)}, u32[]{:S(2)}) collective-permute-start(bf16[128,768]{1,0:T(8,128)(2,1)S(1)} %get-tuple-element.48), channel_id=1, source_target_pairs={{2,0},{3,1},{0,2},{1,3},{6,4},{7,5},{4,6},{5,7},{10,8},{11,9},{8,1... | collective-permute-start | bytes 589832 | tf_op jit(solution)/shard_map/ppermute | solution.py:365
  34.1 2.4 %collective-permute-start.9 = (bf16[128,768]{1,0:T(8,128)(2,1)S(1)}, bf16[128,768]{1,0:T(8,128)(2,1)S(1)}, u32[]{:S(2)}, u32[]{:S(2)}) collective-permute-start(bf16[128,768]{1,0:T(8,128)(2,1)S(1)} %get-tuple-element.49), channel_id=1, source_target_pairs={{5,0},{6,1},{7,2},{4,3},{1,4},{2,5},{3,6},{0,7},{13,8},{14,9},{15,... | collective-permute-start | bytes 589832 | tf_op jit(solution)/shard_map/ppermute | solution.py:365
  36.4 3.1 %collective-permute-start.3 = (bf16[128,768]{1,0:T(8,128)(2,1)S(1)}, bf16[128,768]{1,0:T(8,128)(2,1)S(1)}, u32[]{:S(2)}, u32[]{:S(2)}) collective-permute-start(bf16[128,768]{1,0:T(8,128)(2,1)S(1)} %get-tuple-element.40), channel_id=1, source_target_pairs={{1,0},{2,1},{3,2},{0,3},{5,4},{6,5},{7,6},{4,7},{9,8},{10,9},{11,1... | collective-permute-start | bytes 589832 | tf_op jit(solution)/shard_map/ppermute | solution.py:365
  39.6 0.0 copy-start
  39.6 0.1 collective-permute-start.5
  39.7 4.9 %shard_map.107 = (bf16[128,768]{1,0:T(8,128)(2,1)S(1)}, bf16[128,768]{1,0:T(8,128)(2,1)S(1)}) custom-call(bf16[128,768]{1,0:T(8,128)(2,1)S(1)} %collective-permute-done.10.refs_0_, bf16[128,768]{1,0:T(8,128)(2,1)S(1)} %collective-permute-done.11.refs_1_, bf16[768,3072]{1,0:T(8,128)(2,1)S(1)} %get-tuple-element.45.refs_2_, ...), custom_call_target="tpu_custom_call" | custom-call | tf_op jit(solution)/shard_map/pallas_call | solution.py:65
  44.6 0.0 copy-start.1
  44.6 2.8 %collective-permute-start.12 = (bf16[128,768]{1,0:T(8,128)(2,1)S(1)}, bf16[128,768]{1,0:T(8,128)(2,1)S(1)}, u32[]{:S(2)}, u32[]{:S(2)}) collective-permute-start(bf16[128,768]{1,0:T(8,128)(2,1)S(1)} %get-tuple-element.52), channel_id=1, source_target_pairs={{7,0},{4,1},{5,2},{6,3},{3,4},{0,5},{1,6},{2,7},{15,8},{12,9},{13,... | collective-permute-start | bytes 589832 | tf_op jit(solution)/shard_map/ppermute | solution.py:365
  47.4 3.5 %collective-permute-start.13 = (bf16[128,768]{1,0:T(8,128)(2,1)S(1)}, bf16[128,768]{1,0:T(8,128)(2,1)S(1)}, u32[]{:S(2)}, u32[]{:S(2)}) collective-permute-start(bf16[128,768]{1,0:T(8,128)(2,1)S(1)} %get-tuple-element.53), channel_id=1, source_target_pairs={{6,0},{7,1},{4,2},{5,3},{2,4},{3,5},{0,6},{1,7},{14,8},{15,9},{12,... | collective-permute-start | bytes 589832 | tf_op jit(solution)/shard_map/ppermute | solution.py:365
  50.9 1.2 %shard_map.106.early_ref = f32[256,768]{1,0:T(8,128)S(1)} custom-call(bf16[256,768]{1,0:T(8,128)(2,1)S(1)} %copy-done, f32[256,8]{1,0:T(8,128)S(1)} %get-tuple-element.31.slots_ref, f32[256,8]{1,0:T(8,128)S(1)} %get-tuple-element.32.weights_ref, bf16[128,768]{1,0:T(8,128)(2,1)S(1)} %get-tuple-element.39.refs_0_, ...), custom_call_target="tpu_custom_call" | custom-call | tf_op jit(solution)/shard_map/pallas_call | solution.py:65
  52.2 0.9 collective-permute-done.12.refs_0_
  53.0 3.1 %collective-permute-done.13.refs_1_ = bf16[128,768]{1,0:T(8,128)(2,1)S(1)} collective-permute-done((bf16[128,768]{1,0:T(8,128)(2,1)S(1)}, bf16[128,768]{1,0:T(8,128)(2,1)S(1)}, u32[]{:S(2)}, u32[]{:S(2)}) %collective-permute-start.13) | collective-permute-done | bytes 196640 | tf_op jit(solution)/shard_map/ppermute | solution.py:365
  56.1 1.1 %shard_map.108 = (f32[256,768]{1,0:T(8,128)S(1)}, f32[16,768]{1,0:T(8,128)S(1)}, bf16[16,768]{1,0:T(8,128)(2,1)S(1)}) custom-call(f32[256,768]{1,0:T(8,128)S(1)} %shard_map.106.early_ref, f32[256,8]{1,0:T(8,128)S(1)} %get-tuple-element.31.slots_ref, f32[256,8]{1,0:T(8,128)S(1)} %get-tuple-element.32.weights_ref, s32[1,16]{1,0:T(1,128)S(1)} %copy-done.1, ...), custom_call_target="tpu_custom_call" | custom-call | tf_op jit(solution)/shard_map/pallas_call | solution.py:65
  57.2 20.7 %all_to_all.5 = bf16[16,16,768]{2,1,0:T(8,128)(2,1)S(1)} all-to-all(bf16[16,16,768]{2,1,0:T(8,128)(2,1)S(1)} %broadcast_in_dim.2), channel_id=1, replica_groups={{0,4,16,20,34,38,50,54,64,68,80,84,98,102,114,118},{8,12,24,28,42,46,58..., dimensions={0} | all-to-all | bytes 786432 | tf_op jit(solution)/shard_map/all_to_all | solution.py:382
  78.0 2.7 %collective-permute-start.14 = (bf16[16,16,768]{2,1,0:T(8,128)(2,1)S(1)}, bf16[16,16,768]{2,1,0:T(8,128)(2,1)S(1)}, u32[]{:S(2)}, u32[]{:S(2)}) collective-permute-start(bf16[16,16,768]{2,1,0:T(8,128)(2,1)S(1)} %all_to_all.5), channel_id=1, source_target_pairs={{0,3},{1,0},{2,1},{3,2},{4,7},{5,4},{6,5},{7,6},{8,11},{9,8},{10,9... | collective-permute-start | bytes 1179656 | tf_op jit(solution)/shard_map/ppermute | solution.py:387
  80.7 0.8 convert_element_type.3
  81.4 4.9 %collective-permute-start.17 = (bf16[16,16,768]{2,1,0:T(8,128)(2,1)S(1)}, bf16[16,16,768]{2,1,0:T(8,128)(2,1)S(1)}, u32[]{:S(2)}, u32[]{:S(2)}) collective-permute-start(bf16[16,16,768]{2,1,0:T(8,128)(2,1)S(1)} %all_to_all.5), channel_id=1, source_target_pairs={{0,8},{8,0},{16,24},{24,16},{32,40},{40,32},{48,56},{56,48},{64,72... | collective-permute-start | bytes 1179656 | tf_op jit(solution)/shard_map/ppermute | solution.py:391
  86.4 4.3 %collective-permute-start.20 = (bf16[16,16,768]{2,1,0:T(8,128)(2,1)S(1)}, bf16[16,16,768]{2,1,0:T(8,128)(2,1)S(1)}, u32[]{:S(2)}, u32[]{:S(2)}) collective-permute-start(bf16[16,16,768]{2,1,0:T(8,128)(2,1)S(1)} %collective-permute-done.16), channel_id=1, source_target_pairs={{0,8},{8,0},{16,24},{24,16},{32,40},{40,32},{48,56},{56,48},{64,72... | collective-permute-start | bytes 1179656 | tf_op jit(solution)/shard_map/ppermute | solution.py:391
  90.7 0.0 collective-permute-start.19
  90.7 0.5 collective-permute-start.18
  91.4 1.8 %collective-permute-done.18 = bf16[16,16,768]{2,1,0:T(8,128)(2,1)S(1)} collective-permute-done((bf16[16,16,768]{2,1,0:T(8,128)(2,1)S(1)}, bf16[16,16,768]{2,1,0:T(8,128)(2,1)S(1)}, u32[]{:S(2)}, u32[]{:S(2)}) %collective-permute-start.18) | collective-permute-done | bytes 393248 | tf_op jit(solution)/shard_map/ppermute | solution.py:391
  93.3 3.8 %shard_map.109 = (f32[8,768]{1,0:T(8,128)}, f32[8,768]{1,0:T(8,128)}) custom-call(bf16[1024,768]{1,0:T(8,128)(2,1)S(1)} %bitcast.8, bf16[1024,768]{1,0:T(8,128)(2,1)S(1)} %bitcast.7, f32[16,768]{1,0:T(8,128)S(1)} %get-tuple-element.56.embedded_ref), custom_call_target="tpu_custom_call" | custom-call | tf_op jit(solution)/shard_map/pallas_call | solution.py:65
  (32 shorter events, 0.3 us)
Async XLA Ops:
  2.8 8.7 %collective-permute-start = (bf16[128,768]{1,0:T(8,128)(2,1)S(1)}, bf16[128,768]{1,0:T(8,128)(2,1)S(1)}, u32[]{:S(2)}, u32[]{:S(2)}) collective-permute-start(bf16[128,768]{1,0:T(8,128)(2,1)S(1)} %get-tuple-element.34), channel_id=1, source_target_pairs={{0,1},{1,2},{2,3},{3,0},{4,5},{5,6},{6,7},{7,4},{8,9},{9,10},{10,1... | collective-permute-start | bytes 589832 | tf_op jit(solution)/shard_map/ppermute | solution.py:365
  5.0 11.7 %collective-permute-start.1 = (bf16[128,768]{1,0:T(8,128)(2,1)S(1)}, bf16[128,768]{1,0:T(8,128)(2,1)S(1)}, u32[]{:S(2)}, u32[]{:S(2)}) collective-permute-start(bf16[128,768]{1,0:T(8,128)(2,1)S(1)} %get-tuple-element.35), channel_id=1, source_target_pairs={{0,3},{1,0},{2,1},{3,2},{4,7},{5,4},{6,5},{7,6},{8,11},{9,8},{10,9... | collective-permute-start | bytes 589832 | tf_op jit(solution)/shard_map/ppermute | solution.py:365
  6.3 10.3 %collective-permute-start.2 = (bf16[128,768]{1,0:T(8,128)(2,1)S(1)}, bf16[128,768]{1,0:T(8,128)(2,1)S(1)}, u32[]{:S(2)}, u32[]{:S(2)}) collective-permute-start(bf16[128,768]{1,0:T(8,128)(2,1)S(1)} %get-tuple-element.36), channel_id=1, source_target_pairs={{0,4},{1,5},{2,6},{3,7},{4,0},{5,1},{6,2},{7,3},{8,12},{9,13},{10,... | collective-permute-start | bytes 589832 | tf_op jit(solution)/shard_map/ppermute | solution.py:365
  10.0 16.3 %collective-permute-start.6 = (bf16[128,768]{1,0:T(8,128)(2,1)S(1)}, bf16[128,768]{1,0:T(8,128)(2,1)S(1)}, u32[]{:S(2)}, u32[]{:S(2)}) collective-permute-start(bf16[128,768]{1,0:T(8,128)(2,1)S(1)} %get-tuple-element.43), channel_id=1, source_target_pairs={{0,2},{1,3},{2,0},{3,1},{4,6},{5,7},{6,4},{7,5},{8,10},{9,11},{10,... | collective-permute-start | bytes 589832 | tf_op jit(solution)/shard_map/ppermute | solution.py:365
  11.6 15.8 %collective-permute-start.7 = (bf16[128,768]{1,0:T(8,128)(2,1)S(1)}, bf16[128,768]{1,0:T(8,128)(2,1)S(1)}, u32[]{:S(2)}, u32[]{:S(2)}) collective-permute-start(bf16[128,768]{1,0:T(8,128)(2,1)S(1)} %get-tuple-element.44), channel_id=1, source_target_pairs={{0,5},{1,6},{2,7},{3,4},{4,1},{5,2},{6,3},{7,0},{8,13},{9,14},{10,... | collective-permute-start | bytes 589832 | tf_op jit(solution)/shard_map/ppermute | solution.py:365
  11.6 28.0 %collective-permute-start.10 = (bf16[128,768]{1,0:T(8,128)(2,1)S(1)}, bf16[128,768]{1,0:T(8,128)(2,1)S(1)}, u32[]{:S(2)}, u32[]{:S(2)}) collective-permute-start(bf16[128,768]{1,0:T(8,128)(2,1)S(1)} %get-tuple-element.50), channel_id=1, source_target_pairs={{0,7},{1,4},{2,5},{3,6},{4,3},{5,0},{6,1},{7,2},{8,15},{9,12},{10,... | collective-permute-start | bytes 589832 | tf_op jit(solution)/shard_map/ppermute | solution.py:365
  16.6 22.9 %collective-permute-start.11 = (bf16[128,768]{1,0:T(8,128)(2,1)S(1)}, bf16[128,768]{1,0:T(8,128)(2,1)S(1)}, u32[]{:S(2)}, u32[]{:S(2)}) collective-permute-start(bf16[128,768]{1,0:T(8,128)(2,1)S(1)} %get-tuple-element.51), channel_id=1, source_target_pairs={{0,6},{1,7},{2,4},{3,5},{4,2},{5,3},{6,0},{7,1},{8,14},{9,15},{10,... | collective-permute-start | bytes 589832 | tf_op jit(solution)/shard_map/ppermute | solution.py:365
  32.3 12.3 %collective-permute-start.8 = (bf16[128,768]{1,0:T(8,128)(2,1)S(1)}, bf16[128,768]{1,0:T(8,128)(2,1)S(1)}, u32[]{:S(2)}, u32[]{:S(2)}) collective-permute-start(bf16[128,768]{1,0:T(8,128)(2,1)S(1)} %get-tuple-element.48), channel_id=1, source_target_pairs={{2,0},{3,1},{0,2},{1,3},{6,4},{7,5},{4,6},{5,7},{10,8},{11,9},{8,1... | collective-permute-start | bytes 589832 | tf_op jit(solution)/shard_map/ppermute | solution.py:365
  34.1 13.3 %collective-permute-start.9 = (bf16[128,768]{1,0:T(8,128)(2,1)S(1)}, bf16[128,768]{1,0:T(8,128)(2,1)S(1)}, u32[]{:S(2)}, u32[]{:S(2)}) collective-permute-start(bf16[128,768]{1,0:T(8,128)(2,1)S(1)} %get-tuple-element.49), channel_id=1, source_target_pairs={{5,0},{6,1},{7,2},{4,3},{1,4},{2,5},{3,6},{0,7},{13,8},{14,9},{15,... | collective-permute-start | bytes 589832 | tf_op jit(solution)/shard_map/ppermute | solution.py:365
  36.4 14.5 %collective-permute-start.3 = (bf16[128,768]{1,0:T(8,128)(2,1)S(1)}, bf16[128,768]{1,0:T(8,128)(2,1)S(1)}, u32[]{:S(2)}, u32[]{:S(2)}) collective-permute-start(bf16[128,768]{1,0:T(8,128)(2,1)S(1)} %get-tuple-element.40), channel_id=1, source_target_pairs={{1,0},{2,1},{3,2},{0,3},{5,4},{6,5},{7,6},{4,7},{9,8},{10,9},{11,1... | collective-permute-start | bytes 589832 | tf_op jit(solution)/shard_map/ppermute | solution.py:365
  39.5 11.4 %collective-permute-start.4 = (bf16[128,768]{1,0:T(8,128)(2,1)S(1)}, bf16[128,768]{1,0:T(8,128)(2,1)S(1)}, u32[]{:S(2)}, u32[]{:S(2)}) collective-permute-start(bf16[128,768]{1,0:T(8,128)(2,1)S(1)} %get-tuple-element.41), channel_id=1, source_target_pairs={{3,0},{0,1},{1,2},{2,3},{7,4},{4,5},{5,6},{6,7},{11,8},{8,9},{9,10... | collective-permute-start | bytes 589832 | tf_op jit(solution)/shard_map/ppermute | solution.py:365
  39.6 11.4 %copy-start = (bf16[256,768]{1,0:T(8,128)(2,1)S(1)}, bf16[256,768]{1,0:T(8,128)(2,1)}, u32[]{:S(2)}) copy-start(bf16[256,768]{1,0:T(8,128)(2,1)} %tokens_ref.1) | copy-start | bytes 1179652
  39.6 11.4 %collective-permute-start.5 = (bf16[128,768]{1,0:T(8,128)(2,1)S(1)}, bf16[128,768]{1,0:T(8,128)(2,1)S(1)}, u32[]{:S(2)}, u32[]{:S(2)}) collective-permute-start(bf16[128,768]{1,0:T(8,128)(2,1)S(1)} %get-tuple-element.42), channel_id=1, source_target_pairs={{4,0},{5,1},{6,2},{7,3},{0,4},{1,5},{2,6},{3,7},{12,8},{13,9},{14,... | collective-permute-start | bytes 589832 | tf_op jit(solution)/shard_map/ppermute | solution.py:365
  44.6 11.5 %copy-start.1 = (s32[1,16]{1,0:T(1,128)S(1)}, s32[1,16]{1,0:T(1,128)}, u32[]{:S(2)}) copy-start(s32[1,16]{1,0:T(1,128)} %lengths_ref.1) | copy-start | bytes 196
  44.6 8.4 %collective-permute-start.12 = (bf16[128,768]{1,0:T(8,128)(2,1)S(1)}, bf16[128,768]{1,0:T(8,128)(2,1)S(1)}, u32[]{:S(2)}, u32[]{:S(2)}) collective-permute-start(bf16[128,768]{1,0:T(8,128)(2,1)S(1)} %get-tuple-element.52), channel_id=1, source_target_pairs={{7,0},{4,1},{5,2},{6,3},{3,4},{0,5},{1,6},{2,7},{15,8},{12,9},{13,... | collective-permute-start | bytes 589832 | tf_op jit(solution)/shard_map/ppermute | solution.py:365
  47.4 8.7 %collective-permute-start.13 = (bf16[128,768]{1,0:T(8,128)(2,1)S(1)}, bf16[128,768]{1,0:T(8,128)(2,1)S(1)}, u32[]{:S(2)}, u32[]{:S(2)}) collective-permute-start(bf16[128,768]{1,0:T(8,128)(2,1)S(1)} %get-tuple-element.53), channel_id=1, source_target_pairs={{6,0},{7,1},{4,2},{5,3},{2,4},{3,5},{0,6},{1,7},{14,8},{15,9},{12,... | collective-permute-start | bytes 589832 | tf_op jit(solution)/shard_map/ppermute | solution.py:365
  78.0 8.4 %collective-permute-start.16 = (bf16[16,16,768]{2,1,0:T(8,128)(2,1)S(1)}, bf16[16,16,768]{2,1,0:T(8,128)(2,1)S(1)}, u32[]{:S(2)}, u32[]{:S(2)}) collective-permute-start(bf16[16,16,768]{2,1,0:T(8,128)(2,1)S(1)} %all_to_all.5), channel_id=1, source_target_pairs={{0,1},{1,2},{2,3},{3,0},{4,5},{5,6},{6,7},{7,4},{8,9},{9,10},{10,1... | collective-permute-start | bytes 1179656 | tf_op jit(solution)/shard_map/ppermute | solution.py:389
  78.0 12.7 %collective-permute-start.15 = (bf16[16,16,768]{2,1,0:T(8,128)(2,1)S(1)}, bf16[16,16,768]{2,1,0:T(8,128)(2,1)S(1)}, u32[]{:S(2)}, u32[]{:S(2)}) collective-permute-start(bf16[16,16,768]{2,1,0:T(8,128)(2,1)S(1)} %all_to_all.5), channel_id=1, source_target_pairs={{0,96},{8,104},{16,112},{24,120},{32,0},{40,8},{48,16},{56,24},{64... | collective-permute-start | bytes 1179656 | tf_op jit(solution)/shard_map/ppermute | solution.py:388
  78.0 12.7 %collective-permute-start.14 = (bf16[16,16,768]{2,1,0:T(8,128)(2,1)S(1)}, bf16[16,16,768]{2,1,0:T(8,128)(2,1)S(1)}, u32[]{:S(2)}, u32[]{:S(2)}) collective-permute-start(bf16[16,16,768]{2,1,0:T(8,128)(2,1)S(1)} %all_to_all.5), channel_id=1, source_target_pairs={{0,3},{1,0},{2,1},{3,2},{4,7},{5,4},{6,5},{7,6},{8,11},{9,8},{10,9... | collective-permute-start | bytes 1179656 | tf_op jit(solution)/shard_map/ppermute | solution.py:387
  81.4 9.9 %collective-permute-start.17 = (bf16[16,16,768]{2,1,0:T(8,128)(2,1)S(1)}, bf16[16,16,768]{2,1,0:T(8,128)(2,1)S(1)}, u32[]{:S(2)}, u32[]{:S(2)}) collective-permute-start(bf16[16,16,768]{2,1,0:T(8,128)(2,1)S(1)} %all_to_all.5), channel_id=1, source_target_pairs={{0,8},{8,0},{16,24},{24,16},{32,40},{40,32},{48,56},{56,48},{64,72... | collective-permute-start | bytes 1179656 | tf_op jit(solution)/shard_map/ppermute | solution.py:391
  86.4 6.8 %collective-permute-start.20 = (bf16[16,16,768]{2,1,0:T(8,128)(2,1)S(1)}, bf16[16,16,768]{2,1,0:T(8,128)(2,1)S(1)}, u32[]{:S(2)}, u32[]{:S(2)}) collective-permute-start(bf16[16,16,768]{2,1,0:T(8,128)(2,1)S(1)} %collective-permute-done.16), channel_id=1, source_target_pairs={{0,8},{8,0},{16,24},{24,16},{32,40},{40,32},{48,56},{56,48},{64,72... | collective-permute-start | bytes 1179656 | tf_op jit(solution)/shard_map/ppermute | solution.py:391
  90.7 2.5 %collective-permute-start.19 = (bf16[16,16,768]{2,1,0:T(8,128)(2,1)S(1)}, bf16[16,16,768]{2,1,0:T(8,128)(2,1)S(1)}, u32[]{:S(2)}, u32[]{:S(2)}) collective-permute-start(bf16[16,16,768]{2,1,0:T(8,128)(2,1)S(1)} %collective-permute-done.15), channel_id=1, source_target_pairs={{0,8},{8,0},{16,24},{24,16},{32,40},{40,32},{48,56},{56,48},{64,72... | collective-permute-start | bytes 1179656 | tf_op jit(solution)/shard_map/ppermute | solution.py:391
  90.7 2.5 %collective-permute-start.18 = (bf16[16,16,768]{2,1,0:T(8,128)(2,1)S(1)}, bf16[16,16,768]{2,1,0:T(8,128)(2,1)S(1)}, u32[]{:S(2)}, u32[]{:S(2)}) collective-permute-start(bf16[16,16,768]{2,1,0:T(8,128)(2,1)S(1)} %collective-permute-done.14), channel_id=1, source_target_pairs={{0,8},{8,0},{16,24},{24,16},{32,40},{40,32},{48,56},{56,48},{64,72... | collective-permute-start | bytes 1179656 | tf_op jit(solution)/shard_map/ppermute | solution.py:391

commit v12 on v11

--- a/solution.py
+++ b/solution.py
@@ -277,22 +277,39 @@
     rounded_ref[...] = embedded.astype(bf16)
 
 
-def gradient_kernel(queries_ref, docs_ref, embedded_ref, query_grad_ref, doc_grad_ref):
+def exp_sums(docs_ref, queries_ref):
+    scores = dot_nt(docs_ref[...], queries_ref[...])
+    return jnp.sum(jnp.exp(logit_scale * scores), axis=0, keepdims=True)
+
+
+def own_scores(embedded, docs_ref, queries_ref):
+    stacked = jnp.concatenate(split(embedded), axis=0)
+    count = embedded.shape[0] // 2
+    return fold(dot_nt(stacked, docs_ref[...]))[:count], fold(dot_nt(stacked, queries_ref[...]))[count:]
+
+
+def early_gradient_kernel(queries_ref, docs_ref, embedded_ref, _, sums_ref, rows_ref, cols_ref):
+    sums_ref[...] = exp_sums(docs_ref, queries_ref)
+    rows_ref[...], cols_ref[...] = own_scores(embedded_ref[...], docs_ref, queries_ref)
+
+
+def gradient_kernel(
+    queries_ref, docs_ref, more_queries_ref, more_docs_ref, embedded_ref, sums_ref, rows_ref, cols_ref,
+    query_grad_ref, doc_grad_ref,
+):
     rank = lax.axis_index("dp") // 2 * (lax.axis_size("expert") // plane) + lax.axis_index("expert") // plane
-    first = rank * (embedded_ref.shape[0] // 2)
     embedded = embedded_ref[...]
     count = embedded.shape[0] // 2
-    total = queries_ref.shape[0]
+    first = rank * count
+    here = queries_ref.shape[0]
+    total = 2 * here
     queries, documents = embedded[:count], embedded[count:]
-    all_queries, all_docs = queries_ref[...], docs_ref[...]
-    block = 256
-    sums = jnp.zeros((1, total), f32)
-    for at in range(0, total, block):
-        scores = dot_nt(docs_ref[at : at + block, :], all_queries)
-        sums = sums + jnp.sum(jnp.exp(logit_scale * scores), axis=0, keepdims=True)
-    stacked = jnp.concatenate(split(embedded), axis=0)
-    rows = fold(dot_nt(stacked, all_docs))[:count]
-    cols = fold(dot_nt(stacked, all_queries))[count:]
+    sums = sums_ref[...] + exp_sums(more_docs_ref, queries_ref)
+    more_sums = exp_sums(docs_ref, more_queries_ref) + exp_sums(more_docs_ref, more_queries_ref)
+    sums = jnp.concatenate([sums, more_sums], axis=1)
+    more_rows, more_cols = own_scores(embedded, more_docs_ref, more_queries_ref)
+    rows = jnp.concatenate([rows_ref[...], more_rows], axis=1)
+    cols = jnp.concatenate([cols_ref[...], more_cols], axis=1)
     own = iota((count, total), 1) == first + iota((count, total), 0)
     pair = jnp.exp(logit_scale * jnp.sum(queries * documents, axis=-1, keepdims=True))
     rows = jnp.where(own, 0.0, jnp.exp(logit_scale * rows))
@@ -301,8 +318,11 @@
     diagonal = pair / row_sum - 1.0
     likely = jnp.concatenate([rows / row_sum, cols / sums], axis=0)
     likely = jnp.concatenate(split(likely), axis=0)
-    query_grad_ref[...] = logit_scale * (fold(dot(likely, all_docs))[:count] + diagonal * documents)
-    doc_grad_ref[...] = logit_scale * (fold(dot(likely, all_queries))[count:] + diagonal * queries)
+    near, far = likely[:, :here], likely[:, here:]
+    by_docs = fold(dot(near, docs_ref[...]) + dot(far, more_docs_ref[...]))[:count]
+    by_queries = fold(dot(near, queries_ref[...]) + dot(far, more_queries_ref[...]))[count:]
+    query_grad_ref[...] = logit_scale * (by_docs + diagonal * documents)
+    doc_grad_ref[...] = logit_scale * (by_queries + diagonal * queries)
 
 
 def route(tokens, routes, norm_gain, router_weight, gate, up):
@@ -344,9 +364,18 @@
     )
 
 
-def info_nce(queries, docs, embedded):
-    out = jax.ShapeDtypeStruct((embedded.shape[0] // 2, embedded.shape[1]), f32)
-    return call(gradient_kernel, [out, out], queries, docs, embedded)
+def info_nce(queries, docs, more_queries, more_docs, embedded, after):
+    count, here = embedded.shape[0] // 2, queries.shape[0]
+    scores = jax.ShapeDtypeStruct((count, here), f32)
+    early = call(
+        early_gradient_kernel,
+        [jax.ShapeDtypeStruct((1, here), f32), scores, scores],
+        queries, docs, embedded, after,
+    )
+    out = jax.ShapeDtypeStruct((count, embedded.shape[1]), f32)
+    return call(
+        gradient_kernel, [out, out], queries, docs, more_queries, more_docs, embedded, *early
+    )
 
 
 def body(tokens, routes, lengths, norm_gain, router_weight, gate_weight, up_weight, down_weight):
@@ -388,11 +417,15 @@
         lax.ppermute(own, "dp", [(i, (i - line) % groups) for i in range(groups)]),
         lax.ppermute(own, "expert", pairs((1, 0), False)),
     ]
-    blocks += [lax.ppermute(x, "dp", swap) for x in blocks]
+    more = [lax.ppermute(x, "dp", swap) for x in blocks]
     half = rounded.shape[0] // 2
-    queries = jnp.concatenate([x[:, :half] for x in blocks]).reshape(-1, width)
-    docs = jnp.concatenate([x[:, half:] for x in blocks]).reshape(-1, width)
-    query_grad, doc_grad = info_nce(queries, docs, embedded)
+
+    def apart(xs):
+        return [
+            jnp.concatenate([x[:, at : at + half] for x in xs]).reshape(-1, width) for at in (0, half)
+        ]
+
+    query_grad, doc_grad = info_nce(*apart(blocks), *apart(more), embedded, more[0])
     return (mixed.astype(bf16), query_grad, doc_grad)
 
 

time: 97.3 us -> 96.8 us (level)
  waiting for transfers between devices: 6.81 us -> 5.03 us
    ppermute x4, waiting for transfers between devices: 1.81 us -> 0.04 us  [body(): more = [lax.ppermute(x, 'dp', swap) for x in blocks]]
    pallas_call x7 -> x8, Pallas kernels: 27.9 us -> 28 us  [call(): pl.pallas_call(kernel, out_shape=outs, in_specs=[left if at in outside el...]
  transfers between devices with their start and end apart: 21 -> 21, of which waited for: 4 -> 3; matrix products, arithmetic and copies ran while one was open for 1% -> 1% of each run, Pallas kernels for 21% -> 22%
where the time goes in v12:
time: 96.8 us; the launch traced here: 96.5 us
  starting transfers between devices  40.2 us (42%)
  Pallas kernels  28 us (29%)
  blocking collectives  20.7 us (21%)
  waiting for transfers between devices  5.03 us (5%)
  other arithmetic  1.18 us (1%)
    pallas_call x8, Pallas kernels, call(): pl.pallas_call(kernel, out_shape=outs, in_specs=[left if at in outside el...  28 us
    ppermute x14, starting transfers between devices, send(): return x if move == (0, 0) else lax.ppermute(x, 'expert', pairs(move, back))  27.3 us
    all_to_all x1, blocking collectives, body(): lax.all_to_all(copies, ('dp', 'expert'), split_axis=0, concat_axis=0, til...  20.7 us
    ppermute x4, starting transfers between devices, body(): more = [lax.ppermute(x, 'dp', swap) for x in blocks]  10.2 us
    ppermute x14, waiting for transfers between devices, send(): return x if move == (0, 0) else lax.ppermute(x, 'expert', pairs(move, back))  4.99 us
    ppermute x1, starting transfers between devices, body(): lax.ppermute(own, 'expert', pairs((3, 0), False))  2.67 us
  transfers between devices with their start and end apart: 21, of which 3 were waited for; matrix products, arithmetic and copies ran while one was open for 1% of the time, Pallas kernels for 22%

profile of v12, /device:TPU:1, one launch (start us, length us, event | category | flops | bytes accessed | tf_op | source)
XLA Modules:
  0.0 96.5 jit_solution(3968581250888221163)
XLA Ops:
  0.6 2.2 %shard_map.103 = (bf16[128,768]{1,0:T(8,128)(2,1)S(1)}, bf16[128,768]{1,0:T(8,128)(2,1)S(1)}, bf16[128,768]{1,0:T(8,128)(2,1)S(1)}, bf16[128,768]{1,0:T(8,128)(2...) custom-call(bf16[256,768]{1,0:T(8,128)(2,1)} %tokens_ref.1, ...), custom_call_target="tpu_custom_call" | custom-call | tf_op jit(solution)/shard_map/pallas_call | solution.py:65
  2.8 2.1 %collective-permute-start = (bf16[128,768]{1,0:T(8,128)(2,1)S(1)}, bf16[128,768]{1,0:T(8,128)(2,1)S(1)}, u32[]{:S(2)}, u32[]{:S(2)}) collective-permute-start(bf16[128,768]{1,0:T(8,128)(2,1)S(1)} %get-tuple-element.37), channel_id=1, source_target_pairs={{0,1},{1,2},{2,3},{3,0},{4,5},{5,6},{6,7},{7,4},{8,9},{9,10},{10,1... | collective-permute-start | bytes 589832 | tf_op jit(solution)/shard_map/ppermute | solution.py:394
  5.0 1.3 %collective-permute-start.1 = (bf16[128,768]{1,0:T(8,128)(2,1)S(1)}, bf16[128,768]{1,0:T(8,128)(2,1)S(1)}, u32[]{:S(2)}, u32[]{:S(2)}) collective-permute-start(bf16[128,768]{1,0:T(8,128)(2,1)S(1)} %get-tuple-element.38), channel_id=1, source_target_pairs={{0,3},{1,0},{2,1},{3,2},{4,7},{5,4},{6,5},{7,6},{8,11},{9,8},{10,9... | collective-permute-start | bytes 589832 | tf_op jit(solution)/shard_map/ppermute | solution.py:394
  6.3 3.7 %collective-permute-start.2 = (bf16[128,768]{1,0:T(8,128)(2,1)S(1)}, bf16[128,768]{1,0:T(8,128)(2,1)S(1)}, u32[]{:S(2)}, u32[]{:S(2)}) collective-permute-start(bf16[128,768]{1,0:T(8,128)(2,1)S(1)} %get-tuple-element.39), channel_id=1, source_target_pairs={{0,4},{1,5},{2,6},{3,7},{4,0},{5,1},{6,2},{7,3},{8,12},{9,13},{10,... | collective-permute-start | bytes 589832 | tf_op jit(solution)/shard_map/ppermute | solution.py:394
  10.0 1.5 %collective-permute-start.6 = (bf16[128,768]{1,0:T(8,128)(2,1)S(1)}, bf16[128,768]{1,0:T(8,128)(2,1)S(1)}, u32[]{:S(2)}, u32[]{:S(2)}) collective-permute-start(bf16[128,768]{1,0:T(8,128)(2,1)S(1)} %get-tuple-element.46), channel_id=1, source_target_pairs={{0,2},{1,3},{2,0},{3,1},{4,6},{5,7},{6,4},{7,5},{8,10},{9,11},{10,... | collective-permute-start | bytes 589832 | tf_op jit(solution)/shard_map/ppermute | solution.py:394
  11.6 5.1 %collective-permute-start.10 = (bf16[128,768]{1,0:T(8,128)(2,1)S(1)}, bf16[128,768]{1,0:T(8,128)(2,1)S(1)}, u32[]{:S(2)}, u32[]{:S(2)}) collective-permute-start(bf16[128,768]{1,0:T(8,128)(2,1)S(1)} %get-tuple-element.53), channel_id=1, source_target_pairs={{0,7},{1,4},{2,5},{3,6},{4,3},{5,0},{6,1},{7,2},{8,15},{9,12},{10,... | collective-permute-start | bytes 589832 | tf_op jit(solution)/shard_map/ppermute | solution.py:394
  16.6 9.7 %shard_map.104 = (bf16[128,768]{1,0:T(8,128)(2,1)S(1)}, bf16[128,768]{1,0:T(8,128)(2,1)S(1)}, bf16[128,768]{1,0:T(8,128)(2,1)S(1)}, bf16[128,768]{1,0:T(8,128)(2...) custom-call(bf16[128,768]{1,0:T(8,128)(2,1)S(1)} %get-tuple-element., ...), custom_call_target="tpu_custom_call", output_to_operand_aliasing={{4}: (7, {}), {5}: (8, {})} | custom-call | tf_op jit(solution)/shard_map/pallas_call | solution.py:65
  26.4 1.0 %collective-permute-done.7.refs_1_ = bf16[128,768]{1,0:T(8,128)(2,1)S(1)} collective-permute-done((bf16[128,768]{1,0:T(8,128)(2,1)S(1)}, bf16[128,768]{1,0:T(8,128)(2,1)S(1)}, u32[]{:S(2)}, u32[]{:S(2)}) %collective-permute-start.7) | collective-permute-done | bytes 196640 | tf_op jit(solution)/shard_map/ppermute | solution.py:394
  27.4 5.0 %shard_map.105 = (bf16[128,768]{1,0:T(8,128)(2,1)S(1)}, bf16[128,768]{1,0:T(8,128)(2,1)S(1)}) custom-call(bf16[128,768]{1,0:T(8,128)(2,1)S(1)} %collective-permute-done.6.refs_0_, bf16[128,768]{1,0:T(8,128)(2,1)S(1)} %collective-permute-done.7.refs_1_, bf16[768,3072]{1,0:T(8,128)(2,1)S(1)} %get-tuple-element.48.refs_2_, ...), custom_call_target="tpu_custom_call" | custom-call | tf_op jit(solution)/shard_map/pallas_call | solution.py:65
  32.3 1.7 %collective-permute-start.8 = (bf16[128,768]{1,0:T(8,128)(2,1)S(1)}, bf16[128,768]{1,0:T(8,128)(2,1)S(1)}, u32[]{:S(2)}, u32[]{:S(2)}) collective-permute-start(bf16[128,768]{1,0:T(8,128)(2,1)S(1)} %get-tuple-element.51), channel_id=1, source_target_pairs={{2,0},{3,1},{0,2},{1,3},{6,4},{7,5},{4,6},{5,7},{10,8},{11,9},{8,1... | collective-permute-start | bytes 589832 | tf_op jit(solution)/shard_map/ppermute | solution.py:394
  34.1 2.4 %collective-permute-start.9 = (bf16[128,768]{1,0:T(8,128)(2,1)S(1)}, bf16[128,768]{1,0:T(8,128)(2,1)S(1)}, u32[]{:S(2)}, u32[]{:S(2)}) collective-permute-start(bf16[128,768]{1,0:T(8,128)(2,1)S(1)} %get-tuple-element.52), channel_id=1, source_target_pairs={{5,0},{6,1},{7,2},{4,3},{1,4},{2,5},{3,6},{0,7},{13,8},{14,9},{15,... | collective-permute-start | bytes 589832 | tf_op jit(solution)/shard_map/ppermute | solution.py:394
  36.4 3.1 %collective-permute-start.3 = (bf16[128,768]{1,0:T(8,128)(2,1)S(1)}, bf16[128,768]{1,0:T(8,128)(2,1)S(1)}, u32[]{:S(2)}, u32[]{:S(2)}) collective-permute-start(bf16[128,768]{1,0:T(8,128)(2,1)S(1)} %get-tuple-element.43), channel_id=1, source_target_pairs={{1,0},{2,1},{3,2},{0,3},{5,4},{6,5},{7,6},{4,7},{9,8},{10,9},{11,1... | collective-permute-start | bytes 589832 | tf_op jit(solution)/shard_map/ppermute | solution.py:394
  39.6 0.1 collective-permute-start.5
  39.7 5.0 %shard_map.107 = (bf16[128,768]{1,0:T(8,128)(2,1)S(1)}, bf16[128,768]{1,0:T(8,128)(2,1)S(1)}) custom-call(bf16[128,768]{1,0:T(8,128)(2,1)S(1)} %collective-permute-done.10.refs_0_, bf16[128,768]{1,0:T(8,128)(2,1)S(1)} %collective-permute-done.11.refs_1_, bf16[768,3072]{1,0:T(8,128)(2,1)S(1)} %get-tuple-element.48.refs_2_, ...), custom_call_target="tpu_custom_call" | custom-call | tf_op jit(solution)/shard_map/pallas_call | solution.py:65
  44.7 2.7 %collective-permute-start.12 = (bf16[128,768]{1,0:T(8,128)(2,1)S(1)}, bf16[128,768]{1,0:T(8,128)(2,1)S(1)}, u32[]{:S(2)}, u32[]{:S(2)}) collective-permute-start(bf16[128,768]{1,0:T(8,128)(2,1)S(1)} %get-tuple-element.55), channel_id=1, source_target_pairs={{7,0},{4,1},{5,2},{6,3},{3,4},{0,5},{1,6},{2,7},{15,8},{12,9},{13,... | collective-permute-start | bytes 589832 | tf_op jit(solution)/shard_map/ppermute | solution.py:394
  47.4 3.5 %collective-permute-start.13 = (bf16[128,768]{1,0:T(8,128)(2,1)S(1)}, bf16[128,768]{1,0:T(8,128)(2,1)S(1)}, u32[]{:S(2)}, u32[]{:S(2)}) collective-permute-start(bf16[128,768]{1,0:T(8,128)(2,1)S(1)} %get-tuple-element.56), channel_id=1, source_target_pairs={{6,0},{7,1},{4,2},{5,3},{2,4},{3,5},{0,6},{1,7},{14,8},{15,9},{12,... | collective-permute-start | bytes 589832 | tf_op jit(solution)/shard_map/ppermute | solution.py:394
  50.9 1.2 %shard_map.106.early_ref = f32[256,768]{1,0:T(8,128)S(1)} custom-call(bf16[256,768]{1,0:T(8,128)(2,1)S(1)} %copy-done, f32[256,8]{1,0:T(8,128)S(1)} %get-tuple-element.34.slots_ref, f32[256,8]{1,0:T(8,128)S(1)} %get-tuple-element.35.weights_ref, bf16[128,768]{1,0:T(8,128)(2,1)S(1)} %get-tuple-element.42.refs_0_, ...), custom_call_target="tpu_custom_call" | custom-call | tf_op jit(solution)/shard_map/pallas_call | solution.py:65
  52.1 0.8 collective-permute-done.12.refs_0_
  53.0 3.1 %collective-permute-done.13.refs_1_ = bf16[128,768]{1,0:T(8,128)(2,1)S(1)} collective-permute-done((bf16[128,768]{1,0:T(8,128)(2,1)S(1)}, bf16[128,768]{1,0:T(8,128)(2,1)S(1)}, u32[]{:S(2)}, u32[]{:S(2)}) %collective-permute-start.13) | collective-permute-done | bytes 196640 | tf_op jit(solution)/shard_map/ppermute | solution.py:394
  56.1 1.1 %shard_map.108 = (f32[256,768]{1,0:T(8,128)S(1)}, f32[16,768]{1,0:T(8,128)S(1)}, bf16[16,768]{1,0:T(8,128)(2,1)S(1)}) custom-call(f32[256,768]{1,0:T(8,128)S(1)} %shard_map.106.early_ref, f32[256,8]{1,0:T(8,128)S(1)} %get-tuple-element.34.slots_ref, f32[256,8]{1,0:T(8,128)S(1)} %get-tuple-element.35.weights_ref, s32[1,16]{1,0:T(1,128)S(1)} %copy-done.1, ...), custom_call_target="tpu_custom_call" | custom-call | tf_op jit(solution)/shard_map/pallas_call | solution.py:65
  57.2 20.7 %all_to_all.5 = bf16[16,16,768]{2,1,0:T(8,128)(2,1)S(1)} all-to-all(bf16[16,16,768]{2,1,0:T(8,128)(2,1)S(1)} %broadcast_in_dim.2), channel_id=1, replica_groups={{0,4,16,20,34,38,50,54,64,68,80,84,98,102,114,118},{8,12,24,28,42,46,58..., dimensions={0} | all-to-all | bytes 786432 | tf_op jit(solution)/shard_map/all_to_all | solution.py:411
  78.0 0.8 convert_element_type.3
  78.7 2.7 %collective-permute-start.14 = (bf16[16,16,768]{2,1,0:T(8,128)(2,1)S(1)}, bf16[16,16,768]{2,1,0:T(8,128)(2,1)S(1)}, u32[]{:S(2)}, u32[]{:S(2)}) collective-permute-start(bf16[16,16,768]{2,1,0:T(8,128)(2,1)S(1)} %all_to_all.5), channel_id=1, source_target_pairs={{0,3},{1,0},{2,1},{3,2},{4,7},{5,4},{6,5},{7,6},{8,11},{9,8},{10,9... | collective-permute-start | bytes 1179656 | tf_op jit(solution)/shard_map/ppermute | solution.py:416
  81.4 5.0 %collective-permute-start.17 = (bf16[16,16,768]{2,1,0:T(8,128)(2,1)S(1)}, bf16[16,16,768]{2,1,0:T(8,128)(2,1)S(1)}, u32[]{:S(2)}, u32[]{:S(2)}) collective-permute-start(bf16[16,16,768]{2,1,0:T(8,128)(2,1)S(1)} %all_to_all.5), channel_id=1, source_target_pairs={{0,8},{8,0},{16,24},{24,16},{32,40},{40,32},{48,56},{56,48},{64,72... | collective-permute-start | bytes 1179656 | tf_op jit(solution)/shard_map/ppermute | solution.py:420
  86.5 4.2 %collective-permute-start.20 = (bf16[16,16,768]{2,1,0:T(8,128)(2,1)S(1)}, bf16[16,16,768]{2,1,0:T(8,128)(2,1)S(1)}, u32[]{:S(2)}, u32[]{:S(2)}) collective-permute-start(bf16[16,16,768]{2,1,0:T(8,128)(2,1)S(1)} %collective-permute-done.16), channel_id=1, source_target_pairs={{0,8},{8,0},{16,24},{24,16},{32,40},{40,32},{48,56},{56,48},{64,72... | collective-permute-start | bytes 1179656 | tf_op jit(solution)/shard_map/ppermute | solution.py:420
  90.8 0.1 collective-permute-start.19
  90.9 0.9 collective-permute-start.18
  91.8 0.2 maximum_bitcast_fusion
  92.0 0.8 shard_map.109
  92.9 0.2 fusion
  93.2 0.2 maximum_bitcast_fusion.2
  93.4 3.0 %shard_map.110 = (f32[8,768]{1,0:T(8,128)}, f32[8,768]{1,0:T(8,128)}) custom-call(bf16[512,768]{1,0:T(8,128)(2,1)S(1)} %get-tuple-element.81.queries_ref, bf16[512,768]{1,0:T(8,128)(2,1)S(1)} %get-tuple-element.82.docs_ref, bf16[512,768]{1,0:T(8,128)(2,1)S(1)} %get-tuple-element.83.more_queries_ref, bf16[512,768]{1,0:T(8,128)(2,1)S(1)} %get-tuple-element.84.more_docs_ref, ...), custom_call_target="tpu_custom_call" | custom-call | tf_op jit(solution)/shard_map/pallas_call | solution.py:65
  (35 shorter events, 0.4 us)
Async XLA Ops:
  2.8 8.7 %collective-permute-start = (bf16[128,768]{1,0:T(8,128)(2,1)S(1)}, bf16[128,768]{1,0:T(8,128)(2,1)S(1)}, u32[]{:S(2)}, u32[]{:S(2)}) collective-permute-start(bf16[128,768]{1,0:T(8,128)(2,1)S(1)} %get-tuple-element.37), channel_id=1, source_target_pairs={{0,1},{1,2},{2,3},{3,0},{4,5},{5,6},{6,7},{7,4},{8,9},{9,10},{10,1... | collective-permute-start | bytes 589832 | tf_op jit(solution)/shard_map/ppermute | solution.py:394
  5.0 11.7 %collective-permute-start.1 = (bf16[128,768]{1,0:T(8,128)(2,1)S(1)}, bf16[128,768]{1,0:T(8,128)(2,1)S(1)}, u32[]{:S(2)}, u32[]{:S(2)}) collective-permute-start(bf16[128,768]{1,0:T(8,128)(2,1)S(1)} %get-tuple-element.38), channel_id=1, source_target_pairs={{0,3},{1,0},{2,1},{3,2},{4,7},{5,4},{6,5},{7,6},{8,11},{9,8},{10,9... | collective-permute-start | bytes 589832 | tf_op jit(solution)/shard_map/ppermute | solution.py:394
  6.3 10.3 %collective-permute-start.2 = (bf16[128,768]{1,0:T(8,128)(2,1)S(1)}, bf16[128,768]{1,0:T(8,128)(2,1)S(1)}, u32[]{:S(2)}, u32[]{:S(2)}) collective-permute-start(bf16[128,768]{1,0:T(8,128)(2,1)S(1)} %get-tuple-element.39), channel_id=1, source_target_pairs={{0,4},{1,5},{2,6},{3,7},{4,0},{5,1},{6,2},{7,3},{8,12},{9,13},{10,... | collective-permute-start | bytes 589832 | tf_op jit(solution)/shard_map/ppermute | solution.py:394
  10.0 16.3 %collective-permute-start.6 = (bf16[128,768]{1,0:T(8,128)(2,1)S(1)}, bf16[128,768]{1,0:T(8,128)(2,1)S(1)}, u32[]{:S(2)}, u32[]{:S(2)}) collective-permute-start(bf16[128,768]{1,0:T(8,128)(2,1)S(1)} %get-tuple-element.46), channel_id=1, source_target_pairs={{0,2},{1,3},{2,0},{3,1},{4,6},{5,7},{6,4},{7,5},{8,10},{9,11},{10,... | collective-permute-start | bytes 589832 | tf_op jit(solution)/shard_map/ppermute | solution.py:394
  11.6 15.8 %collective-permute-start.7 = (bf16[128,768]{1,0:T(8,128)(2,1)S(1)}, bf16[128,768]{1,0:T(8,128)(2,1)S(1)}, u32[]{:S(2)}, u32[]{:S(2)}) collective-permute-start(bf16[128,768]{1,0:T(8,128)(2,1)S(1)} %get-tuple-element.47), channel_id=1, source_target_pairs={{0,5},{1,6},{2,7},{3,4},{4,1},{5,2},{6,3},{7,0},{8,13},{9,14},{10,... | collective-permute-start | bytes 589832 | tf_op jit(solution)/shard_map/ppermute | solution.py:394
  11.6 28.0 %collective-permute-start.10 = (bf16[128,768]{1,0:T(8,128)(2,1)S(1)}, bf16[128,768]{1,0:T(8,128)(2,1)S(1)}, u32[]{:S(2)}, u32[]{:S(2)}) collective-permute-start(bf16[128,768]{1,0:T(8,128)(2,1)S(1)} %get-tuple-element.53), channel_id=1, source_target_pairs={{0,7},{1,4},{2,5},{3,6},{4,3},{5,0},{6,1},{7,2},{8,15},{9,12},{10,... | collective-permute-start | bytes 589832 | tf_op jit(solution)/shard_map/ppermute | solution.py:394
  16.6 22.9 %collective-permute-start.11 = (bf16[128,768]{1,0:T(8,128)(2,1)S(1)}, bf16[128,768]{1,0:T(8,128)(2,1)S(1)}, u32[]{:S(2)}, u32[]{:S(2)}) collective-permute-start(bf16[128,768]{1,0:T(8,128)(2,1)S(1)} %get-tuple-element.54), channel_id=1, source_target_pairs={{0,6},{1,7},{2,4},{3,5},{4,2},{5,3},{6,0},{7,1},{8,14},{9,15},{10,... | collective-permute-start | bytes 589832 | tf_op jit(solution)/shard_map/ppermute | solution.py:394
  32.3 12.3 %collective-permute-start.8 = (bf16[128,768]{1,0:T(8,128)(2,1)S(1)}, bf16[128,768]{1,0:T(8,128)(2,1)S(1)}, u32[]{:S(2)}, u32[]{:S(2)}) collective-permute-start(bf16[128,768]{1,0:T(8,128)(2,1)S(1)} %get-tuple-element.51), channel_id=1, source_target_pairs={{2,0},{3,1},{0,2},{1,3},{6,4},{7,5},{4,6},{5,7},{10,8},{11,9},{8,1... | collective-permute-start | bytes 589832 | tf_op jit(solution)/shard_map/ppermute | solution.py:394
  34.1 13.3 %collective-permute-start.9 = (bf16[128,768]{1,0:T(8,128)(2,1)S(1)}, bf16[128,768]{1,0:T(8,128)(2,1)S(1)}, u32[]{:S(2)}, u32[]{:S(2)}) collective-permute-start(bf16[128,768]{1,0:T(8,128)(2,1)S(1)} %get-tuple-element.52), channel_id=1, source_target_pairs={{5,0},{6,1},{7,2},{4,3},{1,4},{2,5},{3,6},{0,7},{13,8},{14,9},{15,... | collective-permute-start | bytes 589832 | tf_op jit(solution)/shard_map/ppermute | solution.py:394
  36.4 14.5 %collective-permute-start.3 = (bf16[128,768]{1,0:T(8,128)(2,1)S(1)}, bf16[128,768]{1,0:T(8,128)(2,1)S(1)}, u32[]{:S(2)}, u32[]{:S(2)}) collective-permute-start(bf16[128,768]{1,0:T(8,128)(2,1)S(1)} %get-tuple-element.43), channel_id=1, source_target_pairs={{1,0},{2,1},{3,2},{0,3},{5,4},{6,5},{7,6},{4,7},{9,8},{10,9},{11,1... | collective-permute-start | bytes 589832 | tf_op jit(solution)/shard_map/ppermute | solution.py:394
  39.5 11.4 %collective-permute-start.4 = (bf16[128,768]{1,0:T(8,128)(2,1)S(1)}, bf16[128,768]{1,0:T(8,128)(2,1)S(1)}, u32[]{:S(2)}, u32[]{:S(2)}) collective-permute-start(bf16[128,768]{1,0:T(8,128)(2,1)S(1)} %get-tuple-element.44), channel_id=1, source_target_pairs={{3,0},{0,1},{1,2},{2,3},{7,4},{4,5},{5,6},{6,7},{11,8},{8,9},{9,10... | collective-permute-start | bytes 589832 | tf_op jit(solution)/shard_map/ppermute | solution.py:394
  39.6 11.4 %copy-start = (bf16[256,768]{1,0:T(8,128)(2,1)S(1)}, bf16[256,768]{1,0:T(8,128)(2,1)}, u32[]{:S(2)}) copy-start(bf16[256,768]{1,0:T(8,128)(2,1)} %tokens_ref.1) | copy-start | bytes 1179652
  39.6 16.5 %copy-start.1 = (s32[1,16]{1,0:T(1,128)S(1)}, s32[1,16]{1,0:T(1,128)}, u32[]{:S(2)}) copy-start(s32[1,16]{1,0:T(1,128)} %lengths_ref.1) | copy-start | bytes 196
  39.6 11.3 %collective-permute-start.5 = (bf16[128,768]{1,0:T(8,128)(2,1)S(1)}, bf16[128,768]{1,0:T(8,128)(2,1)S(1)}, u32[]{:S(2)}, u32[]{:S(2)}) collective-permute-start(bf16[128,768]{1,0:T(8,128)(2,1)S(1)} %get-tuple-element.45), channel_id=1, source_target_pairs={{4,0},{5,1},{6,2},{7,3},{0,4},{1,5},{2,6},{3,7},{12,8},{13,9},{14,... | collective-permute-start | bytes 589832 | tf_op jit(solution)/shard_map/ppermute | solution.py:394
  44.7 8.3 %collective-permute-start.12 = (bf16[128,768]{1,0:T(8,128)(2,1)S(1)}, bf16[128,768]{1,0:T(8,128)(2,1)S(1)}, u32[]{:S(2)}, u32[]{:S(2)}) collective-permute-start(bf16[128,768]{1,0:T(8,128)(2,1)S(1)} %get-tuple-element.55), channel_id=1, source_target_pairs={{7,0},{4,1},{5,2},{6,3},{3,4},{0,5},{1,6},{2,7},{15,8},{12,9},{13,... | collective-permute-start | bytes 589832 | tf_op jit(solution)/shard_map/ppermute | solution.py:394
  47.4 8.7 %collective-permute-start.13 = (bf16[128,768]{1,0:T(8,128)(2,1)S(1)}, bf16[128,768]{1,0:T(8,128)(2,1)S(1)}, u32[]{:S(2)}, u32[]{:S(2)}) collective-permute-start(bf16[128,768]{1,0:T(8,128)(2,1)S(1)} %get-tuple-element.56), channel_id=1, source_target_pairs={{6,0},{7,1},{4,2},{5,3},{2,4},{3,5},{0,6},{1,7},{14,8},{15,9},{12,... | collective-permute-start | bytes 589832 | tf_op jit(solution)/shard_map/ppermute | solution.py:394
  78.0 8.5 %collective-permute-start.16 = (bf16[16,16,768]{2,1,0:T(8,128)(2,1)S(1)}, bf16[16,16,768]{2,1,0:T(8,128)(2,1)S(1)}, u32[]{:S(2)}, u32[]{:S(2)}) collective-permute-start(bf16[16,16,768]{2,1,0:T(8,128)(2,1)S(1)} %all_to_all.5), channel_id=1, source_target_pairs={{0,1},{1,2},{2,3},{3,0},{4,5},{5,6},{6,7},{7,4},{8,9},{9,10},{10,1... | collective-permute-start | bytes 1179656 | tf_op jit(solution)/shard_map/ppermute | solution.py:418
  78.7 12.0 %collective-permute-start.15 = (bf16[16,16,768]{2,1,0:T(8,128)(2,1)S(1)}, bf16[16,16,768]{2,1,0:T(8,128)(2,1)S(1)}, u32[]{:S(2)}, u32[]{:S(2)}) collective-permute-start(bf16[16,16,768]{2,1,0:T(8,128)(2,1)S(1)} %all_to_all.5), channel_id=1, source_target_pairs={{0,96},{8,104},{16,112},{24,120},{32,0},{40,8},{48,16},{56,24},{64... | collective-permute-start | bytes 1179656 | tf_op jit(solution)/shard_map/ppermute | solution.py:417
  78.7 12.1 %collective-permute-start.14 = (bf16[16,16,768]{2,1,0:T(8,128)(2,1)S(1)}, bf16[16,16,768]{2,1,0:T(8,128)(2,1)S(1)}, u32[]{:S(2)}, u32[]{:S(2)}) collective-permute-start(bf16[16,16,768]{2,1,0:T(8,128)(2,1)S(1)} %all_to_all.5), channel_id=1, source_target_pairs={{0,3},{1,0},{2,1},{3,2},{4,7},{5,4},{6,5},{7,6},{8,11},{9,8},{10,9... | collective-permute-start | bytes 1179656 | tf_op jit(solution)/shard_map/ppermute | solution.py:416
  81.4 10.6 %collective-permute-start.17 = (bf16[16,16,768]{2,1,0:T(8,128)(2,1)S(1)}, bf16[16,16,768]{2,1,0:T(8,128)(2,1)S(1)}, u32[]{:S(2)}, u32[]{:S(2)}) collective-permute-start(bf16[16,16,768]{2,1,0:T(8,128)(2,1)S(1)} %all_to_all.5), channel_id=1, source_target_pairs={{0,8},{8,0},{16,24},{24,16},{32,40},{40,32},{48,56},{56,48},{64,72... | collective-permute-start | bytes 1179656 | tf_op jit(solution)/shard_map/ppermute | solution.py:420
  86.5 6.6 %collective-permute-start.20 = (bf16[16,16,768]{2,1,0:T(8,128)(2,1)S(1)}, bf16[16,16,768]{2,1,0:T(8,128)(2,1)S(1)}, u32[]{:S(2)}, u32[]{:S(2)}) collective-permute-start(bf16[16,16,768]{2,1,0:T(8,128)(2,1)S(1)} %collective-permute-done.16), channel_id=1, source_target_pairs={{0,8},{8,0},{16,24},{24,16},{32,40},{40,32},{48,56},{56,48},{64,72... | collective-permute-start | bytes 1179656 | tf_op jit(solution)/shard_map/ppermute | solution.py:420
  90.8 2.3 %collective-permute-start.19 = (bf16[16,16,768]{2,1,0:T(8,128)(2,1)S(1)}, bf16[16,16,768]{2,1,0:T(8,128)(2,1)S(1)}, u32[]{:S(2)}, u32[]{:S(2)}) collective-permute-start(bf16[16,16,768]{2,1,0:T(8,128)(2,1)S(1)} %collective-permute-done.15), channel_id=1, source_target_pairs={{0,8},{8,0},{16,24},{24,16},{32,40},{40,32},{48,56},{56,48},{64,72... | collective-permute-start | bytes 1179656 | tf_op jit(solution)/shard_map/ppermute | solution.py:420
  90.9 2.3 %collective-permute-start.18 = (bf16[16,16,768]{2,1,0:T(8,128)(2,1)S(1)}, bf16[16,16,768]{2,1,0:T(8,128)(2,1)S(1)}, u32[]{:S(2)}, u32[]{:S(2)}) collective-permute-start(bf16[16,16,768]{2,1,0:T(8,128)(2,1)S(1)} %collective-permute-done.14), channel_id=1, source_target_pairs={{0,8},{8,0},{16,24},{24,16},{32,40},{40,32},{48,56},{56,48},{64,72... | collective-permute-start | bytes 1179656 | tf_op jit(solution)/shard_map/ppermute | solution.py:420
